TPU v7x, 256 devices: a whole 4x4x8 slice. The times are simulated.
256 devices in a mesh: ctx: 16 (over x_hi, z), tp: 16 (over y, x_lo, core).
Axes of the slice: x: 4 (x_hi: 2, x_lo: 2; x = x_hi * 2 + x_lo), y: 4, z: 8, core: 2. Of those that a mesh axis runs over, the one named last changes fastest.
Arguments:
- queries: bfloat16 [12288, 8192], P('ctx', 'tp'), may hold values from -6 to 6
- keys_in: bfloat16 [12288, 8192], P('ctx', 'tp'), may hold values from -6 to 6
- values_in: bfloat16 [12288, 8192], P('ctx', 'tp'), may hold values from -6 to 6
- short_taps: bfloat16 [3, 8192], P(None, 'tp'), may hold values from -3.5 to 3.5
- filters: bfloat16 [8192, 128], P('tp'), may hold values from -0.5 to 0.5
- skip_gain: float32 [8192], P('tp'), may hold values from -1 to 1
- out_weight: bfloat16 [8192, 8192], P('tp'), may hold values from -0.0625 to 0.0625
- residual: bfloat16 [12288, 8192], P(('ctx', 'tp')), may hold values from -6 to 6
Outputs:
- block_out: bfloat16 [12288, 8192], P(('ctx', 'tp'))
All inputs are finite; a program needn't handle non-finite values.
Results may differ from a plain program's by a relative error of at most 0.022.
Values may be sent and summed in bfloat16 or wider, within the bound.
No kernel may reach another device: no remote copies, remote signals or barrier semaphores. Data moves between devices by JAX's collectives and lax.ppermute only.
A program may use at most 128 MiB of HBM per device.

v0:
```python
import math

import jax
import jax.numpy as jnp
from jax import lax
from jax.sharding import PartitionSpec as P


def from_behind(shard, axis, by):
    peers = lax.axis_size(axis)
    pairs = [(i, i + by) for i in range(peers) if 0 <= i + by < peers]
    return lax.ppermute(shard, axis, pairs)


def featurize(sequence, tap_weights, out_rows):
    result = jnp.zeros((out_rows, sequence.shape[1]), jnp.float32)
    for offset in range(tap_weights.shape[0]):
        start = tap_weights.shape[0] - 1 - offset
        result = result + tap_weights[offset].astype(jnp.float32) * sequence[
            start : start + out_rows
        ].astype(jnp.float32)
    return result


def skewed_band(lag_row, tap_count):
    lane_width = lag_row.shape[0]
    flipped = lag_row[:, ::-1]
    padded = jnp.concatenate([flipped, jnp.zeros((lane_width, 1), lag_row.dtype)], axis=1)
    tiled = jnp.tile(padded, (1, tap_count))
    stride = 2 * tap_count - 1
    window = tiled[:, tap_count - 1 : tap_count - 1 + tap_count * stride]
    return window.reshape(lane_width, tap_count, stride)[:, :, :tap_count]


def causal_filter(product_ext, filters):
    span_rows, channels = product_ext.shape
    tap_count = filters.shape[1]
    block_count = span_rows // tap_count
    lane_width = math.gcd(channels, 128)
    lane_groups = channels // lane_width
    lanes = product_ext.reshape(span_rows, lane_groups, lane_width).transpose(1, 0, 2)
    kernels = filters.reshape(lane_groups, lane_width, tap_count)

    def one_group(operands):
        lane_seq, kernel = operands
        near_row = jnp.concatenate(
            [jnp.zeros((lane_width, tap_count - 1), kernel.dtype), kernel], axis=1
        )
        far_row = jnp.concatenate(
            [kernel[:, 1:], jnp.zeros((lane_width, tap_count), kernel.dtype)], axis=1
        )
        near_band = skewed_band(near_row, tap_count)
        far_band = skewed_band(far_row, tap_count)
        blocked = lane_seq.reshape(block_count, tap_count, lane_width)
        result = jnp.einsum(
            "cim,bmc->bic", near_band, blocked[1:], preferred_element_type=jnp.float32
        )
        result = result + jnp.einsum(
            "cim,bmc->bic", far_band, blocked[:-1], preferred_element_type=jnp.float32
        )
        return result.reshape((block_count - 1) * tap_count, lane_width)

    filtered_all = lax.map(one_group, (lanes, kernels))
    return filtered_all.transpose(1, 0, 2).reshape(span_rows - tap_count, channels)


def body(queries, keys_in, values_in, short_taps, filters, skip_gain, out_weight, residual):
    seq_rows, channels = queries.shape
    tap_count = filters.shape[1]
    short_rim = short_taps.shape[0] - 1
    q_rim, k_rim, v_rim = from_behind(
        (
            queries[seq_rows - short_rim :],
            keys_in[seq_rows - tap_count - short_rim :],
            values_in[seq_rows - tap_count - short_rim :],
        ),
        "ctx",
        1,
    )
    q_feat = featurize(jnp.concatenate([q_rim, queries]), short_taps, seq_rows)
    k_feat = featurize(jnp.concatenate([k_rim, keys_in]), short_taps, seq_rows + tap_count)
    v_feat = featurize(jnp.concatenate([v_rim, values_in]), short_taps, seq_rows + tap_count)
    product_ext = (k_feat * v_feat).astype(jnp.bfloat16)
    product_own = product_ext[tap_count:]
    filtered = causal_filter(product_ext, filters)
    gated = (q_feat * (filtered + skip_gain * product_own.astype(jnp.float32))).astype(jnp.bfloat16)
    summed = lax.psum_scatter(
        jnp.dot(gated, out_weight, preferred_element_type=jnp.float32).astype(jnp.bfloat16),
        "tp",
        scatter_dimension=0,
        tiled=True,
    ).astype(jnp.float32)
    return (residual.astype(jnp.float32) + summed).astype(jnp.bfloat16)


def solution(mesh):
    in_specs = (
        P("ctx", "tp"),
        P("ctx", "tp"),
        P("ctx", "tp"),
        P(None, "tp"),
        P("tp", None),
        P("tp"),
        P("tp", None),
        P(("ctx", "tp"), None),
    )
    out_specs = P(("ctx", "tp"), None)
    return jax.shard_map(body, mesh=mesh, in_specs=in_specs, out_specs=out_specs, check_vma=False)
```

profile of v0, /device:TPU:4, one launch (start us, length us, event | category | flops | bytes accessed | tf_op | source)
XLA Modules:
  0.0 686.1 jit_solution(6651308451010022686)
XLA Ops:
  23.3 5.4 collective-permute-done.2
  30.9 487.6 %while.10 = (s32[]{:T(128)}, f32[4,768,128]{1,2,0:T(8,128)}, bf16[4,896,128]{1,2,0:T(8,128)(2,1)S(1)}, bf16[4,128,128]{2,1,0:T(8,128)(2,1)}, s32[]{:T(128)}, /*index=5*/s32[]{:T(128)}, s32[]{}, bf16[]{:T(256)}) while((s32[]{:T(128)}, f32[4,768,128]{1,2,0:T(8,128)}, bf16[4,896,128]{1,2,0:T(8,128)(2,1)S(1)}, bf16[4,128,128]{2,1,0:T(8,128)(2,1)}, ...), condition=%wide.region_1.2_spmd, body=%wide.region_0.1_spmd.sunk | while | flops 50429952 | bytes 133101424 | solution.py:63
  36.2 12.3 %copy.43 = bf16[16,8,128,256]{3,1,2,0:T(8,128)(2,1)} copy(bf16[16,8,128,256]{3,2,1,0:T(8,128)(2,1)} %bitcast.58) | data formatting | bytes 16777216 | tf_op jit(solution)/shard_map/while
  48.5 9.0 %slice.176 = bf16[128,32640]{1,0:T(8,128)(2,1)} slice(bf16[128,32768]{1,0:T(8,128)(2,1)} %bitcast.60), slice={[0:128], [127:32767]} | slice | bytes 16711680 | tf_op jit(solution)/shard_map/while/body/eval_jaxpr/slice | solution.py:31
  57.5 29.5 %reshape.38 = bf16[128,128,255]{2,1,0:T(8,128)(2,1)} reshape(bf16[128,32640]{1,0:T(8,128)(2,1)} %slice.176) | data formatting | bytes 16711680 | tf_op jit(solution)/shard_map/while/body/eval_jaxpr/reshape | solution.py:32
  96.1 12.3 %copy.46 = bf16[16,8,128,256]{3,1,2,0:T(8,128)(2,1)} copy(bf16[16,8,128,256]{3,2,1,0:T(8,128)(2,1)} %bitcast.59) | data formatting | bytes 16777216 | tf_op jit(solution)/shard_map/while
  108.5 9.0 %slice.178 = bf16[128,32640]{1,0:T(8,128)(2,1)} slice(bf16[128,32768]{1,0:T(8,128)(2,1)} %bitcast.61), slice={[0:128], [127:32767]} | slice | bytes 16711680 | tf_op jit(solution)/shard_map/while/body/eval_jaxpr/slice | solution.py:31
  117.5 29.5 %reshape.39 = bf16[128,128,255]{2,1,0:T(8,128)(2,1)} reshape(bf16[128,32640]{1,0:T(8,128)(2,1)} %slice.178) | data formatting | bytes 16711680 | tf_op jit(solution)/shard_map/while/body/eval_jaxpr/reshape | solution.py:32
  147.4 4.4 fusion.32
  158.0 12.3 %copy.43 = bf16[16,8,128,256]{3,1,2,0:T(8,128)(2,1)} copy(bf16[16,8,128,256]{3,2,1,0:T(8,128)(2,1)} %bitcast.58) | data formatting | bytes 16777216 | tf_op jit(solution)/shard_map/while
  170.3 9.0 %slice.176 = bf16[128,32640]{1,0:T(8,128)(2,1)} slice(bf16[128,32768]{1,0:T(8,128)(2,1)} %bitcast.60), slice={[0:128], [127:32767]} | slice | bytes 16711680 | tf_op jit(solution)/shard_map/while/body/eval_jaxpr/slice | solution.py:31
  179.3 29.5 %reshape.38 = bf16[128,128,255]{2,1,0:T(8,128)(2,1)} reshape(bf16[128,32640]{1,0:T(8,128)(2,1)} %slice.176) | data formatting | bytes 16711680 | tf_op jit(solution)/shard_map/while/body/eval_jaxpr/reshape | solution.py:32
  217.9 12.3 %copy.46 = bf16[16,8,128,256]{3,1,2,0:T(8,128)(2,1)} copy(bf16[16,8,128,256]{3,2,1,0:T(8,128)(2,1)} %bitcast.59) | data formatting | bytes 16777216 | tf_op jit(solution)/shard_map/while
  230.3 9.0 %slice.178 = bf16[128,32640]{1,0:T(8,128)(2,1)} slice(bf16[128,32768]{1,0:T(8,128)(2,1)} %bitcast.61), slice={[0:128], [127:32767]} | slice | bytes 16711680 | tf_op jit(solution)/shard_map/while/body/eval_jaxpr/slice | solution.py:31
  239.3 29.5 %reshape.39 = bf16[128,128,255]{2,1,0:T(8,128)(2,1)} reshape(bf16[128,32640]{1,0:T(8,128)(2,1)} %slice.178) | data formatting | bytes 16711680 | tf_op jit(solution)/shard_map/while/body/eval_jaxpr/reshape | solution.py:32
  269.2 4.4 fusion.32
  279.8 12.3 %copy.43 = bf16[16,8,128,256]{3,1,2,0:T(8,128)(2,1)} copy(bf16[16,8,128,256]{3,2,1,0:T(8,128)(2,1)} %bitcast.58) | data formatting | bytes 16777216 | tf_op jit(solution)/shard_map/while
  292.2 9.0 %slice.176 = bf16[128,32640]{1,0:T(8,128)(2,1)} slice(bf16[128,32768]{1,0:T(8,128)(2,1)} %bitcast.60), slice={[0:128], [127:32767]} | slice | bytes 16711680 | tf_op jit(solution)/shard_map/while/body/eval_jaxpr/slice | solution.py:31
  301.2 29.5 %reshape.38 = bf16[128,128,255]{2,1,0:T(8,128)(2,1)} reshape(bf16[128,32640]{1,0:T(8,128)(2,1)} %slice.176) | data formatting | bytes 16711680 | tf_op jit(solution)/shard_map/while/body/eval_jaxpr/reshape | solution.py:32
  339.8 12.3 %copy.46 = bf16[16,8,128,256]{3,1,2,0:T(8,128)(2,1)} copy(bf16[16,8,128,256]{3,2,1,0:T(8,128)(2,1)} %bitcast.59) | data formatting | bytes 16777216 | tf_op jit(solution)/shard_map/while
  352.1 9.0 %slice.178 = bf16[128,32640]{1,0:T(8,128)(2,1)} slice(bf16[128,32768]{1,0:T(8,128)(2,1)} %bitcast.61), slice={[0:128], [127:32767]} | slice | bytes 16711680 | tf_op jit(solution)/shard_map/while/body/eval_jaxpr/slice | solution.py:31
  361.2 29.5 %reshape.39 = bf16[128,128,255]{2,1,0:T(8,128)(2,1)} reshape(bf16[128,32640]{1,0:T(8,128)(2,1)} %slice.178) | data formatting | bytes 16711680 | tf_op jit(solution)/shard_map/while/body/eval_jaxpr/reshape | solution.py:32
  391.0 4.4 fusion.32
  401.7 12.3 %copy.43 = bf16[16,8,128,256]{3,1,2,0:T(8,128)(2,1)} copy(bf16[16,8,128,256]{3,2,1,0:T(8,128)(2,1)} %bitcast.58) | data formatting | bytes 16777216 | tf_op jit(solution)/shard_map/while
  414.0 9.0 %slice.176 = bf16[128,32640]{1,0:T(8,128)(2,1)} slice(bf16[128,32768]{1,0:T(8,128)(2,1)} %bitcast.60), slice={[0:128], [127:32767]} | slice | bytes 16711680 | tf_op jit(solution)/shard_map/while/body/eval_jaxpr/slice | solution.py:31
  423.0 29.5 %reshape.38 = bf16[128,128,255]{2,1,0:T(8,128)(2,1)} reshape(bf16[128,32640]{1,0:T(8,128)(2,1)} %slice.176) | data formatting | bytes 16711680 | tf_op jit(solution)/shard_map/while/body/eval_jaxpr/reshape | solution.py:32
  461.6 12.3 %copy.46 = bf16[16,8,128,256]{3,1,2,0:T(8,128)(2,1)} copy(bf16[16,8,128,256]{3,2,1,0:T(8,128)(2,1)} %bitcast.59) | data formatting | bytes 16777216 | tf_op jit(solution)/shard_map/while
  474.0 9.0 %slice.178 = bf16[128,32640]{1,0:T(8,128)(2,1)} slice(bf16[128,32768]{1,0:T(8,128)(2,1)} %bitcast.61), slice={[0:128], [127:32767]} | slice | bytes 16711680 | tf_op jit(solution)/shard_map/while/body/eval_jaxpr/slice | solution.py:31
  483.0 29.5 %reshape.39 = bf16[128,128,255]{2,1,0:T(8,128)(2,1)} reshape(bf16[128,32640]{1,0:T(8,128)(2,1)} %slice.178) | data formatting | bytes 16711680 | tf_op jit(solution)/shard_map/while/body/eval_jaxpr/reshape | solution.py:32
  512.9 4.4 fusion.32
  521.2 13.0 %convolution_convert_fusion = bf16[768,8192]{1,0:T(8,128)(2,1)} fusion(bf16[768,512]{0,1:T(8,128)(2,1)S(1)} %fusion.11, bf16[512,8192]{1,0:T(8,128)(2,1)} %param.16), kind=kOutput, calls=%fused_computation.10 | convolution fusion | flops 6448742400 | bytes 21757952 | tf_op jit(solution)/shard_map/dot_general | solution.py:88
  534.2 142.9 %reduce-scatter.2.cloned.1.call-done = bf16[48,8192]{1,0:T(8,128)(2,1)} async-done(((bf16[768,8192]{1,0:T(8,128)(2,1)}), bf16[48,8192]{1,0:T(8,128)(2,1)}) %reduce-scatter.2.cloned.1.call-update) | async-done | bytes 786448 | tf_op jit(solution)/shard_map/reduce_scatter | solution.py:87
  (119 shorter events, 86.1 us)
Async XLA Ops:
  6.5 10.9 %copy-start.1 = (bf16[768,512]{1,0:T(8,128)(2,1)S(1)}, bf16[768,512]{1,0:T(8,128)(2,1)}, u32[]{:S(2)}) copy-start(bf16[768,512]{1,0:T(8,128)(2,1)} %param.10) | copy-start | bytes 2359300
  6.5 670.6 %reduce-scatter.2.cloned.1.call-start = ((), (), s32[]{:S(2)}) async-start(), calls=%async_computation.1 | async-start | bytes 13369344 | tf_op jit(solution)/shard_map/reduce_scatter | solution.py:87
  8.2 15.1 %copy-start.6 = (bf16[3,512]{1,0:T(4,128)(2,1)S(1)}, bf16[3,512]{1,0:T(4,128)(2,1)}, u32[]{:S(2)}) copy-start(bf16[3,512]{1,0:T(4,128)(2,1)} %param.13) | copy-start | bytes 9220
  8.2 15.1 %collective-permute-start.1 = (bf16[130,512]{0,1:T(8,128)(2,1)S(1)}, bf16[130,512]{0,1:T(8,128)(2,1)S(1)}, u32[]{:S(2)}, u32[]{:S(2)}) collective-permute-start(bf16[130,512]{0,1:T(8,128)(2,1)S(1)} %slice.100), channel_id=1, source_target_pairs={{0,16},{16,32},{32,48},{48,64},{64,80},{80,96},{96,112},{112,128},... | collective-permute-start | bytes 399368 | tf_op jit(solution)/shard_map/ppermute | solution.py:12
  13.6 15.1 %collective-permute-start.2 = (bf16[130,512]{0,1:T(8,128)(2,1)S(1)}, bf16[130,512]{0,1:T(8,128)(2,1)S(1)}, u32[]{:S(2)}, u32[]{:S(2)}) collective-permute-start(bf16[130,512]{0,1:T(8,128)(2,1)S(1)} %slice.105), channel_id=1, source_target_pairs={{0,16},{16,32},{32,48},{48,64},{64,80},{80,96},{96,112},{112,128},... | collective-permute-start | bytes 399368 | tf_op jit(solution)/shard_map/ppermute | solution.py:12
  18.2 500.3 %collective-permute-start = (bf16[2,512]{0,1:T(8,128)(2,1)}, bf16[2,512]{0,1:T(8,128)(2,1)}, u32[]{:S(2)}, u32[]{:S(2)}) collective-permute-start(bf16[2,512]{0,1:T(8,128)(2,1)} %copy.18), channel_id=1, source_target_pairs={{0,16},{16,32},{32,48},{48,64},{64,80},{80,96},{96,112},{112,128},... | collective-permute-start | bytes 6152 | tf_op jit(solution)/shard_map/ppermute | solution.py:12
  23.2 7.7 %copy-start.3 = (f32[1,512]{1,0:T(1,128)}, f32[1,512]{1,0:T(1,128)S(1)}, u32[]{:S(2)}) copy-start(f32[1,512]{1,0:T(1,128)S(1)} %get-tuple-element.42) | copy-start | bytes 6148
  23.2 7.7 %copy-start.4 = (f32[1,512]{1,0:T(1,128)}, f32[1,512]{1,0:T(1,128)S(1)}, u32[]{:S(2)}) copy-start(f32[1,512]{1,0:T(1,128)S(1)} %get-tuple-element.43) | copy-start | bytes 6148
  23.3 7.7 %copy-start.5 = (f32[1,512]{1,0:T(1,128)}, f32[1,512]{1,0:T(1,128)S(1)}, u32[]{:S(2)}) copy-start(f32[1,512]{1,0:T(1,128)S(1)} %get-tuple-element.44) | copy-start | bytes 6148
  30.9 487.6 %copy-start = (bf16[768,512]{0,1:T(8,128)(2,1)S(1)}, bf16[768,512]{0,1:T(8,128)(2,1)}, u32[]{:S(2)}) copy-start(bf16[768,512]{0,1:T(8,128)(2,1)} %copy.17) | copy-start | bytes 2359300
  30.9 487.6 %copy-start.7 = (f32[512]{0:T(512)S(1)}, f32[512]{0:T(512)}, u32[]{:S(2)}) copy-start(f32[512]{0:T(512)} %param.15) | copy-start | bytes 6148
  534.2 142.9 %copy-start.2 = (bf16[48,8192]{1,0:T(8,128)(2,1)S(1)}, bf16[48,8192]{1,0:T(8,128)(2,1)}, u32[]{:S(2)}) copy-start(bf16[48,8192]{1,0:T(8,128)(2,1)} %param.17) | copy-start | bytes 2359300
Sparse Core Ops, SparseCore 0:
  534.4 142.7 reduce-scatter.1
where the time goes:
time: 688 us; the launch traced here: 686 us
  local copies, waits for them, and re-layouts  457 us (66%)
  waiting for transfers between devices  148 us (22%)
  matrix products  48.5 us (7%)
  between operations  13.6 us (2%)
  starting transfers between devices  11.5 us (2%)
  other arithmetic  7.11 us (1%)
    reshape x8, local copies, waits for them, and re-layouts, skewed_band(): return window.reshape(lane_width, tap_count, stride)[:, :, :tap_count]  236 us
    reduce_scatter x1, waiting for transfers between devices, body(): lax.psum_scatter(jnp.dot(gated, out_weight, preferred_element_type=jnp.fl...  143 us
    while x32, local copies, waits for them, and re-layouts  103 us
    slice x8, local copies, waits for them, and re-layouts, skewed_band(): window = tiled[:, tap_count - 1:tap_count - 1 + tap_count * stride]  72.3 us
    another operation x8, local copies, waits for them, and re-layouts, skewed_band(): tiled = jnp.tile(padded, (1, tap_count))  30.4 us
    dot_general x4, matrix products, one_group(): jnp.einsum('cim,bmc->bic', near_band, blocked[1:], preferred_element_type...  17.7 us
    dot_general x4, matrix products, one_group(): jnp.einsum('cim,bmc->bic', far_band, blocked[:-1], preferred_element_type...  17.7 us
  transfers between devices with their start and end apart: 4, of which 2 were waited for; matrix products, arithmetic and copies ran while one was open for 72% of the time, Pallas kernels for 0%

commit v1 on v0

v1 whole, which is shorter than its diff:
```python
import math
import functools
import numpy as np
import jax
import jax.numpy as jnp
from jax import lax
from jax.experimental import pallas as pl
from jax.experimental.pallas import tpu as pltpu
from jax.sharding import PartitionSpec as P

BLK = 128
N_Y, N_X, N_C = 4, 2, 2


def split_bf16(matrix):
    high = matrix.astype(jnp.bfloat16)
    low = (matrix - high.astype(np.float64)).astype(jnp.bfloat16)
    return high, low


def transform_tables(taps):
    span = 2 * taps
    freq = np.arange(taps)[:, None] + 0.5
    time = np.arange(span)[None, :]
    angle = 2.0 * np.pi * freq * time / span
    forward = np.concatenate([np.cos(angle), -np.sin(angle)], axis=0)
    inverse = (2.0 / span) * forward.T[taps:]
    f_high, f_low = split_bf16(forward)
    g_high, g_low = split_bf16(inverse)
    return np.concatenate([f_high, f_low], axis=0), np.concatenate([g_high, g_low], axis=0)


def short_filter(window, taps):
    rows = window.shape[0] - 16
    wide = window.astype(jnp.float32)
    total = taps[0:1] * wide[16 : 16 + rows]
    for j in range(1, taps.shape[0]):
        total = total + taps[j : j + 1] * wide[16 - j : 16 - j + rows]
    return total


def gate_kernel(place_ref, order_ref, q_ref, k_ref, v_ref, halo_ref, taps_ref, filt_ref, skip_ref, f_ref, g_ref, keep_ref, give_ref, prod_ref, gated_ref):
    rows = q_ref.shape[0]
    blocks = rows // BLK
    taps = taps_ref[...].astype(jnp.float32)
    skip = skip_ref[...]
    tail = BLK + 16

    def window(ref, base, b):
        if b == 0:
            return halo_ref[base : base + tail]
        if b == 1:
            return jnp.concatenate([halo_ref[base + BLK : base + tail], ref[0:BLK]], axis=0)
        return ref[(b - 1) * BLK - 16 : b * BLK]

    spec = lax.dot_general(
        f_ref[:, :BLK], filt_ref[...], (((1,), (1,)), ((), ())), preferred_element_type=jnp.float32
    )
    spec = spec[: 2 * BLK] + spec[2 * BLK :]
    h_re, h_im = spec[:BLK], spec[BLK:]
    for b in range(blocks + 1):
        prod = short_filter(window(k_ref, 16, b), taps) * short_filter(window(v_ref, 16 + tail, b), taps)
        prod_ref[b * BLK : (b + 1) * BLK] = prod.astype(jnp.bfloat16)
        if b == 0:
            continue
        x = jnp.dot(f_ref[...], prod_ref[(b - 1) * BLK : (b + 1) * BLK], preferred_element_type=jnp.float32)
        x = x[: 2 * BLK] + x[2 * BLK :]
        x_re, x_im = x[:BLK], x[BLK:]
        y = jnp.concatenate([x_re * h_re - x_im * h_im, x_re * h_im + x_im * h_re], axis=0)
        y_high = y.astype(jnp.bfloat16)
        y_low = (y - y_high.astype(jnp.float32)).astype(jnp.bfloat16)
        z = jnp.dot(g_ref[...], y_high, preferred_element_type=jnp.float32)
        z = z[:BLK] + z[BLK:] + jnp.dot(g_ref[:BLK], y_low, preferred_element_type=jnp.float32)
        own = prod_ref[b * BLK : (b + 1) * BLK].astype(jnp.float32)
        if b == 1:
            q_win = jnp.concatenate([halo_ref[0:16], q_ref[0:BLK]], axis=0)
        else:
            q_win = q_ref[(b - 1) * BLK - 16 : b * BLK]
        gated = short_filter(q_win, taps) * (z + skip * own)
        gated_ref[(b - 1) * BLK : b * BLK] = gated.astype(jnp.bfloat16)

    slots = N_Y * N_X
    piece = keep_ref.shape[0] // slots
    for slot in range(slots):
        for which, ref in ((0, keep_ref), (1, give_ref)):
            group = order_ref[(place_ref[0] * 2 + which) * slots + slot]
            start = pl.multiple_of(group * piece, 16)
            ref[slot * piece : (slot + 1) * piece] = gated_ref[pl.ds(start, piece)]


def row_order():
    table = []
    for y in range(N_Y):
        for x in range(N_X):
            for c in range(N_C):
                for dc in range(N_C):
                    for dx in range(N_X):
                        for dy in range(N_Y):
                            table.append((((y + dy) % N_Y) * N_X + (x + dx) % N_X) * N_C + (c + dc) % N_C)
    return np.array(table, np.int32)


def gate(place, queries, keys_in, values_in, halo, short_taps, filters, skip_gain):
    rows, channels = queries.shape
    width = 256
    f_tab, g_tab = transform_tables(filters.shape[1])
    col = lambda i, *_: (0, i)
    fixed = lambda i, *_: (0, 0)
    half = jax.ShapeDtypeStruct((rows // 2, channels), jnp.bfloat16)
    return pl.pallas_call(
        gate_kernel,
        grid_spec=pltpu.PrefetchScalarGridSpec(
            num_scalar_prefetch=2,
            grid=(channels // width,),
            in_specs=[
                pl.BlockSpec((rows, width), col),
                pl.BlockSpec((rows, width), col),
                pl.BlockSpec((rows, width), col),
                pl.BlockSpec((halo.shape[0], width), col),
                pl.BlockSpec((short_taps.shape[0], width), col),
                pl.BlockSpec((width, filters.shape[1]), lambda i, *_: (i, 0)),
                pl.BlockSpec((1, width), col),
                pl.BlockSpec(f_tab.shape, fixed),
                pl.BlockSpec(g_tab.shape, fixed),
            ],
            out_specs=[pl.BlockSpec((rows // 2, width), col)] * 2,
            scratch_shapes=[
                pltpu.VMEM((rows + BLK, width), jnp.bfloat16),
                pltpu.VMEM((rows, width), jnp.bfloat16),
            ],
        ),
        out_shape=[half, half],
        compiler_params=pltpu.CompilerParams(vmem_limit_bytes=32 * 1024 * 1024),
        cost_estimate=pl.CostEstimate(flops=6 * 10**9, bytes_accessed=4 * 10**6, transcendentals=0),
        name="gate",
    )(place, jnp.asarray(row_order()), queries, keys_in, values_in, halo, short_taps, filters, skip_gain[None, :], f_tab, g_tab)


TILE = 256


def project_kernel(pieces, a_ref, b_ref, wa_ref, wb_ref, *out_refs):
    acc = jnp.dot(a_ref[...], wa_ref[...], preferred_element_type=jnp.float32)
    acc = acc + jnp.dot(b_ref[...], wb_ref[...], preferred_element_type=jnp.float32)
    acc = acc.astype(jnp.bfloat16)
    for ref, spans in zip(out_refs, pieces):
        at = 0
        for start, stop in spans:
            ref[at : at + stop - start] = acc[start:stop]
            at += stop - start


def project(mine, theirs, weight, weight_pair, first, count, pieces):
    rows, depth = mine.shape
    sizes = [sum(stop - start for start, stop in spans) for spans in pieces]
    lhs = pl.BlockSpec((rows, depth), lambda j: (0, 0))
    rhs = pl.BlockSpec((depth, TILE), lambda j: (0, j + first // TILE))
    return pl.pallas_call(
        functools.partial(project_kernel, pieces),
        grid=(count // TILE,),
        out_shape=[jax.ShapeDtypeStruct((n, count), jnp.bfloat16) for n in sizes],
        in_specs=[lhs, lhs, rhs, rhs],
        out_specs=[pl.BlockSpec((n, TILE), lambda j: (0, j)) for n in sizes],
        compiler_params=pltpu.CompilerParams(vmem_limit_bytes=32 * 1024 * 1024),
        cost_estimate=pl.CostEstimate(
            flops=4 * rows * depth * count, bytes_accessed=2 * (2 * depth + rows) * count, transcendentals=0
        ),
        name="project",
    )(mine, theirs, weight, weight_pair)


def moved(dy=0, dx=0, dc=0):
    pairs = []
    for y in range(N_Y):
        for x in range(N_X):
            for c in range(N_C):
                source = (y * N_X + x) * N_C + c
                target = (((y + dy) % N_Y) * N_X + (x + dx) % N_X) * N_C + (c + dc) % N_C
                pairs.append((source, target))
    return pairs


def send(array, **step):
    return lax.ppermute(array, "tp", moved(**step))


def add(*arrays):
    total = arrays[0].astype(jnp.float32)
    for array in arrays[1:]:
        total = total + array.astype(jnp.float32)
    return total


def reduce_y(first, second):
    far_second = send(second[2], dy=1)
    far_first = send(first[2], dy=-1)
    up_first = send(first[1], dy=1)
    down_second = send(second[3], dy=-1)
    up_second = send(add(second[1], far_second).astype(jnp.bfloat16), dy=1)
    down_first = send(add(first[3], far_first).astype(jnp.bfloat16), dy=-1)
    return add(first[0], up_first, down_first), add(second[0], down_second, up_second)


X_FIRST = 1792


def body(queries, keys_in, values_in, short_taps, filters, skip_gain, out_weight, residual):
    rows = queries.shape[0]
    width = out_weight.shape[1]
    tail = filters.shape[1] + 16
    peers = lax.axis_size("ctx")
    piece = rows // (N_Y * N_X * N_C)
    weight_pair = send(out_weight, dc=1)
    rim = jnp.concatenate([queries[rows - 16 :], keys_in[rows - tail :], values_in[rows - tail :]])
    halo = lax.ppermute(rim, "ctx", [(i, i + 1) for i in range(peers - 1)])

    place = lax.axis_index("tp").astype(jnp.int32)[None]
    keep, give = gate(place, queries, keys_in, values_in, halo, short_taps, filters, skip_gain)
    theirs = send(give, dc=1)

    half = rows // (2 * N_C)
    by_x = (((0, half),), ((half, 2 * half),))
    by_y = tuple(((s * piece, (s + 1) * piece), (half + s * piece, half + (s + 1) * piece)) for s in range(N_Y))
    y_first = width // 2 - X_FIRST
    multiply = functools.partial(project, keep, theirs, out_weight, weight_pair)
    a0_keep, a0_give = multiply(0, X_FIRST, by_x)
    a0_got = send(a0_give, dx=1)
    b0 = multiply(2 * X_FIRST, y_first, by_y)
    b1 = multiply(2 * X_FIRST + y_first, y_first, by_y)
    a1_keep, a1_give = multiply(X_FIRST, X_FIRST, by_x)
    a1_got = send(a1_give, dx=1)

    b0_sum, b1_sum = reduce_y(b0, b1)
    b0_got = send(b0_sum[piece:].astype(jnp.bfloat16), dx=1)
    b1_got = send(b1_sum[piece:].astype(jnp.bfloat16), dx=1)

    def sections(keep_part, got):
        total = add(keep_part, got)
        return [total[: piece]] + [total[s * piece : (s + 1) * piece].astype(jnp.bfloat16) for s in range(1, N_Y)]

    a0_sum, a1_sum = reduce_y(sections(a0_keep, a0_got), sections(a1_keep, a1_got))
    summed = jnp.concatenate(
        [a0_sum, a1_sum, add(b0_sum[:piece], b0_got), add(b1_sum[:piece], b1_got)], axis=1
    )
    return (residual.astype(jnp.float32) + summed).astype(jnp.bfloat16)


def solution(mesh):
    in_specs = (
        P("ctx", "tp"),
        P("ctx", "tp"),
        P("ctx", "tp"),
        P(None, "tp"),
        P("tp", None),
        P("tp"),
        P("tp", None),
        P(("ctx", "tp"), None),
    )
    out_specs = P(("ctx", "tp"), None)
    return jax.shard_map(body, mesh=mesh, in_specs=in_specs, out_specs=out_specs, check_vma=False)
```

time: 688 us -> 117 us (0.17)
  local copies, waits for them, and re-layouts: 457 us -> 11.2 us
  waiting for transfers between devices: 148 us -> 48 us
  matrix products: 48.5 us -> 0 us
  Pallas kernels: 0 us -> 30.1 us
  between operations: 13.6 us -> 0.24 us
  starting transfers between devices: 11.5 us -> 24 us
    reshape x8 -> x0, local copies, waits for them, and re-layouts: 236 us -> none  [skewed_band(): return window.reshape(lane_width, tap_count, stride)[:, :, :tap_count]]
    reduce_scatter x1 -> x0, waiting for transfers between devices: 143 us -> none  [body(): lax.psum_scatter(jnp.dot(gated, out_weight, preferred_element_type=jnp.fl...]
    while x32 -> x0, local copies, waits for them, and re-layouts: 103 us -> none
    slice x28 -> x7, local copies, waits for them, and re-layouts: 75.4 us -> 2.67 us  [the longest x1 0.92 us: body(): values_in[rows - tail:]]
    dot_general x9 -> x0, matrix products: 48.5 us -> none  [the longest x4 17.7 us: one_group(): jnp.einsum('cim,bmc->bic', near_band, blocked[1:], preferred_element_type...]
    ppermute x3 -> x19, waiting for transfers between devices: 5.36 us -> 48 us  [the longest x18 36.2 us: send(): return lax.ppermute(array, 'tp', moved(**step))]
    another operation x8 -> x0, local copies, waits for them, and re-layouts: 30.4 us -> none  [skewed_band(): tiled = jnp.tile(padded, (1, tap_count))]
    pallas_call x0 -> x5, Pallas kernels: none -> 30.1 us  [the longest x4 25 us: project(): pl.pallas_call(functools.partial(project_kernel, pieces), grid=(count //...]
  transfers between devices with their start and end apart: 4 -> 19, of which waited for: 2 -> 9; matrix products, arithmetic and copies ran while one was open for 72% -> 3% of each run, Pallas kernels for 0% -> 20%
where the time goes in v1:
time: 117 us; the launch traced here: 116 us
  waiting for transfers between devices  48 us (41%)
  Pallas kernels  30.1 us (26%)
  starting transfers between devices  24 us (21%)
  local copies, waits for them, and re-layouts  11.2 us (10%)
  other arithmetic  2.16 us (2%)
    ppermute x18, waiting for transfers between devices, send(): return lax.ppermute(array, 'tp', moved(**step))  36.2 us
    pallas_call x4, Pallas kernels, project(): pl.pallas_call(functools.partial(project_kernel, pieces), grid=(count //...  25 us
    ppermute x18, starting transfers between devices, send(): return lax.ppermute(array, 'tp', moved(**step))  20.2 us
    ppermute x1, waiting for transfers between devices, body(): halo = lax.ppermute(rim, 'ctx', [(i, i + 1) for i in range(peers - 1)])  11.9 us
    unnamed x24, local copies, waits for them, and re-layouts  8.57 us
    pallas_call x1, Pallas kernels, gate(): pl.pallas_call(gate_kernel, grid_spec=pltpu.PrefetchScalarGridSpec(num_sc...  5.08 us
    ppermute x1, starting transfers between devices, body(): halo = lax.ppermute(rim, 'ctx', [(i, i + 1) for i in range(peers - 1)])  3.83 us
  transfers between devices with their start and end apart: 19, of which 9 were waited for; matrix products, arithmetic and copies ran while one was open for 3% of the time, Pallas kernels for 20%

profile of v1, /device:TPU:4, one launch (start us, length us, event | category | flops | bytes accessed | tf_op | source)
XLA Modules:
  0.0 115.8 jit_solution(18117731906926618878)
XLA Ops:
  0.0 0.9 slice.54
  0.9 0.9 slice.55
  2.6 3.8 %collective-permute-start = (bf16[304,512]{1,0:T(8,128)(2,1)S(1)}, bf16[304,512]{1,0:T(8,128)(2,1)S(1)}, u32[]{:S(2)}, u32[]{:S(2)}) collective-permute-start(bf16[304,512]{1,0:T(8,128)(2,1)S(1)} %pad_maximum_fusion), channel_id=1, source_target_pairs={{0,16},{16,32},{32,48},{48,64},{64,80},{80,96},{96,112},{112,128},... | collective-permute-start | bytes 933896 | tf_op jit(solution)/shard_map/ppermute | solution.py:215
  6.4 11.9 %collective-permute-done.halo_ref = bf16[304,512]{1,0:T(8,128)(2,1)S(1)} collective-permute-done((bf16[304,512]{1,0:T(8,128)(2,1)S(1)}, bf16[304,512]{1,0:T(8,128)(2,1)S(1)}, u32[]{:S(2)}, u32[]{:S(2)}) %collective-permute-start) | collective-permute-done | bytes 311328 | tf_op jit(solution)/shard_map/ppermute | solution.py:215
  18.3 1.3 %copy-done = bf16[768,512]{1,0:T(8,128)(2,1)S(1)} copy-done((bf16[768,512]{1,0:T(8,128)(2,1)S(1)}, bf16[768,512]{1,0:T(8,128)(2,1)}, u32[]{:S(2)}) %copy-start) | copy-done | bytes 786456
  19.6 1.3 %copy-done.1 = bf16[768,512]{1,0:T(8,128)(2,1)S(1)} copy-done((bf16[768,512]{1,0:T(8,128)(2,1)S(1)}, bf16[768,512]{1,0:T(8,128)(2,1)}, u32[]{:S(2)}) %copy-start.1) | copy-done | bytes 786456
  21.0 1.1 copy-done.2
  22.1 0.9 copy-done.3
  24.4 0.9 copy-done.6
  25.3 0.9 copy-done.7
  26.9 5.1 %gate.1 = (bf16[384,512]{1,0:T(8,128)(2,1)S(1)}, bf16[384,512]{1,0:T(8,128)(2,1)S(1)}) custom-call(s32[1]{0:T(128)} %bitcast.place_ref, s32[256]{0:T(256)S(1)} %copy-done.8, bf16[768,512]{1,0:T(8,128)(2,1)S(1)} %copy-done.2, bf16[768,512]{1,0:T(8,128)(2,1)S(1)} %copy-done, bf16[768,512]{1,0:T(8,128)(2,1)S(1)} %copy-done.1, ...), custom_call_target="tpu_custom_call" | custom-call | flops 6000000000 | bytes 4000000 | tf_op jit(solution)/shard_map/gate/pallas_call | solution.py:110
  32.1 1.7 %collective-permute-done.1.b_ref = bf16[384,512]{1,0:T(8,128)(2,1)S(1)} collective-permute-done((bf16[384,512]{1,0:T(8,128)(2,1)S(1)}, bf16[384,512]{1,0:T(8,128)(2,1)S(1)}, u32[]{:S(2)}, u32[]{:S(2)}) %collective-permute-start.1) | collective-permute-done | bytes 393248 | tf_op jit(solution)/shard_map/ppermute | solution.py:184
  33.8 7.0 %project.6 = (bf16[96,2304]{1,0:T(8,128)(2,1)S(1)}, bf16[96,2304]{1,0:T(8,128)(2,1)S(1)}, bf16[96,2304]{1,0:T(8,128)(2,1)S(1)}, bf16[96,2304]{1,0:T(8,128)(2,1)S(1)}) custom-call(bf16[384,512]{1,0:T(8,128)(2,1)S(1)} %get-tuple-element.19.a_ref, bf16[384,512]{1,0:T(8,128)(2,1)S(1)} %collective-permute-done.1.b_ref, bf16[512,8192]{1,0:T(8,128)(2,1)S(1)} %bitcast.3, ...), custom_call_target="tpu_custom_call" | custom-call | flops 1811939328 | bytes 6488064 | tf_op jit(solution)/shard_map/project/pallas_call | solution.py:158
  40.8 3.1 %collective-permute-start.12 = (bf16[96,2304]{1,0:T(8,128)(2,1)S(1)}, bf16[96,2304]{1,0:T(8,128)(2,1)S(1)}, u32[]{:S(2)}, u32[]{:S(2)}) collective-permute-start(bf16[96,2304]{1,0:T(8,128)(2,1)S(1)} %get-tuple-element.28), channel_id=1, source_target_pairs={{0,12},{1,13},{2,14},{3,15},{4,0},{5,1},{6,2},{7,3},{8,4},{9,5},{1... | collective-permute-start | bytes 1327112 | tf_op jit(solution)/shard_map/ppermute | solution.py:184
  43.9 5.5 %project.4 = (bf16[192,1792]{1,0:T(8,128)(2,1)S(1)}, bf16[192,1792]{1,0:T(8,128)(2,1)S(1)}) custom-call(bf16[384,512]{1,0:T(8,128)(2,1)S(1)} %get-tuple-element.19.a_ref, bf16[384,512]{1,0:T(8,128)(2,1)S(1)} %collective-permute-done.1.b_ref, bf16[512,8192]{1,0:T(8,128)(2,1)S(1)} %bitcast.3, bf16[512,8192]{1,0:T(8,128)(2,1)} %collective-permute-done.2.wb_ref), custom_call_target="tpu_custom_call" | custom-call | flops 1409286144 | bytes 5046272 | tf_op jit(solution)/shard_map/project/pallas_call | solution.py:158
  49.4 2.2 %collective-permute-start.3 = (bf16[192,1792]{1,0:T(8,128)(2,1)S(1)}, bf16[192,1792]{1,0:T(8,128)(2,1)S(1)}, u32[]{:S(2)}, u32[]{:S(2)}) collective-permute-start(bf16[192,1792]{1,0:T(8,128)(2,1)S(1)} %get-tuple-element.22), channel_id=1, source_target_pairs={{0,2},{1,3},{2,0},{3,1},{4,6},{5,7},{6,4},{7,5},{8,10},{9,11},{10,... | collective-permute-start | bytes 2064392 | tf_op jit(solution)/shard_map/ppermute | solution.py:184
  51.6 5.5 %project.5 = (bf16[192,1792]{1,0:T(8,128)(2,1)S(1)}, bf16[192,1792]{1,0:T(8,128)(2,1)S(1)}) custom-call(bf16[384,512]{1,0:T(8,128)(2,1)S(1)} %get-tuple-element.19.a_ref, bf16[384,512]{1,0:T(8,128)(2,1)S(1)} %collective-permute-done.1.b_ref, bf16[512,8192]{1,0:T(8,128)(2,1)S(1)} %bitcast.3, bf16[512,8192]{1,0:T(8,128)(2,1)} %collective-permute-done.2.wb_ref), custom_call_target="tpu_custom_call" | custom-call | flops 1409286144 | bytes 5046272 | tf_op jit(solution)/shard_map/project/pallas_call | solution.py:158
  57.4 7.0 %project.7 = (bf16[96,2304]{1,0:T(8,128)(2,1)S(1)}, bf16[96,2304]{1,0:T(8,128)(2,1)S(1)}, bf16[96,2304]{1,0:T(8,128)(2,1)S(1)}, bf16[96,2304]{1,0:T(8,128)(2,1)S(1)}) custom-call(bf16[384,512]{1,0:T(8,128)(2,1)S(1)} %get-tuple-element.19.a_ref, bf16[384,512]{1,0:T(8,128)(2,1)S(1)} %collective-permute-done.1.b_ref, bf16[512,8192]{1,0:T(8,128)(2,1)S(1)} %bitcast.3, ...), custom_call_target="tpu_custom_call" | custom-call | flops 1811939328 | bytes 6488064 | tf_op jit(solution)/shard_map/project/pallas_call | solution.py:158
  65.0 2.7 %collective-permute-start.15 = (bf16[96,2304]{1,0:T(8,128)(2,1)S(1)}, bf16[96,2304]{1,0:T(8,128)(2,1)S(1)}, u32[]{:S(2)}, u32[]{:S(2)}) collective-permute-start(bf16[96,2304]{1,0:T(8,128)(2,1)S(1)} %get-tuple-element.30), channel_id=1, source_target_pairs={{0,12},{1,13},{2,14},{3,15},{4,0},{5,1},{6,2},{7,3},{8,4},{9,5},{1... | collective-permute-start | bytes 1327112 | tf_op jit(solution)/shard_map/ppermute | solution.py:184
  67.8 11.8 %collective-permute-done.16 = bf16[96,2304]{1,0:T(8,128)(2,1)S(1)} collective-permute-done((bf16[96,2304]{1,0:T(8,128)(2,1)S(1)}, bf16[96,2304]{1,0:T(8,128)(2,1)S(1)}, u32[]{:S(2)}, u32[]{:S(2)}) %collective-permute-start.16) | collective-permute-done | bytes 442400 | tf_op jit(solution)/shard_map/ppermute | solution.py:184
  79.8 2.1 %collective-permute-start.17 = (bf16[96,2304]{1,0:T(8,128)(2,1)S(1)}, bf16[96,2304]{1,0:T(8,128)(2,1)S(1)}, u32[]{:S(2)}, u32[]{:S(2)}) collective-permute-start(bf16[96,2304]{1,0:T(8,128)(2,1)S(1)} %add_convert_fusion), channel_id=1, source_target_pairs={{0,4},{1,5},{2,6},{3,7},{4,8},{5,9},{6,10},{7,11},{8,12},{9,13},{1... | collective-permute-start | bytes 1327112 | tf_op jit(solution)/shard_map/ppermute | solution.py:184
  82.1 1.3 %collective-permute-start.5 = (bf16[48,1792]{1,0:T(8,128)(2,1)S(1)}, bf16[48,1792]{1,0:T(8,128)(2,1)S(1)}, u32[]{:S(2)}, u32[]{:S(2)}) collective-permute-start(bf16[48,1792]{1,0:T(8,128)(2,1)S(1)} %get-tuple-element.38), channel_id=1, source_target_pairs={{0,12},{1,13},{2,14},{3,15},{4,0},{5,1},{6,2},{7,3},{8,4},{9,5},{1... | collective-permute-start | bytes 516104 | tf_op jit(solution)/shard_map/ppermute | solution.py:184
  83.6 10.5 %collective-permute-done.5 = bf16[48,1792]{1,0:T(8,128)(2,1)S(1)} collective-permute-done((bf16[48,1792]{1,0:T(8,128)(2,1)S(1)}, bf16[48,1792]{1,0:T(8,128)(2,1)S(1)}, u32[]{:S(2)}, u32[]{:S(2)}) %collective-permute-start.5) | collective-permute-done | bytes 172064 | tf_op jit(solution)/shard_map/ppermute | solution.py:184
  94.1 6.6 %collective-permute-done.9 = bf16[48,1792]{1,0:T(8,128)(2,1)S(1)} collective-permute-done((bf16[48,1792]{1,0:T(8,128)(2,1)S(1)}, bf16[48,1792]{1,0:T(8,128)(2,1)S(1)}, u32[]{:S(2)}, u32[]{:S(2)}) %collective-permute-start.9) | collective-permute-done | bytes 172064 | tf_op jit(solution)/shard_map/ppermute | solution.py:184
  100.8 3.3 %collective-permute-start.8 = (bf16[48,1792]{1,0:T(8,128)(2,1)S(1)}, bf16[48,1792]{1,0:T(8,128)(2,1)S(1)}, u32[]{:S(2)}, u32[]{:S(2)}) collective-permute-start(bf16[48,1792]{1,0:T(8,128)(2,1)S(1)} %get-tuple-element.39), channel_id=1, source_target_pairs={{0,12},{1,13},{2,14},{3,15},{4,0},{5,1},{6,2},{7,3},{8,4},{9,5},{1... | collective-permute-start | bytes 516104 | tf_op jit(solution)/shard_map/ppermute | solution.py:184
  104.4 2.0 %collective-permute-start.10 = (bf16[48,1792]{1,0:T(8,128)(2,1)S(1)}, bf16[48,1792]{1,0:T(8,128)(2,1)S(1)}, u32[]{:S(2)}, u32[]{:S(2)}) collective-permute-start(bf16[48,1792]{1,0:T(8,128)(2,1)S(1)} %add_convert_fusion.2), channel_id=1, source_target_pairs={{0,4},{1,5},{2,6},{3,7},{4,8},{5,9},{6,10},{7,11},{8,12},{9,13},{1... | collective-permute-start | bytes 516104 | tf_op jit(solution)/shard_map/ppermute | solution.py:184
  106.4 1.4 %collective-permute-start.14 = (bf16[48,2304]{1,0:T(8,128)(2,1)S(1)}, bf16[48,2304]{1,0:T(8,128)(2,1)S(1)}, u32[]{:S(2)}, u32[]{:S(2)}) collective-permute-start(bf16[48,2304]{1,0:T(8,128)(2,1)S(1)} %slice.93), channel_id=1, source_target_pairs={{0,2},{1,3},{2,0},{3,1},{4,6},{5,7},{6,4},{7,5},{8,10},{9,11},{10,... | collective-permute-start | bytes 663560 | tf_op jit(solution)/shard_map/ppermute | solution.py:184
  108.0 1.1 collective-permute-start.18
  109.6 1.5 %collective-permute-done.10 = bf16[48,1792]{1,0:T(8,128)(2,1)S(1)} collective-permute-done((bf16[48,1792]{1,0:T(8,128)(2,1)S(1)}, bf16[48,1792]{1,0:T(8,128)(2,1)S(1)}, u32[]{:S(2)}, u32[]{:S(2)}) %collective-permute-start.10) | collective-permute-done | bytes 172064 | tf_op jit(solution)/shard_map/ppermute | solution.py:184
  111.1 1.2 %collective-permute-done.14 = bf16[48,2304]{1,0:T(8,128)(2,1)S(1)} collective-permute-done((bf16[48,2304]{1,0:T(8,128)(2,1)S(1)}, bf16[48,2304]{1,0:T(8,128)(2,1)S(1)}, u32[]{:S(2)}, u32[]{:S(2)}) %collective-permute-start.14) | collective-permute-done | bytes 221216 | tf_op jit(solution)/shard_map/ppermute | solution.py:184
  112.4 2.3 %collective-permute-done.18 = bf16[48,2304]{1,0:T(8,128)(2,1)S(1)} collective-permute-done((bf16[48,2304]{1,0:T(8,128)(2,1)S(1)}, bf16[48,2304]{1,0:T(8,128)(2,1)S(1)}, u32[]{:S(2)}, u32[]{:S(2)}) %collective-permute-start.18) | collective-permute-done | bytes 221216 | tf_op jit(solution)/shard_map/ppermute | solution.py:184
  114.7 1.0 fusion
  (57 shorter events, 5.5 us)
Async XLA Ops:
  0.0 33.8 %collective-permute-start.2 = (bf16[512,8192]{1,0:T(8,128)(2,1)}, bf16[512,8192]{1,0:T(8,128)(2,1)}, u32[]{:S(2)}, u32[]{:S(2)}) collective-permute-start(bf16[512,8192]{1,0:T(8,128)(2,1)} %wa_ref.7), channel_id=1, source_target_pairs={{0,1},{1,0},{2,3},{3,2},{4,5},{5,4},{6,7},{7,6},{8,9},{9,8},{10,11... | collective-permute-start | bytes 25165832 | tf_op jit(solution)/shard_map/ppermute | solution.py:184
  2.6 15.7 %collective-permute-start = (bf16[304,512]{1,0:T(8,128)(2,1)S(1)}, bf16[304,512]{1,0:T(8,128)(2,1)S(1)}, u32[]{:S(2)}, u32[]{:S(2)}) collective-permute-start(bf16[304,512]{1,0:T(8,128)(2,1)S(1)} %pad_maximum_fusion), channel_id=1, source_target_pairs={{0,16},{16,32},{32,48},{48,64},{64,80},{80,96},{96,112},{112,128},... | collective-permute-start | bytes 933896 | tf_op jit(solution)/shard_map/ppermute | solution.py:215
  18.3 15.5 %slice-start = ((s8[8388608]{0:T(1024)(128)(4,1)}), s8[4194304]{0:T(1024)(128)(4,1)S(1)}, s32[]{:S(2)}) async-start(s8[8388608]{0:T(1024)(128)(4,1)} %bitcast.2), calls=%async_computation | async-start | bytes 8388608
  18.3 1.3 %copy-start = (bf16[768,512]{1,0:T(8,128)(2,1)S(1)}, bf16[768,512]{1,0:T(8,128)(2,1)}, u32[]{:S(2)}) copy-start(bf16[768,512]{1,0:T(8,128)(2,1)} %k_ref.1) | copy-start | bytes 2359300
  19.6 1.3 %copy-start.1 = (bf16[768,512]{1,0:T(8,128)(2,1)S(1)}, bf16[768,512]{1,0:T(8,128)(2,1)}, u32[]{:S(2)}) copy-start(bf16[768,512]{1,0:T(8,128)(2,1)} %v_ref.1) | copy-start | bytes 2359300
  21.0 1.1 copy-start.2
  22.1 0.9 copy-start.3
  23.0 0.7 copy-start.4
  23.7 0.7 copy-start.5
  24.4 0.9 copy-start.6
  25.3 0.9 copy-start.7
  26.2 0.7 copy-start.8
  26.9 6.9 %slice-start.1 = ((s8[8388608]{0:T(1024)(128)(4,1)}), s8[4194304]{0:T(1024)(128)(4,1)S(1)}, s32[]{:S(2)}) async-start(s8[8388608]{0:T(1024)(128)(4,1)} %bitcast.2), calls=%async_computation.1 | async-start | bytes 8388608
  32.0 1.8 %collective-permute-start.1 = (bf16[384,512]{1,0:T(8,128)(2,1)S(1)}, bf16[384,512]{1,0:T(8,128)(2,1)S(1)}, u32[]{:S(2)}, u32[]{:S(2)}) collective-permute-start(bf16[384,512]{1,0:T(8,128)(2,1)S(1)} %get-tuple-element.20), channel_id=1, source_target_pairs={{0,1},{1,0},{2,3},{3,2},{4,5},{5,4},{6,7},{7,6},{8,9},{9,8},{10,11... | collective-permute-start | bytes 1179656 | tf_op jit(solution)/shard_map/ppermute | solution.py:184
  40.8 24.2 %collective-permute-start.12 = (bf16[96,2304]{1,0:T(8,128)(2,1)S(1)}, bf16[96,2304]{1,0:T(8,128)(2,1)S(1)}, u32[]{:S(2)}, u32[]{:S(2)}) collective-permute-start(bf16[96,2304]{1,0:T(8,128)(2,1)S(1)} %get-tuple-element.28), channel_id=1, source_target_pairs={{0,12},{1,13},{2,14},{3,15},{4,0},{5,1},{6,2},{7,3},{8,4},{9,5},{1... | collective-permute-start | bytes 1327112 | tf_op jit(solution)/shard_map/ppermute | solution.py:184
  49.4 30.4 %collective-permute-start.3 = (bf16[192,1792]{1,0:T(8,128)(2,1)S(1)}, bf16[192,1792]{1,0:T(8,128)(2,1)S(1)}, u32[]{:S(2)}, u32[]{:S(2)}) collective-permute-start(bf16[192,1792]{1,0:T(8,128)(2,1)S(1)} %get-tuple-element.22), channel_id=1, source_target_pairs={{0,2},{1,3},{2,0},{3,1},{4,6},{5,7},{6,4},{7,5},{8,10},{9,11},{10,... | collective-permute-start | bytes 2064392 | tf_op jit(solution)/shard_map/ppermute | solution.py:184
  57.2 24.9 %collective-permute-start.7 = (bf16[192,1792]{1,0:T(8,128)(2,1)S(1)}, bf16[192,1792]{1,0:T(8,128)(2,1)S(1)}, u32[]{:S(2)}, u32[]{:S(2)}) collective-permute-start(bf16[192,1792]{1,0:T(8,128)(2,1)S(1)} %get-tuple-element.24), channel_id=1, source_target_pairs={{0,2},{1,3},{2,0},{3,1},{4,6},{5,7},{6,4},{7,5},{8,10},{9,11},{10,... | collective-permute-start | bytes 2064392 | tf_op jit(solution)/shard_map/ppermute | solution.py:184
  57.3 43.5 %collective-permute-start.11 = (bf16[96,2304]{1,0:T(8,128)(2,1)S(1)}, bf16[96,2304]{1,0:T(8,128)(2,1)S(1)}, u32[]{:S(2)}, u32[]{:S(2)}) collective-permute-start(bf16[96,2304]{1,0:T(8,128)(2,1)S(1)} %get-tuple-element.26), channel_id=1, source_target_pairs={{0,4},{1,5},{2,6},{3,7},{4,8},{5,9},{6,10},{7,11},{8,12},{9,13},{1... | collective-permute-start | bytes 1327112 | tf_op jit(solution)/shard_map/ppermute | solution.py:184
  64.3 15.3 %collective-permute-start.16 = (bf16[96,2304]{1,0:T(8,128)(2,1)S(1)}, bf16[96,2304]{1,0:T(8,128)(2,1)S(1)}, u32[]{:S(2)}, u32[]{:S(2)}) collective-permute-start(bf16[96,2304]{1,0:T(8,128)(2,1)S(1)} %get-tuple-element.32), channel_id=1, source_target_pairs={{0,4},{1,5},{2,6},{3,7},{4,8},{5,9},{6,10},{7,11},{8,12},{9,13},{1... | collective-permute-start | bytes 1327112 | tf_op jit(solution)/shard_map/ppermute | solution.py:184
  65.0 39.4 %collective-permute-start.15 = (bf16[96,2304]{1,0:T(8,128)(2,1)S(1)}, bf16[96,2304]{1,0:T(8,128)(2,1)S(1)}, u32[]{:S(2)}, u32[]{:S(2)}) collective-permute-start(bf16[96,2304]{1,0:T(8,128)(2,1)S(1)} %get-tuple-element.30), channel_id=1, source_target_pairs={{0,12},{1,13},{2,14},{3,15},{4,0},{5,1},{6,2},{7,3},{8,4},{9,5},{1... | collective-permute-start | bytes 1327112 | tf_op jit(solution)/shard_map/ppermute | solution.py:184
  79.7 24.4 %collective-permute-start.13 = (bf16[96,2304]{1,0:T(8,128)(2,1)S(1)}, bf16[96,2304]{1,0:T(8,128)(2,1)S(1)}, u32[]{:S(2)}, u32[]{:S(2)}) collective-permute-start(bf16[96,2304]{1,0:T(8,128)(2,1)S(1)} %add_convert_fusion.1), channel_id=1, source_target_pairs={{0,12},{1,13},{2,14},{3,15},{4,0},{5,1},{6,2},{7,3},{8,4},{9,5},{1... | collective-permute-start | bytes 1327112 | tf_op jit(solution)/shard_map/ppermute | solution.py:184
  79.8 26.6 %collective-permute-start.17 = (bf16[96,2304]{1,0:T(8,128)(2,1)S(1)}, bf16[96,2304]{1,0:T(8,128)(2,1)S(1)}, u32[]{:S(2)}, u32[]{:S(2)}) collective-permute-start(bf16[96,2304]{1,0:T(8,128)(2,1)S(1)} %add_convert_fusion), channel_id=1, source_target_pairs={{0,4},{1,5},{2,6},{3,7},{4,8},{5,9},{6,10},{7,11},{8,12},{9,13},{1... | collective-permute-start | bytes 1327112 | tf_op jit(solution)/shard_map/ppermute | solution.py:184
  82.1 12.0 %collective-permute-start.5 = (bf16[48,1792]{1,0:T(8,128)(2,1)S(1)}, bf16[48,1792]{1,0:T(8,128)(2,1)S(1)}, u32[]{:S(2)}, u32[]{:S(2)}) collective-permute-start(bf16[48,1792]{1,0:T(8,128)(2,1)S(1)} %get-tuple-element.38), channel_id=1, source_target_pairs={{0,12},{1,13},{2,14},{3,15},{4,0},{5,1},{6,2},{7,3},{8,4},{9,5},{1... | collective-permute-start | bytes 516104 | tf_op jit(solution)/shard_map/ppermute | solution.py:184
  94.1 6.6 %collective-permute-start.9 = (bf16[48,1792]{1,0:T(8,128)(2,1)S(1)}, bf16[48,1792]{1,0:T(8,128)(2,1)S(1)}, u32[]{:S(2)}, u32[]{:S(2)}) collective-permute-start(bf16[48,1792]{1,0:T(8,128)(2,1)S(1)} %get-tuple-element.40), channel_id=1, source_target_pairs={{0,4},{1,5},{2,6},{3,7},{4,8},{5,9},{6,10},{7,11},{8,12},{9,13},{1... | collective-permute-start | bytes 516104 | tf_op jit(solution)/shard_map/ppermute | solution.py:184
  100.7 7.3 %collective-permute-start.4 = (bf16[48,1792]{1,0:T(8,128)(2,1)S(1)}, bf16[48,1792]{1,0:T(8,128)(2,1)S(1)}, u32[]{:S(2)}, u32[]{:S(2)}) collective-permute-start(bf16[48,1792]{1,0:T(8,128)(2,1)S(1)} %get-tuple-element.37), channel_id=1, source_target_pairs={{0,4},{1,5},{2,6},{3,7},{4,8},{5,9},{6,10},{7,11},{8,12},{9,13},{1... | collective-permute-start | bytes 516104 | tf_op jit(solution)/shard_map/ppermute | solution.py:184
  100.8 8.8 %collective-permute-start.8 = (bf16[48,1792]{1,0:T(8,128)(2,1)S(1)}, bf16[48,1792]{1,0:T(8,128)(2,1)S(1)}, u32[]{:S(2)}, u32[]{:S(2)}) collective-permute-start(bf16[48,1792]{1,0:T(8,128)(2,1)S(1)} %get-tuple-element.39), channel_id=1, source_target_pairs={{0,12},{1,13},{2,14},{3,15},{4,0},{5,1},{6,2},{7,3},{8,4},{9,5},{1... | collective-permute-start | bytes 516104 | tf_op jit(solution)/shard_map/ppermute | solution.py:184
  104.1 5.4 %collective-permute-start.6 = (bf16[48,1792]{1,0:T(8,128)(2,1)S(1)}, bf16[48,1792]{1,0:T(8,128)(2,1)S(1)}, u32[]{:S(2)}, u32[]{:S(2)}) collective-permute-start(bf16[48,1792]{1,0:T(8,128)(2,1)S(1)} %add_convert_fusion.3), channel_id=1, source_target_pairs={{0,12},{1,13},{2,14},{3,15},{4,0},{5,1},{6,2},{7,3},{8,4},{9,5},{1... | collective-permute-start | bytes 516104 | tf_op jit(solution)/shard_map/ppermute | solution.py:184
  104.4 6.7 %collective-permute-start.10 = (bf16[48,1792]{1,0:T(8,128)(2,1)S(1)}, bf16[48,1792]{1,0:T(8,128)(2,1)S(1)}, u32[]{:S(2)}, u32[]{:S(2)}) collective-permute-start(bf16[48,1792]{1,0:T(8,128)(2,1)S(1)} %add_convert_fusion.2), channel_id=1, source_target_pairs={{0,4},{1,5},{2,6},{3,7},{4,8},{5,9},{6,10},{7,11},{8,12},{9,13},{1... | collective-permute-start | bytes 516104 | tf_op jit(solution)/shard_map/ppermute | solution.py:184
  106.4 5.9 %collective-permute-start.14 = (bf16[48,2304]{1,0:T(8,128)(2,1)S(1)}, bf16[48,2304]{1,0:T(8,128)(2,1)S(1)}, u32[]{:S(2)}, u32[]{:S(2)}) collective-permute-start(bf16[48,2304]{1,0:T(8,128)(2,1)S(1)} %slice.93), channel_id=1, source_target_pairs={{0,2},{1,3},{2,0},{3,1},{4,6},{5,7},{6,4},{7,5},{8,10},{9,11},{10,... | collective-permute-start | bytes 663560 | tf_op jit(solution)/shard_map/ppermute | solution.py:184
  108.0 6.7 %collective-permute-start.18 = (bf16[48,2304]{1,0:T(8,128)(2,1)S(1)}, bf16[48,2304]{1,0:T(8,128)(2,1)S(1)}, u32[]{:S(2)}, u32[]{:S(2)}) collective-permute-start(bf16[48,2304]{1,0:T(8,128)(2,1)S(1)} %slice.92), channel_id=1, source_target_pairs={{0,2},{1,3},{2,0},{3,1},{4,6},{5,7},{6,4},{7,5},{8,10},{9,11},{10,... | collective-permute-start | bytes 663560 | tf_op jit(solution)/shard_map/ppermute | solution.py:184
  111.1 3.7 %copy-start.9 = (bf16[48,8192]{1,0:T(8,128)(2,1)S(1)}, bf16[48,8192]{1,0:T(8,128)(2,1)}, u32[]{:S(2)}) copy-start(bf16[48,8192]{1,0:T(8,128)(2,1)} %param.18) | copy-start | bytes 2359300

commit v2 on v1

v2 whole, which is shorter than its diff:
```python
import math
import functools
import numpy as np
import jax
import jax.numpy as jnp
from jax import lax
from jax.experimental import pallas as pl
from jax.experimental.pallas import tpu as pltpu
from jax.sharding import PartitionSpec as P

BLK = 128
N_Y, N_X, N_C = 4, 2, 2


def split_bf16(matrix):
    high = matrix.astype(jnp.bfloat16)
    low = (matrix - high.astype(np.float64)).astype(jnp.bfloat16)
    return high, low


def transform_tables(taps):
    span = 2 * taps
    freq = np.arange(taps)[:, None] + 0.5
    time = np.arange(span)[None, :]
    angle = 2.0 * np.pi * freq * time / span
    forward = np.concatenate([np.cos(angle), -np.sin(angle)], axis=0)
    inverse = (2.0 / span) * forward.T[taps:]
    f_high, f_low = split_bf16(forward)
    g_high, g_low = split_bf16(inverse)
    return np.concatenate([f_high, f_low], axis=0), np.concatenate([g_high, g_low], axis=0)


def short_filter(wide, taps):
    rows = wide.shape[0] - 16
    total = taps[0:1] * wide[16 : 16 + rows]
    for j in range(1, taps.shape[0]):
        total = total + taps[j : j + 1] * wide[16 - j : 16 - j + rows]
    return total


def spectrum(f_ref, filt_ref):
    spec = lax.dot_general(
        f_ref[:, :BLK], filt_ref[...], (((1,), (1,)), ((), ())), preferred_element_type=jnp.float32
    )
    spec = spec[: 2 * BLK] + spec[2 * BLK :]
    return spec[:BLK], spec[BLK:]


def long_filter(span, h_re, h_im, f_ref, g_ref):
    x = jnp.dot(f_ref[...], span, preferred_element_type=jnp.float32)
    x = x[: 2 * BLK] + x[2 * BLK :]
    x_re, x_im = x[:BLK], x[BLK:]
    y = jnp.concatenate([x_re * h_re - x_im * h_im, x_re * h_im + x_im * h_re], axis=0)
    y_high = y.astype(jnp.bfloat16)
    y_low = (y - y_high.astype(jnp.float32)).astype(jnp.bfloat16)
    z = jnp.dot(g_ref[...], y_high, preferred_element_type=jnp.float32)
    return z[:BLK] + z[BLK:] + jnp.dot(g_ref[:BLK], y_low, preferred_element_type=jnp.float32)


def window(ref, b):
    return ref[b * BLK - 16 : (b + 1) * BLK].astype(jnp.float32)


def rim_kernel(q_ref, k_ref, v_ref, taps_ref, out_ref):
    taps = taps_ref[...].astype(jnp.float32)
    tail = BLK + 16
    at = k_ref.shape[0] - tail
    k_win, v_win = k_ref[at:].astype(jnp.float32), v_ref[at:].astype(jnp.float32)
    out_ref[:BLK] = (short_filter(k_win, taps) * short_filter(v_win, taps)).astype(jnp.bfloat16)
    q_end = pltpu.roll(q_ref[...].astype(jnp.float32), 2, 0)
    k_end = pltpu.roll(k_win[BLK:], 4, 0)
    v_end = pltpu.roll(v_win[BLK:], 6, 0)
    row = lax.broadcasted_iota(jnp.int32, q_end.shape, 0)
    packed = jnp.where(row < 2, q_end, jnp.where(row < 4, k_end, v_end))
    out_ref[BLK:] = packed.astype(jnp.bfloat16)


def late_kernel(first, q_ref, k_ref, v_ref, taps_ref, filt_ref, skip_ref, f_ref, g_ref, out_ref, prod_ref):
    blocks = q_ref.shape[0] // BLK
    taps = taps_ref[...].astype(jnp.float32)
    skip = skip_ref[...]
    h_re, h_im = spectrum(f_ref, filt_ref)
    for b in range(first - 1, blocks):
        at = (b - first + 1) * BLK
        prod = short_filter(window(k_ref, b), taps) * short_filter(window(v_ref, b), taps)
        prod = prod.astype(jnp.bfloat16)
        prod_ref[at : at + BLK] = prod
        if b >= first:
            filtered = long_filter(prod_ref[at - BLK : at + BLK], h_re, h_im, f_ref, g_ref)
            gated = short_filter(window(q_ref, b), taps) * (filtered + skip * prod.astype(jnp.float32))
            out_ref[at - BLK : at] = gated.astype(jnp.bfloat16)


def early_kernel(
    place_ref, order_ref, q_ref, k_ref, v_ref, halo_ref, late_ref, taps_ref, filt_ref, skip_ref, f_ref, g_ref,
    keep_ref, give_ref, prod_ref, gated_ref,
):
    blocks = q_ref.shape[0] // BLK
    taps = taps_ref[...].astype(jnp.float32)
    skip = skip_ref[...]
    rim = halo_ref[BLK:].astype(jnp.float32)

    def rows_of(ref, b, turn):
        if b == 0:
            return jnp.concatenate([pltpu.roll(rim, turn, 0), ref[:BLK].astype(jnp.float32)], axis=0)
        return window(ref, b)

    h_re, h_im = spectrum(f_ref, filt_ref)
    prod_ref[:BLK] = halo_ref[:BLK]
    for b in range(blocks):
        prod = short_filter(rows_of(k_ref, b, 12), taps) * short_filter(rows_of(v_ref, b, 10), taps)
        prod = prod.astype(jnp.bfloat16)
        prod_ref[(b + 1) * BLK : (b + 2) * BLK] = prod
        filtered = long_filter(prod_ref[b * BLK : (b + 2) * BLK], h_re, h_im, f_ref, g_ref)
        gated = short_filter(rows_of(q_ref, b, 14), taps) * (filtered + skip * prod.astype(jnp.float32))
        gated_ref[b * BLK : (b + 1) * BLK] = gated.astype(jnp.bfloat16)
    gated_ref[blocks * BLK :] = late_ref[...]

    slots = N_Y * N_X
    piece = keep_ref.shape[0] // slots
    for slot in range(slots):
        for which, ref in ((0, keep_ref), (1, give_ref)):
            group = order_ref[(place_ref[0] * 2 + which) * slots + slot]
            start = pl.multiple_of(group * piece, 16)
            ref[slot * piece : (slot + 1) * piece] = gated_ref[pl.ds(start, piece)]


def row_order():
    table = []
    for y in range(N_Y):
        for x in range(N_X):
            for c in range(N_C):
                for dc in range(N_C):
                    for dx in range(N_X):
                        for dy in range(N_Y):
                            table.append((((y + dy) % N_Y) * N_X + (x + dx) % N_X) * N_C + (c + dc) % N_C)
    return np.array(table, np.int32)


VMEM_LIMIT = 24 * 1024 * 1024
EARLY = 2
WIDTH = 256


def stay(array):
    return pltpu.with_memory_space_constraint(array, pltpu.HBM)


def column_block(rows, index=0):
    return pl.BlockSpec((rows, WIDTH), lambda i, *_: (index, i))


def whole(shape):
    return pl.BlockSpec(shape, lambda i, *_: (0, 0))


def make_rim(queries, keys_in, values_in, short_taps):
    rows, channels = queries.shape
    part = rows // 4
    return pl.pallas_call(
        rim_kernel,
        grid=(channels // WIDTH,),
        out_shape=jax.ShapeDtypeStruct((BLK + 16, channels), jnp.bfloat16),
        in_specs=[
            column_block(16, rows // 16 - 1),
            column_block(part, rows // part - 1),
            column_block(part, rows // part - 1),
            column_block(short_taps.shape[0]),
        ],
        out_specs=column_block(BLK + 16),
        compiler_params=pltpu.CompilerParams(vmem_limit_bytes=VMEM_LIMIT),
        cost_estimate=pl.CostEstimate(flops=10**9, bytes_accessed=10**6, transcendentals=0),
        name="rim",
    )(stay(queries), stay(keys_in), stay(values_in), stay(short_taps))


def parameter_specs(short_taps, filters, tables):
    return [
        column_block(short_taps.shape[0]),
        pl.BlockSpec((WIDTH, filters.shape[1]), lambda i, *_: (i, 0)),
        column_block(1),
        whole(tables[0].shape),
        whole(tables[1].shape),
    ]


def gate_late(queries, keys_in, values_in, short_taps, filters, skip_gain, tables):
    rows, channels = queries.shape
    out_rows = rows - EARLY * BLK
    return pl.pallas_call(
        functools.partial(late_kernel, EARLY),
        grid=(channels // WIDTH,),
        out_shape=jax.ShapeDtypeStruct((out_rows, channels), jnp.bfloat16),
        in_specs=[column_block(rows)] * 3 + parameter_specs(short_taps, filters, tables),
        out_specs=column_block(out_rows),
        scratch_shapes=[pltpu.VMEM((out_rows + BLK, WIDTH), jnp.bfloat16)],
        compiler_params=pltpu.CompilerParams(vmem_limit_bytes=VMEM_LIMIT),
        cost_estimate=pl.CostEstimate(flops=4 * 10**9, bytes_accessed=3 * 10**6, transcendentals=0),
        name="gate_late",
    )(*map(stay, (queries, keys_in, values_in, short_taps, filters, skip_gain, *tables)))


def gate_early(place, queries, keys_in, values_in, halo, late, short_taps, filters, skip_gain, tables):
    rows, channels = queries.shape
    half = jax.ShapeDtypeStruct((rows // 2, channels), jnp.bfloat16)
    return pl.pallas_call(
        early_kernel,
        grid_spec=pltpu.PrefetchScalarGridSpec(
            num_scalar_prefetch=2,
            grid=(channels // WIDTH,),
            in_specs=[column_block(EARLY * BLK)] * 3
            + [column_block(halo.shape[0]), column_block(late.shape[0])]
            + parameter_specs(short_taps, filters, tables),
            out_specs=[column_block(rows // 2)] * 2,
            scratch_shapes=[
                pltpu.VMEM(((EARLY + 1) * BLK, WIDTH), jnp.bfloat16),
                pltpu.VMEM((rows, WIDTH), jnp.bfloat16),
            ],
        ),
        out_shape=[half, half],
        compiler_params=pltpu.CompilerParams(vmem_limit_bytes=VMEM_LIMIT),
        cost_estimate=pl.CostEstimate(flops=2 * 10**9, bytes_accessed=3 * 10**6, transcendentals=0),
        name="gate_early",
    )(
        place,
        jnp.asarray(row_order()),
        *map(stay, (queries, keys_in, values_in)),
        halo,
        late,
        *map(stay, (short_taps, filters, skip_gain, *tables)),
    )


def project_kernel(first, count, tile, pieces, a_ref, b_ref, wa_ref, wb_ref, *out_refs):
    depth = wa_ref.shape[0]

    def step(wa, wb, *outs):
        acc = jnp.dot(a_ref[...], wa[...], preferred_element_type=jnp.float32)
        acc = acc + jnp.dot(b_ref[...], wb[...], preferred_element_type=jnp.float32)
        acc = acc.astype(jnp.bfloat16)
        for ref, spans in zip(outs, pieces):
            at = 0
            for start, stop in spans:
                ref[at : at + stop - start] = acc[start:stop]
                at += stop - start

    rhs = pl.BlockSpec((depth, tile), lambda j: (0, j))
    pltpu.emit_pipeline(
        step,
        grid=(count // tile,),
        in_specs=[rhs, rhs],
        out_specs=[pl.BlockSpec((ref.shape[0], tile), lambda j: (0, j)) for ref in out_refs],
    )(wa_ref.at[:, pl.ds(first, count)], wb_ref.at[:, pl.ds(first, count)], *out_refs)


def project(mine, theirs, weight, weight_pair, first, count, tile, pieces):
    rows, depth = mine.shape
    sizes = [sum(stop - start for start, stop in spans) for spans in pieces]
    anywhere = pl.BlockSpec(memory_space=pl.ANY)
    return pl.pallas_call(
        functools.partial(project_kernel, first, count, tile, pieces),
        out_shape=[jax.ShapeDtypeStruct((n, count), jnp.bfloat16) for n in sizes],
        in_specs=[pl.BlockSpec(memory_space=pltpu.VMEM)] * 2 + [pl.BlockSpec(memory_space=pltpu.HBM)] * 2,
        out_specs=[anywhere] * len(sizes),
        compiler_params=pltpu.CompilerParams(vmem_limit_bytes=VMEM_LIMIT),
        cost_estimate=pl.CostEstimate(
            flops=4 * rows * depth * count, bytes_accessed=2 * (2 * depth + rows) * count, transcendentals=0
        ),
        name="project",
    )(mine, theirs, stay(weight), stay(weight_pair))


def moved(dy=0, dx=0, dc=0):
    pairs = []
    for y in range(N_Y):
        for x in range(N_X):
            for c in range(N_C):
                source = (y * N_X + x) * N_C + c
                target = (((y + dy) % N_Y) * N_X + (x + dx) % N_X) * N_C + (c + dc) % N_C
                pairs.append((source, target))
    return pairs


def send(array, **step):
    return lax.ppermute(array, "tp", moved(**step))


def add(*arrays):
    total = arrays[0].astype(jnp.float32)
    for array in arrays[1:]:
        total = total + array.astype(jnp.float32)
    return total


def reduce_y(first, second):
    far_second = send(second[2], dy=1)
    far_first = send(first[2], dy=-1)
    up_first = send(first[1], dy=1)
    down_second = send(second[3], dy=-1)
    up_second = send(add(second[1], far_second).astype(jnp.bfloat16), dy=1)
    down_first = send(add(first[3], far_first).astype(jnp.bfloat16), dy=-1)
    return add(first[0], up_first, down_first), add(second[0], down_second, up_second)


X_FIRST = 1792


def body(queries, keys_in, values_in, short_taps, filters, skip_gain, out_weight, residual):
    rows = queries.shape[0]
    width = out_weight.shape[1]
    peers = lax.axis_size("ctx")
    piece = rows // (N_Y * N_X * N_C)
    weight_pair = send(out_weight, dc=1)
    rim = make_rim(queries, keys_in, values_in, short_taps)
    halo = lax.ppermute(rim, "ctx", [(i, i + 1) for i in range(peers - 1)])
    parameters = (short_taps, filters, skip_gain[None, :], transform_tables(filters.shape[1]))
    late = gate_late(queries, keys_in, values_in, *parameters)
    place = lax.axis_index("tp").astype(jnp.int32)[None]
    keep, give = gate_early(place, queries, keys_in, values_in, halo, late, *parameters)
    theirs = send(give, dc=1)

    half = rows // (2 * N_C)
    by_x = (((0, half),), ((half, 2 * half),))
    by_y = tuple(((s * piece, (s + 1) * piece), (half + s * piece, half + (s + 1) * piece)) for s in range(N_Y))
    y_first = width // 2 - X_FIRST

    def multiply(after, *where):
        left = lax.optimization_barrier((keep, after))[0]
        return project(left, theirs, out_weight, weight_pair, *where)

    a0_keep, a0_give = multiply(place, 0, X_FIRST, X_FIRST // 2, by_x)
    a0_got = send(a0_give, dx=1)
    b0 = multiply(a0_keep, 2 * X_FIRST, y_first, y_first // 3, by_y)
    b1 = multiply(b0[0], 2 * X_FIRST + y_first, y_first, y_first // 3, by_y)
    a1_keep, a1_give = multiply(b1[0], X_FIRST, X_FIRST, X_FIRST // 2, by_x)
    a1_got = send(a1_give, dx=1)

    b0_sum, b1_sum = reduce_y(b0, b1)
    b0_got = send(b0_sum[piece:].astype(jnp.bfloat16), dx=1)
    b1_got = send(b1_sum[piece:].astype(jnp.bfloat16), dx=1)

    def sections(keep_part, got):
        total = add(keep_part, got)
        return [total[: piece]] + [total[s * piece : (s + 1) * piece].astype(jnp.bfloat16) for s in range(1, N_Y)]

    a0_sum, a1_sum = reduce_y(sections(a0_keep, a0_got), sections(a1_keep, a1_got))
    summed = jnp.concatenate(
        [a0_sum, a1_sum, add(b0_sum[:piece], b0_got), add(b1_sum[:piece], b1_got)], axis=1
    )
    return (residual.astype(jnp.float32) + summed).astype(jnp.bfloat16)


def solution(mesh):
    in_specs = (
        P("ctx", "tp"),
        P("ctx", "tp"),
        P("ctx", "tp"),
        P(None, "tp"),
        P("tp", None),
        P("tp"),
        P("tp", None),
        P(("ctx", "tp"), None),
    )
    out_specs = P(("ctx", "tp"), None)
    return jax.shard_map(body, mesh=mesh, in_specs=in_specs, out_specs=out_specs, check_vma=False)
```

time: 117 us -> 92.1 us (0.79)
  local copies, waits for them, and re-layouts: 11.2 us -> 0.11 us
  waiting for transfers between devices: 48 us -> 42.3 us
  Pallas kernels: 30.1 us -> 25.4 us
  starting transfers between devices: 24 us -> 21.7 us
    unnamed x24 -> x4, local copies, waits for them, and re-layouts: 8.57 us -> 0.01 us
    ppermute x1, waiting for transfers between devices: 11.9 us -> 4.4 us  [body(): halo = lax.ppermute(rim, 'ctx', [(i, i + 1) for i in range(peers - 1)])]
    pallas_call x5 -> x7, Pallas kernels: 30.1 us -> 25.4 us  [the longest x4 16.6 us: project(): pl.pallas_call(functools.partial(project_kernel, first, count, tile, piec...]
    slice x3 -> x0, local copies, waits for them, and re-layouts: 2.57 us -> none  [the longest x1 0.92 us: body(): values_in[rows - tail:]]
    ppermute x18, starting transfers between devices: 20.2 us -> 17.8 us  [send(): return lax.ppermute(array, 'tp', moved(**step))]
    ppermute x18, waiting for transfers between devices: 36.2 us -> 37.9 us  [send(): return lax.ppermute(array, 'tp', moved(**step))]
  transfers between devices with their start and end apart: 19 -> 19, of which waited for: 9 -> 11; matrix products, arithmetic and copies ran while one was open for 3% -> 1% of each run, Pallas kernels for 20% -> 19%
where the time goes in v2:
time: 92.1 us; the launch traced here: 91.8 us
  waiting for transfers between devices  42.3 us (46%)
  Pallas kernels  25.4 us (28%)
  starting transfers between devices  21.7 us (24%)
  other arithmetic  2.16 us (2%)
    ppermute x18, waiting for transfers between devices, send(): return lax.ppermute(array, 'tp', moved(**step))  37.9 us
    ppermute x18, starting transfers between devices, send(): return lax.ppermute(array, 'tp', moved(**step))  17.8 us
    pallas_call x4, Pallas kernels, project(): pl.pallas_call(functools.partial(project_kernel, first, count, tile, piec...  16.6 us
    ppermute x1, waiting for transfers between devices, body(): halo = lax.ppermute(rim, 'ctx', [(i, i + 1) for i in range(peers - 1)])  4.4 us
    pallas_call x1, Pallas kernels, gate_late(): pl.pallas_call(functools.partial(late_kernel, EARLY), grid=(channels // W...  3.95 us
    ppermute x1, starting transfers between devices, body(): halo = lax.ppermute(rim, 'ctx', [(i, i + 1) for i in range(peers - 1)])  3.83 us
    pallas_call x1, Pallas kernels, gate_early(): pl.pallas_call(early_kernel, grid_spec=pltpu.PrefetchScalarGridSpec(num_s...  3.58 us
  transfers between devices with their start and end apart: 19, of which 11 were waited for; matrix products, arithmetic and copies ran while one was open for 1% of the time, Pallas kernels for 19%

profile of v2, /device:TPU:4, one launch (start us, length us, event | category | flops | bytes accessed | tf_op | source)
XLA Modules:
  0.0 91.8 jit_solution(17727798546576639285)
XLA Ops:
  0.0 1.2 %rim.1 = bf16[144,512]{1,0:T(8,128)(2,1)S(1)} custom-call(bf16[768,512]{1,0:T(8,128)(2,1)} %q_ref.5, bf16[768,512]{1,0:T(8,128)(2,1)} %k_ref.5, bf16[768,512]{1,0:T(8,128)(2,1)} %v_ref.5, bf16[3,512]{1,0:T(4,128)(2,1)} %taps_ref.5), custom_call_target="tpu_custom_call" | custom-call | flops 1000000000 | bytes 1000000 | tf_op jit(solution)/shard_map/rim/pallas_call | solution.py:160
  1.3 3.8 %collective-permute-start = (bf16[144,512]{1,0:T(8,128)(2,1)S(1)}, bf16[144,512]{1,0:T(8,128)(2,1)S(1)}, u32[]{:S(2)}, u32[]{:S(2)}) collective-permute-start(bf16[144,512]{1,0:T(8,128)(2,1)S(1)} %rim.1), channel_id=1, source_target_pairs={{0,16},{16,32},{32,48},{48,64},{64,80},{80,96},{96,112},{112,128},... | collective-permute-start | bytes 442376 | tf_op jit(solution)/shard_map/ppermute | solution.py:315
  5.1 4.0 %gate_late.1.late_ref = bf16[512,512]{1,0:T(8,128)(2,1)S(1)} custom-call(bf16[768,512]{1,0:T(8,128)(2,1)} %q_ref.5, bf16[768,512]{1,0:T(8,128)(2,1)} %k_ref.5, bf16[768,512]{1,0:T(8,128)(2,1)} %v_ref.5, bf16[3,512]{1,0:T(4,128)(2,1)} %taps_ref.5, bf16[512,128]{1,0:T(8,128)(2,1)} %filt_ref.3, f32[1,512]{1,0:T(1,128)} %bitcast.2, ...), custom_call_target="tpu_custom_call" | custom-call | flops 4000000000 | bytes 3000000 | tf_op jit(solution)/shard_map/gate_late/pallas_call | solution.py:190
  9.1 4.4 %collective-permute-done.halo_ref = bf16[144,512]{1,0:T(8,128)(2,1)S(1)} collective-permute-done((bf16[144,512]{1,0:T(8,128)(2,1)S(1)}, bf16[144,512]{1,0:T(8,128)(2,1)S(1)}, u32[]{:S(2)}, u32[]{:S(2)}) %collective-permute-start) | collective-permute-done | bytes 147488 | tf_op jit(solution)/shard_map/ppermute | solution.py:315
  13.5 3.6 %gate_early.1 = (bf16[384,512]{1,0:T(8,128)(2,1)S(1)}, bf16[384,512]{1,0:T(8,128)(2,1)S(1)}) custom-call(s32[1]{0:T(128)} %bitcast.place_ref, s32[256]{0:T(256)S(1)} %copy-done, bf16[768,512]{1,0:T(8,128)(2,1)} %q_ref.5, bf16[768,512]{1,0:T(8,128)(2,1)} %k_ref.5, bf16[768,512]{1,0:T(8,128)(2,1)} %v_ref.5, ...), custom_call_target="tpu_custom_call" | custom-call | flops 2000000000 | bytes 3000000 | tf_op jit(solution)/shard_map/gate_early/pallas_call | solution.py:206
  17.2 1.7 %collective-permute-done.1.b_ref = bf16[384,512]{1,0:T(8,128)(2,1)S(1)} collective-permute-done((bf16[384,512]{1,0:T(8,128)(2,1)S(1)}, bf16[384,512]{1,0:T(8,128)(2,1)S(1)}, u32[]{:S(2)}, u32[]{:S(2)}) %collective-permute-start.1) | collective-permute-done | bytes 393248 | tf_op jit(solution)/shard_map/ppermute | solution.py:285
  18.9 3.7 %project.4 = (bf16[192,1792]{1,0:T(8,128)(2,1)S(1)}, bf16[192,1792]{1,0:T(8,128)(2,1)S(1)}) custom-call(bf16[384,512]{1,0:T(8,128)(2,1)S(1)} %get-tuple-element.32.a_ref, bf16[384,512]{1,0:T(8,128)(2,1)S(1)} %collective-permute-done.1.b_ref, bf16[512,8192]{1,0:T(8,128)(2,1)} %wa_ref.7, bf16[512,8192]{1,0:T(8,128)(2,1)} %collective-permute-done.2.wb_ref), custom_call_target="tpu_custom_call" | custom-call | flops 1409286144 | bytes 5046272 | tf_op jit(solution)/shard_map/project/pallas_call | solution.py:260
  22.6 4.6 %project.5 = (bf16[96,2304]{1,0:T(8,128)(2,1)S(1)}, bf16[96,2304]{1,0:T(8,128)(2,1)S(1)}, bf16[96,2304]{1,0:T(8,128)(2,1)S(1)}, bf16[96,2304]{1,0:T(8,128)(2,1)S(1)}) custom-call(bf16[384,512]{1,0:T(8,128)(2,1)S(1)} %get-tuple-element.32.a_ref, bf16[384,512]{1,0:T(8,128)(2,1)S(1)} %collective-permute-done.1.b_ref, bf16[512,8192]{1,0:T(8,128)(2,1)} %wa_ref.7, ...), custom_call_target="tpu_custom_call" | custom-call | flops 1811939328 | bytes 6488064 | tf_op jit(solution)/shard_map/project/pallas_call | solution.py:260
  27.2 3.1 %collective-permute-start.12 = (bf16[96,2304]{1,0:T(8,128)(2,1)S(1)}, bf16[96,2304]{1,0:T(8,128)(2,1)S(1)}, u32[]{:S(2)}, u32[]{:S(2)}) collective-permute-start(bf16[96,2304]{1,0:T(8,128)(2,1)S(1)} %get-tuple-element.37), channel_id=1, source_target_pairs={{0,12},{1,13},{2,14},{3,15},{4,0},{5,1},{6,2},{7,3},{8,4},{9,5},{1... | collective-permute-start | bytes 1327112 | tf_op jit(solution)/shard_map/ppermute | solution.py:285
  30.3 2.1 %collective-permute-start.3 = (bf16[192,1792]{1,0:T(8,128)(2,1)S(1)}, bf16[192,1792]{1,0:T(8,128)(2,1)S(1)}, u32[]{:S(2)}, u32[]{:S(2)}) collective-permute-start(bf16[192,1792]{1,0:T(8,128)(2,1)S(1)} %get-tuple-element.27), channel_id=1, source_target_pairs={{0,2},{1,3},{2,0},{3,1},{4,6},{5,7},{6,4},{7,5},{8,10},{9,11},{10,... | collective-permute-start | bytes 2064392 | tf_op jit(solution)/shard_map/ppermute | solution.py:285
  32.4 4.6 %project.6 = (bf16[96,2304]{1,0:T(8,128)(2,1)S(1)}, bf16[96,2304]{1,0:T(8,128)(2,1)S(1)}, bf16[96,2304]{1,0:T(8,128)(2,1)S(1)}, bf16[96,2304]{1,0:T(8,128)(2,1)S(1)}) custom-call(bf16[384,512]{1,0:T(8,128)(2,1)S(1)} %get-tuple-element.32.a_ref, bf16[384,512]{1,0:T(8,128)(2,1)S(1)} %collective-permute-done.1.b_ref, bf16[512,8192]{1,0:T(8,128)(2,1)} %wa_ref.7, ...), custom_call_target="tpu_custom_call" | custom-call | flops 1811939328 | bytes 6488064 | tf_op jit(solution)/shard_map/project/pallas_call | solution.py:260
  37.0 3.3 %collective-permute-start.15 = (bf16[96,2304]{1,0:T(8,128)(2,1)S(1)}, bf16[96,2304]{1,0:T(8,128)(2,1)S(1)}, u32[]{:S(2)}, u32[]{:S(2)}) collective-permute-start(bf16[96,2304]{1,0:T(8,128)(2,1)S(1)} %get-tuple-element.38), channel_id=1, source_target_pairs={{0,12},{1,13},{2,14},{3,15},{4,0},{5,1},{6,2},{7,3},{8,4},{9,5},{1... | collective-permute-start | bytes 1327112 | tf_op jit(solution)/shard_map/ppermute | solution.py:285
  40.3 3.7 %project.7 = (bf16[192,1792]{1,0:T(8,128)(2,1)S(1)}, bf16[192,1792]{1,0:T(8,128)(2,1)S(1)}) custom-call(bf16[384,512]{1,0:T(8,128)(2,1)S(1)} %get-tuple-element.32.a_ref, bf16[384,512]{1,0:T(8,128)(2,1)S(1)} %collective-permute-done.1.b_ref, bf16[512,8192]{1,0:T(8,128)(2,1)} %wa_ref.7, bf16[512,8192]{1,0:T(8,128)(2,1)} %collective-permute-done.2.wb_ref), custom_call_target="tpu_custom_call" | custom-call | flops 1409286144 | bytes 5046272 | tf_op jit(solution)/shard_map/project/pallas_call | solution.py:260
  44.3 10.5 %collective-permute-done.16 = bf16[96,2304]{1,0:T(8,128)(2,1)S(1)} collective-permute-done((bf16[96,2304]{1,0:T(8,128)(2,1)S(1)}, bf16[96,2304]{1,0:T(8,128)(2,1)S(1)}, u32[]{:S(2)}, u32[]{:S(2)}) %collective-permute-start.16) | collective-permute-done | bytes 442400 | tf_op jit(solution)/shard_map/ppermute | solution.py:285
  54.9 2.3 %collective-permute-start.17 = (bf16[96,2304]{1,0:T(8,128)(2,1)S(1)}, bf16[96,2304]{1,0:T(8,128)(2,1)S(1)}, u32[]{:S(2)}, u32[]{:S(2)}) collective-permute-start(bf16[96,2304]{1,0:T(8,128)(2,1)S(1)} %add_convert_fusion), channel_id=1, source_target_pairs={{0,4},{1,5},{2,6},{3,7},{4,8},{5,9},{6,10},{7,11},{8,12},{9,13},{1... | collective-permute-start | bytes 1327112 | tf_op jit(solution)/shard_map/ppermute | solution.py:285
  57.1 0.2 fusion.3
  57.3 5.3 %collective-permute-done.7 = bf16[192,1792]{1,0:T(8,128)(2,1)S(1)} collective-permute-done((bf16[192,1792]{1,0:T(8,128)(2,1)S(1)}, bf16[192,1792]{1,0:T(8,128)(2,1)S(1)}, u32[]{:S(2)}, u32[]{:S(2)}) %collective-permute-start.7) | collective-permute-done | bytes 688160 | tf_op jit(solution)/shard_map/ppermute | solution.py:285
  62.6 0.9 collective-permute-start.5
  63.5 0.2 fusion.4
  63.7 5.5 %collective-permute-done.5 = bf16[48,1792]{1,0:T(8,128)(2,1)S(1)} collective-permute-done((bf16[48,1792]{1,0:T(8,128)(2,1)S(1)}, bf16[48,1792]{1,0:T(8,128)(2,1)S(1)}, u32[]{:S(2)}, u32[]{:S(2)}) %collective-permute-start.5) | collective-permute-done | bytes 172064 | tf_op jit(solution)/shard_map/ppermute | solution.py:285
  69.2 6.6 %collective-permute-done.9 = bf16[48,1792]{1,0:T(8,128)(2,1)S(1)} collective-permute-done((bf16[48,1792]{1,0:T(8,128)(2,1)S(1)}, bf16[48,1792]{1,0:T(8,128)(2,1)S(1)}, u32[]{:S(2)}, u32[]{:S(2)}) %collective-permute-start.9) | collective-permute-done | bytes 172064 | tf_op jit(solution)/shard_map/ppermute | solution.py:285
  75.9 3.3 %collective-permute-start.8 = (bf16[48,1792]{1,0:T(8,128)(2,1)S(1)}, bf16[48,1792]{1,0:T(8,128)(2,1)S(1)}, u32[]{:S(2)}, u32[]{:S(2)}) collective-permute-start(bf16[48,1792]{1,0:T(8,128)(2,1)S(1)} %get-tuple-element.47), channel_id=1, source_target_pairs={{0,12},{1,13},{2,14},{3,15},{4,0},{5,1},{6,2},{7,3},{8,4},{9,5},{1... | collective-permute-start | bytes 516104 | tf_op jit(solution)/shard_map/ppermute | solution.py:285
  79.3 0.1 convert_add_fusion.3
  79.5 2.0 %collective-permute-start.10 = (bf16[48,1792]{1,0:T(8,128)(2,1)S(1)}, bf16[48,1792]{1,0:T(8,128)(2,1)S(1)}, u32[]{:S(2)}, u32[]{:S(2)}) collective-permute-start(bf16[48,1792]{1,0:T(8,128)(2,1)S(1)} %add_convert_fusion.2), channel_id=1, source_target_pairs={{0,4},{1,5},{2,6},{3,7},{4,8},{5,9},{6,10},{7,11},{8,12},{9,13},{1... | collective-permute-start | bytes 516104 | tf_op jit(solution)/shard_map/ppermute | solution.py:285
  81.5 0.5 collective-permute-start.14
  82.1 0.1 convert_add_fusion.2
  82.3 1.6 %collective-permute-done.4 = bf16[48,1792]{1,0:T(8,128)(2,1)S(1)} collective-permute-done((bf16[48,1792]{1,0:T(8,128)(2,1)S(1)}, bf16[48,1792]{1,0:T(8,128)(2,1)S(1)}, u32[]{:S(2)}, u32[]{:S(2)}) %collective-permute-start.4) | collective-permute-done | bytes 172064 | tf_op jit(solution)/shard_map/ppermute | solution.py:285
  83.9 1.1 %collective-permute-done.6 = bf16[48,1792]{1,0:T(8,128)(2,1)S(1)} collective-permute-done((bf16[48,1792]{1,0:T(8,128)(2,1)S(1)}, bf16[48,1792]{1,0:T(8,128)(2,1)S(1)}, u32[]{:S(2)}, u32[]{:S(2)}) %collective-permute-start.6) | collective-permute-done | bytes 172064 | tf_op jit(solution)/shard_map/ppermute | solution.py:285
  85.2 1.1 %collective-permute-done.10 = bf16[48,1792]{1,0:T(8,128)(2,1)S(1)} collective-permute-done((bf16[48,1792]{1,0:T(8,128)(2,1)S(1)}, bf16[48,1792]{1,0:T(8,128)(2,1)S(1)}, u32[]{:S(2)}, u32[]{:S(2)}) %collective-permute-start.10) | collective-permute-done | bytes 172064 | tf_op jit(solution)/shard_map/ppermute | solution.py:285
  86.3 2.1 %collective-permute-done.14 = bf16[48,2304]{1,0:T(8,128)(2,1)S(1)} collective-permute-done((bf16[48,2304]{1,0:T(8,128)(2,1)S(1)}, bf16[48,2304]{1,0:T(8,128)(2,1)S(1)}, u32[]{:S(2)}, u32[]{:S(2)}) %collective-permute-start.14) | collective-permute-done | bytes 221216 | tf_op jit(solution)/shard_map/ppermute | solution.py:285
  88.4 2.3 %collective-permute-done.18 = bf16[48,2304]{1,0:T(8,128)(2,1)S(1)} collective-permute-done((bf16[48,2304]{1,0:T(8,128)(2,1)S(1)}, bf16[48,2304]{1,0:T(8,128)(2,1)S(1)}, u32[]{:S(2)}, u32[]{:S(2)}) %collective-permute-start.18) | collective-permute-done | bytes 221216 | tf_op jit(solution)/shard_map/ppermute | solution.py:285
  90.8 1.0 %fusion = bf16[48,8192]{1,0:T(8,128)(2,1)} fusion(f32[48,2304]{1,0:T(8,128)S(1)} %slice_add_fusion, f32[48,2304]{1,0:T(8,128)S(1)} %slice_add_fusion.1, f32[48,1792]{1,0:T(8,128)S(1)} %fusion.1, f32[48,1792]{1,0:T(8,128)S(1)} %fusion.2, bf16[48,8192]{1,0:T(8,128)(2,1)S(1)} %copy-done.1), kind=kLoop, calls=%fused_computation.1 | loop fusion | flops 2359296 | bytes 3145728 | tf_op jit(solution)/shard_map/convert_element_type | solution.py:350
  (34 shorter events, 1.0 us)
Async XLA Ops:
  0.0 18.9 %collective-permute-start.2 = (bf16[512,8192]{1,0:T(8,128)(2,1)}, bf16[512,8192]{1,0:T(8,128)(2,1)}, u32[]{:S(2)}, u32[]{:S(2)}) collective-permute-start(bf16[512,8192]{1,0:T(8,128)(2,1)} %wa_ref.7), channel_id=1, source_target_pairs={{0,1},{1,0},{2,3},{3,2},{4,5},{5,4},{6,7},{7,6},{8,9},{9,8},{10,11... | collective-permute-start | bytes 25165832 | tf_op jit(solution)/shard_map/ppermute | solution.py:285
  1.3 12.2 %collective-permute-start = (bf16[144,512]{1,0:T(8,128)(2,1)S(1)}, bf16[144,512]{1,0:T(8,128)(2,1)S(1)}, u32[]{:S(2)}, u32[]{:S(2)}) collective-permute-start(bf16[144,512]{1,0:T(8,128)(2,1)S(1)} %rim.1), channel_id=1, source_target_pairs={{0,16},{16,32},{32,48},{48,64},{64,80},{80,96},{96,112},{112,128},... | collective-permute-start | bytes 442376 | tf_op jit(solution)/shard_map/ppermute | solution.py:315
  5.1 8.4 %copy-start = (s32[256]{0:T(256)S(1)}, s32[256]{0:T(256)}, u32[]{:S(2)}) copy-start(s32[256]{0:T(256)} %constant.12.clone.order_ref) | copy-start | bytes 3076
  17.1 1.8 %collective-permute-start.1 = (bf16[384,512]{1,0:T(8,128)(2,1)S(1)}, bf16[384,512]{1,0:T(8,128)(2,1)S(1)}, u32[]{:S(2)}, u32[]{:S(2)}) collective-permute-start(bf16[384,512]{1,0:T(8,128)(2,1)S(1)} %get-tuple-element.25), channel_id=1, source_target_pairs={{0,1},{1,0},{2,3},{3,2},{4,5},{5,4},{6,7},{7,6},{8,9},{9,8},{10,11... | collective-permute-start | bytes 1179656 | tf_op jit(solution)/shard_map/ppermute | solution.py:285
  27.2 16.8 %collective-permute-start.12 = (bf16[96,2304]{1,0:T(8,128)(2,1)S(1)}, bf16[96,2304]{1,0:T(8,128)(2,1)S(1)}, u32[]{:S(2)}, u32[]{:S(2)}) collective-permute-start(bf16[96,2304]{1,0:T(8,128)(2,1)S(1)} %get-tuple-element.37), channel_id=1, source_target_pairs={{0,12},{1,13},{2,14},{3,15},{4,0},{5,1},{6,2},{7,3},{8,4},{9,5},{1... | collective-permute-start | bytes 1327112 | tf_op jit(solution)/shard_map/ppermute | solution.py:285
  30.3 24.6 %collective-permute-start.3 = (bf16[192,1792]{1,0:T(8,128)(2,1)S(1)}, bf16[192,1792]{1,0:T(8,128)(2,1)S(1)}, u32[]{:S(2)}, u32[]{:S(2)}) collective-permute-start(bf16[192,1792]{1,0:T(8,128)(2,1)S(1)} %get-tuple-element.27), channel_id=1, source_target_pairs={{0,2},{1,3},{2,0},{3,1},{4,6},{5,7},{6,4},{7,5},{8,10},{9,11},{10,... | collective-permute-start | bytes 2064392 | tf_op jit(solution)/shard_map/ppermute | solution.py:285
  32.4 43.5 %collective-permute-start.11 = (bf16[96,2304]{1,0:T(8,128)(2,1)S(1)}, bf16[96,2304]{1,0:T(8,128)(2,1)S(1)}, u32[]{:S(2)}, u32[]{:S(2)}) collective-permute-start(bf16[96,2304]{1,0:T(8,128)(2,1)S(1)} %get-tuple-element.35), channel_id=1, source_target_pairs={{0,4},{1,5},{2,6},{3,7},{4,8},{5,9},{6,10},{7,11},{8,12},{9,13},{1... | collective-permute-start | bytes 1327112 | tf_op jit(solution)/shard_map/ppermute | solution.py:285
  37.0 42.5 %collective-permute-start.15 = (bf16[96,2304]{1,0:T(8,128)(2,1)S(1)}, bf16[96,2304]{1,0:T(8,128)(2,1)S(1)}, u32[]{:S(2)}, u32[]{:S(2)}) collective-permute-start(bf16[96,2304]{1,0:T(8,128)(2,1)S(1)} %get-tuple-element.38), channel_id=1, source_target_pairs={{0,12},{1,13},{2,14},{3,15},{4,0},{5,1},{6,2},{7,3},{8,4},{9,5},{1... | collective-permute-start | bytes 1327112 | tf_op jit(solution)/shard_map/ppermute | solution.py:285
  40.3 14.4 %collective-permute-start.16 = (bf16[96,2304]{1,0:T(8,128)(2,1)S(1)}, bf16[96,2304]{1,0:T(8,128)(2,1)S(1)}, u32[]{:S(2)}, u32[]{:S(2)}) collective-permute-start(bf16[96,2304]{1,0:T(8,128)(2,1)S(1)} %get-tuple-element.40), channel_id=1, source_target_pairs={{0,4},{1,5},{2,6},{3,7},{4,8},{5,9},{6,10},{7,11},{8,12},{9,13},{1... | collective-permute-start | bytes 1327112 | tf_op jit(solution)/shard_map/ppermute | solution.py:285
  44.1 18.5 %collective-permute-start.7 = (bf16[192,1792]{1,0:T(8,128)(2,1)S(1)}, bf16[192,1792]{1,0:T(8,128)(2,1)S(1)}, u32[]{:S(2)}, u32[]{:S(2)}) collective-permute-start(bf16[192,1792]{1,0:T(8,128)(2,1)S(1)} %get-tuple-element.34), channel_id=1, source_target_pairs={{0,2},{1,3},{2,0},{3,1},{4,6},{5,7},{6,4},{7,5},{8,10},{9,11},{10,... | collective-permute-start | bytes 2064392 | tf_op jit(solution)/shard_map/ppermute | solution.py:285
  54.7 24.5 %collective-permute-start.13 = (bf16[96,2304]{1,0:T(8,128)(2,1)S(1)}, bf16[96,2304]{1,0:T(8,128)(2,1)S(1)}, u32[]{:S(2)}, u32[]{:S(2)}) collective-permute-start(bf16[96,2304]{1,0:T(8,128)(2,1)S(1)} %add_convert_fusion.1), channel_id=1, source_target_pairs={{0,12},{1,13},{2,14},{3,15},{4,0},{5,1},{6,2},{7,3},{8,4},{9,5},{1... | collective-permute-start | bytes 1327112 | tf_op jit(solution)/shard_map/ppermute | solution.py:285
  54.9 26.7 %collective-permute-start.17 = (bf16[96,2304]{1,0:T(8,128)(2,1)S(1)}, bf16[96,2304]{1,0:T(8,128)(2,1)S(1)}, u32[]{:S(2)}, u32[]{:S(2)}) collective-permute-start(bf16[96,2304]{1,0:T(8,128)(2,1)S(1)} %add_convert_fusion), channel_id=1, source_target_pairs={{0,4},{1,5},{2,6},{3,7},{4,8},{5,9},{6,10},{7,11},{8,12},{9,13},{1... | collective-permute-start | bytes 1327112 | tf_op jit(solution)/shard_map/ppermute | solution.py:285
  62.6 6.6 %collective-permute-start.5 = (bf16[48,1792]{1,0:T(8,128)(2,1)S(1)}, bf16[48,1792]{1,0:T(8,128)(2,1)S(1)}, u32[]{:S(2)}, u32[]{:S(2)}) collective-permute-start(bf16[48,1792]{1,0:T(8,128)(2,1)S(1)} %get-tuple-element.46), channel_id=1, source_target_pairs={{0,12},{1,13},{2,14},{3,15},{4,0},{5,1},{6,2},{7,3},{8,4},{9,5},{1... | collective-permute-start | bytes 516104 | tf_op jit(solution)/shard_map/ppermute | solution.py:285
  69.2 6.7 %collective-permute-start.9 = (bf16[48,1792]{1,0:T(8,128)(2,1)S(1)}, bf16[48,1792]{1,0:T(8,128)(2,1)S(1)}, u32[]{:S(2)}, u32[]{:S(2)}) collective-permute-start(bf16[48,1792]{1,0:T(8,128)(2,1)S(1)} %get-tuple-element.48), channel_id=1, source_target_pairs={{0,4},{1,5},{2,6},{3,7},{4,8},{5,9},{6,10},{7,11},{8,12},{9,13},{1... | collective-permute-start | bytes 516104 | tf_op jit(solution)/shard_map/ppermute | solution.py:285
  75.9 8.0 %collective-permute-start.4 = (bf16[48,1792]{1,0:T(8,128)(2,1)S(1)}, bf16[48,1792]{1,0:T(8,128)(2,1)S(1)}, u32[]{:S(2)}, u32[]{:S(2)}) collective-permute-start(bf16[48,1792]{1,0:T(8,128)(2,1)S(1)} %get-tuple-element.45), channel_id=1, source_target_pairs={{0,4},{1,5},{2,6},{3,7},{4,8},{5,9},{6,10},{7,11},{8,12},{9,13},{1... | collective-permute-start | bytes 516104 | tf_op jit(solution)/shard_map/ppermute | solution.py:285
  75.9 9.2 %collective-permute-start.8 = (bf16[48,1792]{1,0:T(8,128)(2,1)S(1)}, bf16[48,1792]{1,0:T(8,128)(2,1)S(1)}, u32[]{:S(2)}, u32[]{:S(2)}) collective-permute-start(bf16[48,1792]{1,0:T(8,128)(2,1)S(1)} %get-tuple-element.47), channel_id=1, source_target_pairs={{0,12},{1,13},{2,14},{3,15},{4,0},{5,1},{6,2},{7,3},{8,4},{9,5},{1... | collective-permute-start | bytes 516104 | tf_op jit(solution)/shard_map/ppermute | solution.py:285
  79.2 5.8 %collective-permute-start.6 = (bf16[48,1792]{1,0:T(8,128)(2,1)S(1)}, bf16[48,1792]{1,0:T(8,128)(2,1)S(1)}, u32[]{:S(2)}, u32[]{:S(2)}) collective-permute-start(bf16[48,1792]{1,0:T(8,128)(2,1)S(1)} %add_convert_fusion.3), channel_id=1, source_target_pairs={{0,12},{1,13},{2,14},{3,15},{4,0},{5,1},{6,2},{7,3},{8,4},{9,5},{1... | collective-permute-start | bytes 516104 | tf_op jit(solution)/shard_map/ppermute | solution.py:285
  79.5 6.7 %collective-permute-start.10 = (bf16[48,1792]{1,0:T(8,128)(2,1)S(1)}, bf16[48,1792]{1,0:T(8,128)(2,1)S(1)}, u32[]{:S(2)}, u32[]{:S(2)}) collective-permute-start(bf16[48,1792]{1,0:T(8,128)(2,1)S(1)} %add_convert_fusion.2), channel_id=1, source_target_pairs={{0,4},{1,5},{2,6},{3,7},{4,8},{5,9},{6,10},{7,11},{8,12},{9,13},{1... | collective-permute-start | bytes 516104 | tf_op jit(solution)/shard_map/ppermute | solution.py:285
  81.5 6.9 %collective-permute-start.14 = (bf16[48,2304]{1,0:T(8,128)(2,1)S(1)}, bf16[48,2304]{1,0:T(8,128)(2,1)S(1)}, u32[]{:S(2)}, u32[]{:S(2)}) collective-permute-start(bf16[48,2304]{1,0:T(8,128)(2,1)S(1)} %slice.81), channel_id=1, source_target_pairs={{0,2},{1,3},{2,0},{3,1},{4,6},{5,7},{6,4},{7,5},{8,10},{9,11},{10,... | collective-permute-start | bytes 663560 | tf_op jit(solution)/shard_map/ppermute | solution.py:285
  83.9 6.9 %collective-permute-start.18 = (bf16[48,2304]{1,0:T(8,128)(2,1)S(1)}, bf16[48,2304]{1,0:T(8,128)(2,1)S(1)}, u32[]{:S(2)}, u32[]{:S(2)}) collective-permute-start(bf16[48,2304]{1,0:T(8,128)(2,1)S(1)} %slice.80), channel_id=1, source_target_pairs={{0,2},{1,3},{2,0},{3,1},{4,6},{5,7},{6,4},{7,5},{8,10},{9,11},{10,... | collective-permute-start | bytes 663560 | tf_op jit(solution)/shard_map/ppermute | solution.py:285
  86.2 4.6 %copy-start.1 = (bf16[48,8192]{1,0:T(8,128)(2,1)S(1)}, bf16[48,8192]{1,0:T(8,128)(2,1)}, u32[]{:S(2)}) copy-start(bf16[48,8192]{1,0:T(8,128)(2,1)} %param.18) | copy-start | bytes 2359300

commit v3 on v2

--- a/solution.py
+++ b/solution.py
@@ -292,11 +292,13 @@
     return total
 
 
-def reduce_y(first, second):
+def reduce_y(first, second, hold=None):
     far_second = send(second[2], dy=1)
     far_first = send(first[2], dy=-1)
     up_first = send(first[1], dy=1)
     down_second = send(second[3], dy=-1)
+    if hold is not None:
+        far_second, far_first, _ = lax.optimization_barrier((far_second, far_first, hold))
     up_second = send(add(second[1], far_second).astype(jnp.bfloat16), dy=1)
     down_first = send(add(first[3], far_first).astype(jnp.bfloat16), dy=-1)
     return add(first[0], up_first, down_first), add(second[0], down_second, up_second)
@@ -330,23 +332,25 @@
 
     a0_keep, a0_give = multiply(place, 0, X_FIRST, X_FIRST // 2, by_x)
     a0_got = send(a0_give, dx=1)
-    b0 = multiply(a0_keep, 2 * X_FIRST, y_first, y_first // 3, by_y)
-    b1 = multiply(b0[0], 2 * X_FIRST + y_first, y_first, y_first // 3, by_y)
+    b0 = multiply(a0_keep, 2 * X_FIRST, y_first, y_first // 2, by_y)
+    b1 = multiply(b0[0], 2 * X_FIRST + y_first, y_first, y_first // 2, by_y)
     a1_keep, a1_give = multiply(b1[0], X_FIRST, X_FIRST, X_FIRST // 2, by_x)
-    a1_got = send(a1_give, dx=1)
-
-    b0_sum, b1_sum = reduce_y(b0, b1)
-    b0_got = send(b0_sum[piece:].astype(jnp.bfloat16), dx=1)
-    b1_got = send(b1_sum[piece:].astype(jnp.bfloat16), dx=1)
+    a1_got = send(lax.optimization_barrier((a1_give, a0_got))[0], dx=1)
+    b0_sum, b1_sum = reduce_y(b0, b1, a0_got)
+    b0_give, b1_give = b0_sum[piece:].astype(jnp.bfloat16), b1_sum[piece:].astype(jnp.bfloat16)
+    b0_sum, b1_sum = b0_sum[:piece], b1_sum[:piece]
+    a0_got, a1_got, b0_give, b1_give = lax.optimization_barrier((a0_got, a1_got, b0_give, b1_give))
+
+    b0_got = send(b0_give, dx=1)
+    b1_give = lax.optimization_barrier((b1_give, b0_got))[0]
+    b1_got = send(b1_give, dx=1)
 
     def sections(keep_part, got):
         total = add(keep_part, got)
-        return [total[: piece]] + [total[s * piece : (s + 1) * piece].astype(jnp.bfloat16) for s in range(1, N_Y)]
-
-    a0_sum, a1_sum = reduce_y(sections(a0_keep, a0_got), sections(a1_keep, a1_got))
-    summed = jnp.concatenate(
-        [a0_sum, a1_sum, add(b0_sum[:piece], b0_got), add(b1_sum[:piece], b1_got)], axis=1
-    )
+        return [total[:piece]] + [total[s * piece : (s + 1) * piece].astype(jnp.bfloat16) for s in range(1, N_Y)]
+
+    a0_sum, a1_sum = reduce_y(sections(a0_keep, a0_got), sections(a1_keep, a1_got), b0_got)
+    summed = jnp.concatenate([a0_sum, a1_sum, add(b0_sum, b0_got), add(b1_sum, b1_got)], axis=1)
     return (residual.astype(jnp.float32) + summed).astype(jnp.bfloat16)
 
 

time: 92.1 us -> 87.8 us (0.953)
  waiting for transfers between devices: 42.3 us -> 33.4 us
  starting transfers between devices: 21.7 us -> 26.5 us
    ppermute x18, waiting for transfers between devices: 37.9 us -> 29 us  [send(): return lax.ppermute(array, 'tp', moved(**step))]
    ppermute x18, starting transfers between devices: 17.8 us -> 22.6 us  [send(): return lax.ppermute(array, 'tp', moved(**step))]
  transfers between devices with their start and end apart: 19 -> 19, of which waited for: 11 -> 11; matrix products, arithmetic and copies ran while one was open for 1% -> 1% of each run, Pallas kernels for 19% -> 24%
where the time goes in v3:
time: 87.8 us; the launch traced here: 87.3 us
  waiting for transfers between devices  33.4 us (38%)
  starting transfers between devices  26.5 us (30%)
  Pallas kernels  25 us (28%)
  other arithmetic  2.14 us (2%)
    ppermute x18, waiting for transfers between devices, send(): return lax.ppermute(array, 'tp', moved(**step))  29 us
    ppermute x18, starting transfers between devices, send(): return lax.ppermute(array, 'tp', moved(**step))  22.6 us
    pallas_call x4, Pallas kernels, project(): pl.pallas_call(functools.partial(project_kernel, first, count, tile, piec...  16.2 us
    ppermute x1, waiting for transfers between devices, body(): halo = lax.ppermute(rim, 'ctx', [(i, i + 1) for i in range(peers - 1)])  4.4 us
    pallas_call x1, Pallas kernels, gate_late(): pl.pallas_call(functools.partial(late_kernel, EARLY), grid=(channels // W...  3.95 us
    ppermute x1, starting transfers between devices, body(): halo = lax.ppermute(rim, 'ctx', [(i, i + 1) for i in range(peers - 1)])  3.83 us
    pallas_call x1, Pallas kernels, gate_early(): pl.pallas_call(early_kernel, grid_spec=pltpu.PrefetchScalarGridSpec(num_s...  3.58 us
  transfers between devices with their start and end apart: 19, of which 11 were waited for; matrix products, arithmetic and copies ran while one was open for 1% of the time, Pallas kernels for 24%

profile of v3, /device:TPU:4, one launch (start us, length us, event | category | flops | bytes accessed | tf_op | source)
XLA Modules:
  0.0 87.3 jit_solution(2885241671738468140)
XLA Ops:
  0.0 1.2 %rim.1 = bf16[144,512]{1,0:T(8,128)(2,1)S(1)} custom-call(bf16[768,512]{1,0:T(8,128)(2,1)} %q_ref.5, bf16[768,512]{1,0:T(8,128)(2,1)} %k_ref.5, bf16[768,512]{1,0:T(8,128)(2,1)} %v_ref.5, bf16[3,512]{1,0:T(4,128)(2,1)} %taps_ref.5), custom_call_target="tpu_custom_call" | custom-call | flops 1000000000 | bytes 1000000 | tf_op jit(solution)/shard_map/rim/pallas_call | solution.py:160
  1.3 3.8 %collective-permute-start = (bf16[144,512]{1,0:T(8,128)(2,1)S(1)}, bf16[144,512]{1,0:T(8,128)(2,1)S(1)}, u32[]{:S(2)}, u32[]{:S(2)}) collective-permute-start(bf16[144,512]{1,0:T(8,128)(2,1)S(1)} %rim.1), channel_id=1, source_target_pairs={{0,16},{16,32},{32,48},{48,64},{64,80},{80,96},{96,112},{112,128},... | collective-permute-start | bytes 442376 | tf_op jit(solution)/shard_map/ppermute | solution.py:317
  5.1 4.0 %gate_late.1.late_ref = bf16[512,512]{1,0:T(8,128)(2,1)S(1)} custom-call(bf16[768,512]{1,0:T(8,128)(2,1)} %q_ref.5, bf16[768,512]{1,0:T(8,128)(2,1)} %k_ref.5, bf16[768,512]{1,0:T(8,128)(2,1)} %v_ref.5, bf16[3,512]{1,0:T(4,128)(2,1)} %taps_ref.5, bf16[512,128]{1,0:T(8,128)(2,1)} %filt_ref.3, f32[1,512]{1,0:T(1,128)} %bitcast.2, ...), custom_call_target="tpu_custom_call" | custom-call | flops 4000000000 | bytes 3000000 | tf_op jit(solution)/shard_map/gate_late/pallas_call | solution.py:190
  9.1 4.4 %collective-permute-done.halo_ref = bf16[144,512]{1,0:T(8,128)(2,1)S(1)} collective-permute-done((bf16[144,512]{1,0:T(8,128)(2,1)S(1)}, bf16[144,512]{1,0:T(8,128)(2,1)S(1)}, u32[]{:S(2)}, u32[]{:S(2)}) %collective-permute-start) | collective-permute-done | bytes 147488 | tf_op jit(solution)/shard_map/ppermute | solution.py:317
  13.5 3.6 %gate_early.1 = (bf16[384,512]{1,0:T(8,128)(2,1)S(1)}, bf16[384,512]{1,0:T(8,128)(2,1)S(1)}) custom-call(s32[1]{0:T(128)} %bitcast.place_ref, s32[256]{0:T(256)S(1)} %copy-done, bf16[768,512]{1,0:T(8,128)(2,1)} %q_ref.5, bf16[768,512]{1,0:T(8,128)(2,1)} %k_ref.5, bf16[768,512]{1,0:T(8,128)(2,1)} %v_ref.5, ...), custom_call_target="tpu_custom_call" | custom-call | flops 2000000000 | bytes 3000000 | tf_op jit(solution)/shard_map/gate_early/pallas_call | solution.py:206
  17.2 1.7 %collective-permute-done.1.b_ref = bf16[384,512]{1,0:T(8,128)(2,1)S(1)} collective-permute-done((bf16[384,512]{1,0:T(8,128)(2,1)S(1)}, bf16[384,512]{1,0:T(8,128)(2,1)S(1)}, u32[]{:S(2)}, u32[]{:S(2)}) %collective-permute-start.1) | collective-permute-done | bytes 393248 | tf_op jit(solution)/shard_map/ppermute | solution.py:285
  18.9 3.7 %project.4 = (bf16[192,1792]{1,0:T(8,128)(2,1)S(1)}, bf16[192,1792]{1,0:T(8,128)(2,1)S(1)}) custom-call(bf16[384,512]{1,0:T(8,128)(2,1)S(1)} %get-tuple-element.42.a_ref, bf16[384,512]{1,0:T(8,128)(2,1)S(1)} %collective-permute-done.1.b_ref, bf16[512,8192]{1,0:T(8,128)(2,1)} %wa_ref.7, bf16[512,8192]{1,0:T(8,128)(2,1)} %collective-permute-done.2.wb_ref), custom_call_target="tpu_custom_call" | custom-call | flops 1409286144 | bytes 5046272 | tf_op jit(solution)/shard_map/project/pallas_call | solution.py:260
  22.6 2.2 %collective-permute-start.3 = (bf16[192,1792]{1,0:T(8,128)(2,1)S(1)}, bf16[192,1792]{1,0:T(8,128)(2,1)S(1)}, u32[]{:S(2)}, u32[]{:S(2)}) collective-permute-start(bf16[192,1792]{1,0:T(8,128)(2,1)S(1)} %get-tuple-element.37), channel_id=1, source_target_pairs={{0,2},{1,3},{2,0},{3,1},{4,6},{5,7},{6,4},{7,5},{8,10},{9,11},{10,... | collective-permute-start | bytes 2064392 | tf_op jit(solution)/shard_map/ppermute | solution.py:285
  24.8 4.4 %project.5 = (bf16[96,2304]{1,0:T(8,128)(2,1)S(1)}, bf16[96,2304]{1,0:T(8,128)(2,1)S(1)}, bf16[96,2304]{1,0:T(8,128)(2,1)S(1)}, bf16[96,2304]{1,0:T(8,128)(2,1)S(1)}) custom-call(bf16[384,512]{1,0:T(8,128)(2,1)S(1)} %get-tuple-element.42.a_ref, bf16[384,512]{1,0:T(8,128)(2,1)S(1)} %collective-permute-done.1.b_ref, bf16[512,8192]{1,0:T(8,128)(2,1)} %wa_ref.7, ...), custom_call_target="tpu_custom_call" | custom-call | flops 1811939328 | bytes 6488064 | tf_op jit(solution)/shard_map/project/pallas_call | solution.py:260
  29.2 4.4 %project.6 = (bf16[96,2304]{1,0:T(8,128)(2,1)S(1)}, bf16[96,2304]{1,0:T(8,128)(2,1)S(1)}, bf16[96,2304]{1,0:T(8,128)(2,1)S(1)}, bf16[96,2304]{1,0:T(8,128)(2,1)S(1)}) custom-call(bf16[384,512]{1,0:T(8,128)(2,1)S(1)} %get-tuple-element.42.a_ref, bf16[384,512]{1,0:T(8,128)(2,1)S(1)} %collective-permute-done.1.b_ref, bf16[512,8192]{1,0:T(8,128)(2,1)} %wa_ref.7, ...), custom_call_target="tpu_custom_call" | custom-call | flops 1811939328 | bytes 6488064 | tf_op jit(solution)/shard_map/project/pallas_call | solution.py:260
  33.6 1.6 %collective-permute-start.6 = (bf16[96,2304]{1,0:T(8,128)(2,1)S(1)}, bf16[96,2304]{1,0:T(8,128)(2,1)S(1)}, u32[]{:S(2)}, u32[]{:S(2)}) collective-permute-start(bf16[96,2304]{1,0:T(8,128)(2,1)S(1)} %get-tuple-element.47), channel_id=1, source_target_pairs={{0,4},{1,5},{2,6},{3,7},{4,8},{5,9},{6,10},{7,11},{8,12},{9,13},{1... | collective-permute-start | bytes 1327112 | tf_op jit(solution)/shard_map/ppermute | solution.py:285
  35.2 1.7 %collective-permute-start.7 = (bf16[96,2304]{1,0:T(8,128)(2,1)S(1)}, bf16[96,2304]{1,0:T(8,128)(2,1)S(1)}, u32[]{:S(2)}, u32[]{:S(2)}) collective-permute-start(bf16[96,2304]{1,0:T(8,128)(2,1)S(1)} %get-tuple-element.48), channel_id=1, source_target_pairs={{0,12},{1,13},{2,14},{3,15},{4,0},{5,1},{6,2},{7,3},{8,4},{9,5},{1... | collective-permute-start | bytes 1327112 | tf_op jit(solution)/shard_map/ppermute | solution.py:285
  36.9 0.4 collective-permute-start.5
  37.2 2.9 %collective-permute-start.9 = (bf16[96,2304]{1,0:T(8,128)(2,1)S(1)}, bf16[96,2304]{1,0:T(8,128)(2,1)S(1)}, u32[]{:S(2)}, u32[]{:S(2)}) collective-permute-start(bf16[96,2304]{1,0:T(8,128)(2,1)S(1)} %get-tuple-element.50), channel_id=1, source_target_pairs={{0,12},{1,13},{2,14},{3,15},{4,0},{5,1},{6,2},{7,3},{8,4},{9,5},{1... | collective-permute-start | bytes 1327112 | tf_op jit(solution)/shard_map/ppermute | solution.py:285
  40.1 3.7 %project.7 = (bf16[192,1792]{1,0:T(8,128)(2,1)S(1)}, bf16[192,1792]{1,0:T(8,128)(2,1)S(1)}) custom-call(bf16[384,512]{1,0:T(8,128)(2,1)S(1)} %get-tuple-element.42.a_ref, bf16[384,512]{1,0:T(8,128)(2,1)S(1)} %collective-permute-done.1.b_ref, bf16[512,8192]{1,0:T(8,128)(2,1)} %wa_ref.7, bf16[512,8192]{1,0:T(8,128)(2,1)} %collective-permute-done.2.wb_ref), custom_call_target="tpu_custom_call" | custom-call | flops 1409286144 | bytes 5046272 | tf_op jit(solution)/shard_map/project/pallas_call | solution.py:260
  43.8 4.1 %collective-permute-done.6 = bf16[96,2304]{1,0:T(8,128)(2,1)S(1)} collective-permute-done((bf16[96,2304]{1,0:T(8,128)(2,1)S(1)}, bf16[96,2304]{1,0:T(8,128)(2,1)S(1)}, u32[]{:S(2)}, u32[]{:S(2)}) %collective-permute-start.6) | collective-permute-done | bytes 442400 | tf_op jit(solution)/shard_map/ppermute | solution.py:285
  47.9 0.4 collective-permute-done.7
  48.4 2.9 %collective-permute-start.8 = (bf16[96,2304]{1,0:T(8,128)(2,1)S(1)}, bf16[96,2304]{1,0:T(8,128)(2,1)S(1)}, u32[]{:S(2)}, u32[]{:S(2)}) collective-permute-start(bf16[96,2304]{1,0:T(8,128)(2,1)S(1)} %add_convert_fusion.1), channel_id=1, source_target_pairs={{0,12},{1,13},{2,14},{3,15},{4,0},{5,1},{6,2},{7,3},{8,4},{9,5},{1... | collective-permute-start | bytes 1327112 | tf_op jit(solution)/shard_map/ppermute | solution.py:285
  51.4 0.3 collective-permute-start.10
  51.8 5.5 %collective-permute-done.5 = bf16[96,2304]{1,0:T(8,128)(2,1)S(1)} collective-permute-done((bf16[96,2304]{1,0:T(8,128)(2,1)S(1)}, bf16[96,2304]{1,0:T(8,128)(2,1)S(1)}, u32[]{:S(2)}, u32[]{:S(2)}) %collective-permute-start.5) | collective-permute-done | bytes 442400 | tf_op jit(solution)/shard_map/ppermute | solution.py:285
  57.4 8.4 %collective-permute-done.8 = bf16[96,2304]{1,0:T(8,128)(2,1)S(1)} collective-permute-done((bf16[96,2304]{1,0:T(8,128)(2,1)S(1)}, bf16[96,2304]{1,0:T(8,128)(2,1)S(1)}, u32[]{:S(2)}, u32[]{:S(2)}) %collective-permute-start.8) | collective-permute-done | bytes 442400 | tf_op jit(solution)/shard_map/ppermute | solution.py:285
  66.6 2.9 %collective-permute-start.13 = (bf16[48,1792]{1,0:T(8,128)(2,1)S(1)}, bf16[48,1792]{1,0:T(8,128)(2,1)S(1)}, u32[]{:S(2)}, u32[]{:S(2)}) collective-permute-start(bf16[48,1792]{1,0:T(8,128)(2,1)S(1)} %get-tuple-element.66), channel_id=1, source_target_pairs={{0,12},{1,13},{2,14},{3,15},{4,0},{5,1},{6,2},{7,3},{8,4},{9,5},{1... | collective-permute-start | bytes 516104 | tf_op jit(solution)/shard_map/ppermute | solution.py:285
  69.5 0.6 collective-permute-start.14
  70.5 0.2 collective-permute-start.11
  70.7 3.1 %collective-permute-start.16 = (bf16[48,1792]{1,0:T(8,128)(2,1)S(1)}, bf16[48,1792]{1,0:T(8,128)(2,1)S(1)}, u32[]{:S(2)}, u32[]{:S(2)}) collective-permute-start(bf16[48,1792]{1,0:T(8,128)(2,1)S(1)} %get-tuple-element.67), channel_id=1, source_target_pairs={{0,12},{1,13},{2,14},{3,15},{4,0},{5,1},{6,2},{7,3},{8,4},{9,5},{1... | collective-permute-start | bytes 516104 | tf_op jit(solution)/shard_map/ppermute | solution.py:285
  73.8 4.2 %collective-permute-done.12 = bf16[48,1792]{1,0:T(8,128)(2,1)S(1)} collective-permute-done((bf16[48,1792]{1,0:T(8,128)(2,1)S(1)}, bf16[48,1792]{1,0:T(8,128)(2,1)S(1)}, u32[]{:S(2)}, u32[]{:S(2)}) %collective-permute-start.12) | collective-permute-done | bytes 172064 | tf_op jit(solution)/shard_map/ppermute | solution.py:285
  78.2 2.1 %collective-permute-start.17 = (bf16[48,1792]{1,0:T(8,128)(2,1)S(1)}, bf16[48,1792]{1,0:T(8,128)(2,1)S(1)}, u32[]{:S(2)}, u32[]{:S(2)}) collective-permute-start(bf16[48,1792]{1,0:T(8,128)(2,1)S(1)} %add_convert_fusion.2), channel_id=1, source_target_pairs={{0,4},{1,5},{2,6},{3,7},{4,8},{5,9},{6,10},{7,11},{8,12},{9,13},{1... | collective-permute-start | bytes 516104 | tf_op jit(solution)/shard_map/ppermute | solution.py:285
  80.3 1.4 %collective-permute-start.18 = (bf16[48,2304]{1,0:T(8,128)(2,1)S(1)}, bf16[48,2304]{1,0:T(8,128)(2,1)S(1)}, u32[]{:S(2)}, u32[]{:S(2)}) collective-permute-start(bf16[48,2304]{1,0:T(8,128)(2,1)S(1)} %slice.80), channel_id=1, source_target_pairs={{0,2},{1,3},{2,0},{3,1},{4,6},{5,7},{6,4},{7,5},{8,10},{9,11},{10,... | collective-permute-start | bytes 663560 | tf_op jit(solution)/shard_map/ppermute | solution.py:285
  81.8 1.8 %collective-permute-done.15 = bf16[48,1792]{1,0:T(8,128)(2,1)S(1)} collective-permute-done((bf16[48,1792]{1,0:T(8,128)(2,1)S(1)}, bf16[48,1792]{1,0:T(8,128)(2,1)S(1)}, u32[]{:S(2)}, u32[]{:S(2)}) %collective-permute-start.15) | collective-permute-done | bytes 172064 | tf_op jit(solution)/shard_map/ppermute | solution.py:285
  83.6 1.3 %collective-permute-done.17 = bf16[48,1792]{1,0:T(8,128)(2,1)S(1)} collective-permute-done((bf16[48,1792]{1,0:T(8,128)(2,1)S(1)}, bf16[48,1792]{1,0:T(8,128)(2,1)S(1)}, u32[]{:S(2)}, u32[]{:S(2)}) %collective-permute-start.17) | collective-permute-done | bytes 172064 | tf_op jit(solution)/shard_map/ppermute | solution.py:285
  85.0 1.3 %collective-permute-done.18 = bf16[48,2304]{1,0:T(8,128)(2,1)S(1)} collective-permute-done((bf16[48,2304]{1,0:T(8,128)(2,1)S(1)}, bf16[48,2304]{1,0:T(8,128)(2,1)S(1)}, u32[]{:S(2)}, u32[]{:S(2)}) %collective-permute-start.18) | collective-permute-done | bytes 221216 | tf_op jit(solution)/shard_map/ppermute | solution.py:285
  86.3 1.0 %fusion = bf16[48,8192]{1,0:T(8,128)(2,1)} fusion(f32[48,2304]{1,0:T(8,128)S(1)} %slice_add_fusion, f32[48,2304]{1,0:T(8,128)S(1)} %slice_add_fusion.1, f32[48,1792]{1,0:T(8,128)S(1)} %fusion.1, f32[48,1792]{1,0:T(8,128)S(1)} %fusion.2, bf16[48,8192]{1,0:T(8,128)(2,1)S(1)} %copy-done.1), kind=kLoop, calls=%fused_computation.1 | loop fusion | flops 2359296 | bytes 3145728 | tf_op jit(solution)/shard_map/convert_element_type | solution.py:354
  (34 shorter events, 1.8 us)
Async XLA Ops:
  0.0 18.9 %collective-permute-start.2 = (bf16[512,8192]{1,0:T(8,128)(2,1)}, bf16[512,8192]{1,0:T(8,128)(2,1)}, u32[]{:S(2)}, u32[]{:S(2)}) collective-permute-start(bf16[512,8192]{1,0:T(8,128)(2,1)} %wa_ref.7), channel_id=1, source_target_pairs={{0,1},{1,0},{2,3},{3,2},{4,5},{5,4},{6,7},{7,6},{8,9},{9,8},{10,11... | collective-permute-start | bytes 25165832 | tf_op jit(solution)/shard_map/ppermute | solution.py:285
  1.3 12.2 %collective-permute-start = (bf16[144,512]{1,0:T(8,128)(2,1)S(1)}, bf16[144,512]{1,0:T(8,128)(2,1)S(1)}, u32[]{:S(2)}, u32[]{:S(2)}) collective-permute-start(bf16[144,512]{1,0:T(8,128)(2,1)S(1)} %rim.1), channel_id=1, source_target_pairs={{0,16},{16,32},{32,48},{48,64},{64,80},{80,96},{96,112},{112,128},... | collective-permute-start | bytes 442376 | tf_op jit(solution)/shard_map/ppermute | solution.py:317
  5.1 8.4 %copy-start = (s32[256]{0:T(256)S(1)}, s32[256]{0:T(256)}, u32[]{:S(2)}) copy-start(s32[256]{0:T(256)} %constant.12.clone.order_ref) | copy-start | bytes 3076
  17.1 1.8 %collective-permute-start.1 = (bf16[384,512]{1,0:T(8,128)(2,1)S(1)}, bf16[384,512]{1,0:T(8,128)(2,1)S(1)}, u32[]{:S(2)}, u32[]{:S(2)}) collective-permute-start(bf16[384,512]{1,0:T(8,128)(2,1)S(1)} %get-tuple-element.35), channel_id=1, source_target_pairs={{0,1},{1,0},{2,3},{3,2},{4,5},{5,4},{6,7},{7,6},{8,9},{9,8},{10,11... | collective-permute-start | bytes 1179656 | tf_op jit(solution)/shard_map/ppermute | solution.py:285
  22.6 25.7 %collective-permute-start.3 = (bf16[192,1792]{1,0:T(8,128)(2,1)S(1)}, bf16[192,1792]{1,0:T(8,128)(2,1)S(1)}, u32[]{:S(2)}, u32[]{:S(2)}) collective-permute-start(bf16[192,1792]{1,0:T(8,128)(2,1)S(1)} %get-tuple-element.37), channel_id=1, source_target_pairs={{0,2},{1,3},{2,0},{3,1},{4,6},{5,7},{6,4},{7,5},{8,10},{9,11},{10,... | collective-permute-start | bytes 2064392 | tf_op jit(solution)/shard_map/ppermute | solution.py:285
  33.6 14.3 %collective-permute-start.6 = (bf16[96,2304]{1,0:T(8,128)(2,1)S(1)}, bf16[96,2304]{1,0:T(8,128)(2,1)S(1)}, u32[]{:S(2)}, u32[]{:S(2)}) collective-permute-start(bf16[96,2304]{1,0:T(8,128)(2,1)S(1)} %get-tuple-element.47), channel_id=1, source_target_pairs={{0,4},{1,5},{2,6},{3,7},{4,8},{5,9},{6,10},{7,11},{8,12},{9,13},{1... | collective-permute-start | bytes 1327112 | tf_op jit(solution)/shard_map/ppermute | solution.py:285
  35.2 13.1 %collective-permute-start.7 = (bf16[96,2304]{1,0:T(8,128)(2,1)S(1)}, bf16[96,2304]{1,0:T(8,128)(2,1)S(1)}, u32[]{:S(2)}, u32[]{:S(2)}) collective-permute-start(bf16[96,2304]{1,0:T(8,128)(2,1)S(1)} %get-tuple-element.48), channel_id=1, source_target_pairs={{0,12},{1,13},{2,14},{3,15},{4,0},{5,1},{6,2},{7,3},{8,4},{9,5},{1... | collective-permute-start | bytes 1327112 | tf_op jit(solution)/shard_map/ppermute | solution.py:285
  36.9 20.5 %collective-permute-start.5 = (bf16[96,2304]{1,0:T(8,128)(2,1)S(1)}, bf16[96,2304]{1,0:T(8,128)(2,1)S(1)}, u32[]{:S(2)}, u32[]{:S(2)}) collective-permute-start(bf16[96,2304]{1,0:T(8,128)(2,1)S(1)} %get-tuple-element.45), channel_id=1, source_target_pairs={{0,4},{1,5},{2,6},{3,7},{4,8},{5,9},{6,10},{7,11},{8,12},{9,13},{1... | collective-permute-start | bytes 1327112 | tf_op jit(solution)/shard_map/ppermute | solution.py:285
  37.2 28.8 %collective-permute-start.9 = (bf16[96,2304]{1,0:T(8,128)(2,1)S(1)}, bf16[96,2304]{1,0:T(8,128)(2,1)S(1)}, u32[]{:S(2)}, u32[]{:S(2)}) collective-permute-start(bf16[96,2304]{1,0:T(8,128)(2,1)S(1)} %get-tuple-element.50), channel_id=1, source_target_pairs={{0,12},{1,13},{2,14},{3,15},{4,0},{5,1},{6,2},{7,3},{8,4},{9,5},{1... | collective-permute-start | bytes 1327112 | tf_op jit(solution)/shard_map/ppermute | solution.py:285
  48.4 17.4 %collective-permute-start.8 = (bf16[96,2304]{1,0:T(8,128)(2,1)S(1)}, bf16[96,2304]{1,0:T(8,128)(2,1)S(1)}, u32[]{:S(2)}, u32[]{:S(2)}) collective-permute-start(bf16[96,2304]{1,0:T(8,128)(2,1)S(1)} %add_convert_fusion.1), channel_id=1, source_target_pairs={{0,12},{1,13},{2,14},{3,15},{4,0},{5,1},{6,2},{7,3},{8,4},{9,5},{1... | collective-permute-start | bytes 1327112 | tf_op jit(solution)/shard_map/ppermute | solution.py:285
  51.4 14.6 %collective-permute-start.10 = (bf16[96,2304]{1,0:T(8,128)(2,1)S(1)}, bf16[96,2304]{1,0:T(8,128)(2,1)S(1)}, u32[]{:S(2)}, u32[]{:S(2)}) collective-permute-start(bf16[96,2304]{1,0:T(8,128)(2,1)S(1)} %add_convert_fusion), channel_id=1, source_target_pairs={{0,4},{1,5},{2,6},{3,7},{4,8},{5,9},{6,10},{7,11},{8,12},{9,13},{1... | collective-permute-start | bytes 1327112 | tf_op jit(solution)/shard_map/ppermute | solution.py:285
  51.7 14.7 %collective-permute-start.4 = (bf16[192,1792]{1,0:T(8,128)(2,1)S(1)}, bf16[192,1792]{1,0:T(8,128)(2,1)S(1)}, u32[]{:S(2)}, u32[]{:S(2)}) collective-permute-start(bf16[192,1792]{1,0:T(8,128)(2,1)S(1)} %get-tuple-element.44), channel_id=1, source_target_pairs={{0,2},{1,3},{2,0},{3,1},{4,6},{5,7},{6,4},{7,5},{8,10},{9,11},{10,... | collective-permute-start | bytes 2064392 | tf_op jit(solution)/shard_map/ppermute | solution.py:285
  66.6 7.2 %collective-permute-start.13 = (bf16[48,1792]{1,0:T(8,128)(2,1)S(1)}, bf16[48,1792]{1,0:T(8,128)(2,1)S(1)}, u32[]{:S(2)}, u32[]{:S(2)}) collective-permute-start(bf16[48,1792]{1,0:T(8,128)(2,1)S(1)} %get-tuple-element.66), channel_id=1, source_target_pairs={{0,12},{1,13},{2,14},{3,15},{4,0},{5,1},{6,2},{7,3},{8,4},{9,5},{1... | collective-permute-start | bytes 516104 | tf_op jit(solution)/shard_map/ppermute | solution.py:285
  69.5 8.5 %collective-permute-start.14 = (bf16[48,2304]{1,0:T(8,128)(2,1)S(1)}, bf16[48,2304]{1,0:T(8,128)(2,1)S(1)}, u32[]{:S(2)}, u32[]{:S(2)}) collective-permute-start(bf16[48,2304]{1,0:T(8,128)(2,1)S(1)} %slice.81), channel_id=1, source_target_pairs={{0,2},{1,3},{2,0},{3,1},{4,6},{5,7},{6,4},{7,5},{8,10},{9,11},{10,... | collective-permute-start | bytes 663560 | tf_op jit(solution)/shard_map/ppermute | solution.py:285
  70.4 7.6 %collective-permute-start.12 = (bf16[48,1792]{1,0:T(8,128)(2,1)S(1)}, bf16[48,1792]{1,0:T(8,128)(2,1)S(1)}, u32[]{:S(2)}, u32[]{:S(2)}) collective-permute-start(bf16[48,1792]{1,0:T(8,128)(2,1)S(1)} %get-tuple-element.68), channel_id=1, source_target_pairs={{0,4},{1,5},{2,6},{3,7},{4,8},{5,9},{6,10},{7,11},{8,12},{9,13},{1... | collective-permute-start | bytes 516104 | tf_op jit(solution)/shard_map/ppermute | solution.py:285
  70.5 11.3 %collective-permute-start.11 = (bf16[48,1792]{1,0:T(8,128)(2,1)S(1)}, bf16[48,1792]{1,0:T(8,128)(2,1)S(1)}, u32[]{:S(2)}, u32[]{:S(2)}) collective-permute-start(bf16[48,1792]{1,0:T(8,128)(2,1)S(1)} %get-tuple-element.65), channel_id=1, source_target_pairs={{0,4},{1,5},{2,6},{3,7},{4,8},{5,9},{6,10},{7,11},{8,12},{9,13},{1... | collective-permute-start | bytes 516104 | tf_op jit(solution)/shard_map/ppermute | solution.py:285
  70.7 12.9 %collective-permute-start.16 = (bf16[48,1792]{1,0:T(8,128)(2,1)S(1)}, bf16[48,1792]{1,0:T(8,128)(2,1)S(1)}, u32[]{:S(2)}, u32[]{:S(2)}) collective-permute-start(bf16[48,1792]{1,0:T(8,128)(2,1)S(1)} %get-tuple-element.67), channel_id=1, source_target_pairs={{0,12},{1,13},{2,14},{3,15},{4,0},{5,1},{6,2},{7,3},{8,4},{9,5},{1... | collective-permute-start | bytes 516104 | tf_op jit(solution)/shard_map/ppermute | solution.py:285
  78.1 5.5 %collective-permute-start.15 = (bf16[48,1792]{1,0:T(8,128)(2,1)S(1)}, bf16[48,1792]{1,0:T(8,128)(2,1)S(1)}, u32[]{:S(2)}, u32[]{:S(2)}) collective-permute-start(bf16[48,1792]{1,0:T(8,128)(2,1)S(1)} %add_convert_fusion.3), channel_id=1, source_target_pairs={{0,12},{1,13},{2,14},{3,15},{4,0},{5,1},{6,2},{7,3},{8,4},{9,5},{1... | collective-permute-start | bytes 516104 | tf_op jit(solution)/shard_map/ppermute | solution.py:285
  78.2 6.7 %collective-permute-start.17 = (bf16[48,1792]{1,0:T(8,128)(2,1)S(1)}, bf16[48,1792]{1,0:T(8,128)(2,1)S(1)}, u32[]{:S(2)}, u32[]{:S(2)}) collective-permute-start(bf16[48,1792]{1,0:T(8,128)(2,1)S(1)} %add_convert_fusion.2), channel_id=1, source_target_pairs={{0,4},{1,5},{2,6},{3,7},{4,8},{5,9},{6,10},{7,11},{8,12},{9,13},{1... | collective-permute-start | bytes 516104 | tf_op jit(solution)/shard_map/ppermute | solution.py:285
  80.3 5.9 %collective-permute-start.18 = (bf16[48,2304]{1,0:T(8,128)(2,1)S(1)}, bf16[48,2304]{1,0:T(8,128)(2,1)S(1)}, u32[]{:S(2)}, u32[]{:S(2)}) collective-permute-start(bf16[48,2304]{1,0:T(8,128)(2,1)S(1)} %slice.80), channel_id=1, source_target_pairs={{0,2},{1,3},{2,0},{3,1},{4,6},{5,7},{6,4},{7,5},{8,10},{9,11},{10,... | collective-permute-start | bytes 663560 | tf_op jit(solution)/shard_map/ppermute | solution.py:285
  83.6 2.7 %copy-start.1 = (bf16[48,8192]{1,0:T(8,128)(2,1)S(1)}, bf16[48,8192]{1,0:T(8,128)(2,1)}, u32[]{:S(2)}) copy-start(bf16[48,8192]{1,0:T(8,128)(2,1)} %param.18) | copy-start | bytes 2359300

commit v4 on v2

--- a/solution.py
+++ b/solution.py
@@ -292,17 +292,7 @@
     return total
 
 
-def reduce_y(first, second):
-    far_second = send(second[2], dy=1)
-    far_first = send(first[2], dy=-1)
-    up_first = send(first[1], dy=1)
-    down_second = send(second[3], dy=-1)
-    up_second = send(add(second[1], far_second).astype(jnp.bfloat16), dy=1)
-    down_first = send(add(first[3], far_first).astype(jnp.bfloat16), dy=-1)
-    return add(first[0], up_first, down_first), add(second[0], down_second, up_second)
-
-
-X_FIRST = 1792
+X_FIRST = (2560, 1536)
 
 
 def body(queries, keys_in, values_in, short_taps, filters, skip_gain, out_weight, residual):
@@ -322,32 +312,65 @@
     half = rows // (2 * N_C)
     by_x = (((0, half),), ((half, 2 * half),))
     by_y = tuple(((s * piece, (s + 1) * piece), (half + s * piece, half + (s + 1) * piece)) for s in range(N_Y))
-    y_first = width // 2 - X_FIRST
-
-    def multiply(after, *where):
+    y_first = (width - sum(X_FIRST)) // 2
+
+    def multiply(after, first, count, pieces):
         left = lax.optimization_barrier((keep, after))[0]
-        return project(left, theirs, out_weight, weight_pair, *where)
-
-    a0_keep, a0_give = multiply(place, 0, X_FIRST, X_FIRST // 2, by_x)
+        return project(left, theirs, out_weight, weight_pair, first, count, count // 2, pieces)
+
+    def narrow(array):
+        return array.astype(jnp.bfloat16)
+
+    a0_keep, a0_give = multiply(place, 0, X_FIRST[0], by_x)
     a0_got = send(a0_give, dx=1)
-    b0 = multiply(a0_keep, 2 * X_FIRST, y_first, y_first // 3, by_y)
-    b1 = multiply(b0[0], 2 * X_FIRST + y_first, y_first, y_first // 3, by_y)
-    a1_keep, a1_give = multiply(b1[0], X_FIRST, X_FIRST, X_FIRST // 2, by_x)
-    a1_got = send(a1_give, dx=1)
-
-    b0_sum, b1_sum = reduce_y(b0, b1)
-    b0_got = send(b0_sum[piece:].astype(jnp.bfloat16), dx=1)
-    b1_got = send(b1_sum[piece:].astype(jnp.bfloat16), dx=1)
-
-    def sections(keep_part, got):
-        total = add(keep_part, got)
-        return [total[: piece]] + [total[s * piece : (s + 1) * piece].astype(jnp.bfloat16) for s in range(1, N_Y)]
-
-    a0_sum, a1_sum = reduce_y(sections(a0_keep, a0_got), sections(a1_keep, a1_got))
+    b0 = multiply(a0_keep, sum(X_FIRST), y_first, by_y)
+    b1 = multiply(b0[0], sum(X_FIRST) + y_first, y_first, by_y)
+    a1_keep, a1_give = multiply(b1[0], X_FIRST[0], X_FIRST[1], by_x)
+
+    b1_far = send(b1[2], dy=1)
+    b0_far = send(b0[2], dy=-1)
+    b0_up = send(b0[1], dy=1)
+    b1_down = send(b1[3], dy=-1)
+    a1_got = send(lax.optimization_barrier((a1_give, a0_got))[0], dx=1)
+
+    b0_far, b1_far, a0_got = lax.optimization_barrier((b0_far, b1_far, a0_got))
+    b1_up = send(narrow(add(b1[1], b1_far)), dy=1)
+    b0_down = send(narrow(add(b0[3], b0_far)), dy=-1)
+
+    a0, a1 = add(a0_keep, a0_got), add(a1_keep, a1_got)
+    edge = sum(X_FIRST) // 2
+    low = [a0[s * piece : (s + 1) * piece, :edge] for s in range(N_Y)]
+    high = [
+        jnp.concatenate([a0[s * piece : (s + 1) * piece, edge:], a1[s * piece : (s + 1) * piece]], axis=1)
+        for s in range(N_Y)
+    ]
+    low_send, high_send = [narrow(part) for part in low], [narrow(part) for part in high]
+    low_send, high_send = lax.optimization_barrier((low_send, high_send))
+    low_far = send(low_send[2], dy=-1)
+    high_far = send(high_send[2], dy=1)
+
+    b0_sum, b1_sum = add(b0[0], b0_up, b0_down), add(b1[0], b1_up, b1_down)
+    b0_give, b1_give = narrow(b0_sum[piece:]), narrow(b1_sum[piece:])
+    b0_give, b1_give, low_send[1], high_send[3] = lax.optimization_barrier((b0_give, b1_give, low_send[1], high_send[3]))
+    b0_got = send(b0_give, dx=1)
+    low_up = send(low_send[1], dy=1)
+    high_down = send(high_send[3], dy=-1)
+
+    b0_got, b1_give = lax.optimization_barrier((b0_got, b1_give))
+    low_down = send(narrow(add(low[3], low_far)), dy=-1)
+    high_up = send(narrow(add(high[1], high_far)), dy=1)
+    b1_got = send(b1_give, dx=1)
+
     summed = jnp.concatenate(
-        [a0_sum, a1_sum, add(b0_sum[:piece], b0_got), add(b1_sum[:piece], b1_got)], axis=1
+        [
+            add(low[0], low_up, low_down),
+            add(high[0], high_down, high_up),
+            add(b0_sum[:piece], b0_got),
+            add(b1_sum[:piece], b1_got),
+        ],
+        axis=1,
     )
-    return (residual.astype(jnp.float32) + summed).astype(jnp.bfloat16)
+    return narrow(residual.astype(jnp.float32) + summed)
 
 
 def solution(mesh):

time: 92.1 us -> 89.2 us (0.969)
  waiting for transfers between devices: 42.3 us -> 35.1 us
  starting transfers between devices: 21.7 us -> 27 us
  Pallas kernels: 25.4 us -> 24.1 us
    ppermute x18, waiting for transfers between devices: 37.9 us -> 30.7 us  [send(): return lax.ppermute(array, 'tp', moved(**step))]
    ppermute x18, starting transfers between devices: 17.8 us -> 23.2 us  [send(): return lax.ppermute(array, 'tp', moved(**step))]
    pallas_call x4, Pallas kernels: 16.6 us -> 15.4 us  [project(): pl.pallas_call(functools.partial(project_kernel, first, count, tile, piec...]
  transfers between devices with their start and end apart: 19 -> 19, of which waited for: 11 -> 11; matrix products, arithmetic and copies ran while one was open for 1% -> 1% of each run, Pallas kernels for 19% -> 22%
where the time goes in v4:
time: 89.2 us; the launch traced here: 89 us
  waiting for transfers between devices  35.1 us (39%)
  starting transfers between devices  27 us (30%)
  Pallas kernels  24.1 us (27%)
  other arithmetic  2.29 us (3%)
    ppermute x18, waiting for transfers between devices, send(): return lax.ppermute(array, 'tp', moved(**step))  30.7 us
    ppermute x18, starting transfers between devices, send(): return lax.ppermute(array, 'tp', moved(**step))  23.2 us
    pallas_call x4, Pallas kernels, project(): pl.pallas_call(functools.partial(project_kernel, first, count, tile, piec...  15.4 us
    ppermute x1, waiting for transfers between devices, body(): halo = lax.ppermute(rim, 'ctx', [(i, i + 1) for i in range(peers - 1)])  4.4 us
    pallas_call x1, Pallas kernels, gate_late(): pl.pallas_call(functools.partial(late_kernel, EARLY), grid=(channels // W...  3.95 us
    ppermute x1, starting transfers between devices, body(): halo = lax.ppermute(rim, 'ctx', [(i, i + 1) for i in range(peers - 1)])  3.83 us
    pallas_call x1, Pallas kernels, gate_early(): pl.pallas_call(early_kernel, grid_spec=pltpu.PrefetchScalarGridSpec(num_s...  3.58 us
  transfers between devices with their start and end apart: 19, of which 11 were waited for; matrix products, arithmetic and copies ran while one was open for 1% of the time, Pallas kernels for 22%

profile of v4, /device:TPU:4, one launch (start us, length us, event | category | flops | bytes accessed | tf_op | source)
XLA Modules:
  0.0 89.0 jit_solution(13287737083059386415)
XLA Ops:
  0.0 1.2 %rim.1 = bf16[144,512]{1,0:T(8,128)(2,1)S(1)} custom-call(bf16[768,512]{1,0:T(8,128)(2,1)} %q_ref.5, bf16[768,512]{1,0:T(8,128)(2,1)} %k_ref.5, bf16[768,512]{1,0:T(8,128)(2,1)} %v_ref.5, bf16[3,512]{1,0:T(4,128)(2,1)} %taps_ref.5), custom_call_target="tpu_custom_call" | custom-call | flops 1000000000 | bytes 1000000 | tf_op jit(solution)/shard_map/rim/pallas_call | solution.py:160
  1.3 3.8 %collective-permute-start = (bf16[144,512]{1,0:T(8,128)(2,1)S(1)}, bf16[144,512]{1,0:T(8,128)(2,1)S(1)}, u32[]{:S(2)}, u32[]{:S(2)}) collective-permute-start(bf16[144,512]{1,0:T(8,128)(2,1)S(1)} %rim.1), channel_id=1, source_target_pairs={{0,16},{16,32},{32,48},{48,64},{64,80},{80,96},{96,112},{112,128},... | collective-permute-start | bytes 442376 | tf_op jit(solution)/shard_map/ppermute | solution.py:305
  5.1 4.0 %gate_late.1.late_ref = bf16[512,512]{1,0:T(8,128)(2,1)S(1)} custom-call(bf16[768,512]{1,0:T(8,128)(2,1)} %q_ref.5, bf16[768,512]{1,0:T(8,128)(2,1)} %k_ref.5, bf16[768,512]{1,0:T(8,128)(2,1)} %v_ref.5, bf16[3,512]{1,0:T(4,128)(2,1)} %taps_ref.5, bf16[512,128]{1,0:T(8,128)(2,1)} %filt_ref.3, f32[1,512]{1,0:T(1,128)} %bitcast.2, ...), custom_call_target="tpu_custom_call" | custom-call | flops 4000000000 | bytes 3000000 | tf_op jit(solution)/shard_map/gate_late/pallas_call | solution.py:190
  9.1 4.4 %collective-permute-done.halo_ref = bf16[144,512]{1,0:T(8,128)(2,1)S(1)} collective-permute-done((bf16[144,512]{1,0:T(8,128)(2,1)S(1)}, bf16[144,512]{1,0:T(8,128)(2,1)S(1)}, u32[]{:S(2)}, u32[]{:S(2)}) %collective-permute-start) | collective-permute-done | bytes 147488 | tf_op jit(solution)/shard_map/ppermute | solution.py:305
  13.5 3.6 %gate_early.1 = (bf16[384,512]{1,0:T(8,128)(2,1)S(1)}, bf16[384,512]{1,0:T(8,128)(2,1)S(1)}) custom-call(s32[1]{0:T(128)} %bitcast.place_ref, s32[256]{0:T(256)S(1)} %copy-done, bf16[768,512]{1,0:T(8,128)(2,1)} %q_ref.5, bf16[768,512]{1,0:T(8,128)(2,1)} %k_ref.5, bf16[768,512]{1,0:T(8,128)(2,1)} %v_ref.5, ...), custom_call_target="tpu_custom_call" | custom-call | flops 2000000000 | bytes 3000000 | tf_op jit(solution)/shard_map/gate_early/pallas_call | solution.py:206
  17.2 1.7 %collective-permute-done.1.b_ref = bf16[384,512]{1,0:T(8,128)(2,1)S(1)} collective-permute-done((bf16[384,512]{1,0:T(8,128)(2,1)S(1)}, bf16[384,512]{1,0:T(8,128)(2,1)S(1)}, u32[]{:S(2)}, u32[]{:S(2)}) %collective-permute-start.1) | collective-permute-done | bytes 393248 | tf_op jit(solution)/shard_map/ppermute | solution.py:285
  18.9 4.5 %project.4 = (bf16[192,2560]{1,0:T(8,128)(2,1)S(1)}, bf16[192,2560]{1,0:T(8,128)(2,1)S(1)}) custom-call(bf16[384,512]{1,0:T(8,128)(2,1)S(1)} %get-tuple-element.55.a_ref, bf16[384,512]{1,0:T(8,128)(2,1)S(1)} %collective-permute-done.1.b_ref, bf16[512,8192]{1,0:T(8,128)(2,1)} %wa_ref.7, bf16[512,8192]{1,0:T(8,128)(2,1)} %collective-permute-done.2.wb_ref), custom_call_target="tpu_custom_call" | custom-call | flops 2013265920 | bytes 7208960 | tf_op jit(solution)/shard_map/project/pallas_call | solution.py:260
  23.4 2.2 %collective-permute-start.5 = (bf16[192,2560]{1,0:T(8,128)(2,1)S(1)}, bf16[192,2560]{1,0:T(8,128)(2,1)S(1)}, u32[]{:S(2)}, u32[]{:S(2)}) collective-permute-start(bf16[192,2560]{1,0:T(8,128)(2,1)S(1)} %get-tuple-element.46), channel_id=1, source_target_pairs={{0,2},{1,3},{2,0},{3,1},{4,6},{5,7},{6,4},{7,5},{8,10},{9,11},{10,... | collective-permute-start | bytes 2949128 | tf_op jit(solution)/shard_map/ppermute | solution.py:285
  25.6 3.8 %project.5 = (bf16[96,2048]{1,0:T(8,128)(2,1)S(1)}, bf16[96,2048]{1,0:T(8,128)(2,1)S(1)}, bf16[96,2048]{1,0:T(8,128)(2,1)S(1)}, bf16[96,2048]{1,0:T(8,128)(2,1)S(1)}) custom-call(bf16[384,512]{1,0:T(8,128)(2,1)S(1)} %get-tuple-element.55.a_ref, bf16[384,512]{1,0:T(8,128)(2,1)S(1)} %collective-permute-done.1.b_ref, bf16[512,8192]{1,0:T(8,128)(2,1)} %wa_ref.7, ...), custom_call_target="tpu_custom_call" | custom-call | flops 1610612736 | bytes 5767168 | tf_op jit(solution)/shard_map/project/pallas_call | solution.py:260
  29.4 3.1 %collective-permute-start.3 = (bf16[96,2048]{1,0:T(8,128)(2,1)S(1)}, bf16[96,2048]{1,0:T(8,128)(2,1)S(1)}, u32[]{:S(2)}, u32[]{:S(2)}) collective-permute-start(bf16[96,2048]{1,0:T(8,128)(2,1)S(1)} %get-tuple-element.42), channel_id=1, source_target_pairs={{0,12},{1,13},{2,14},{3,15},{4,0},{5,1},{6,2},{7,3},{8,4},{9,5},{1... | collective-permute-start | bytes 1179656 | tf_op jit(solution)/shard_map/ppermute | solution.py:285
  32.5 3.8 %project.6 = (bf16[96,2048]{1,0:T(8,128)(2,1)S(1)}, bf16[96,2048]{1,0:T(8,128)(2,1)S(1)}, bf16[96,2048]{1,0:T(8,128)(2,1)S(1)}, bf16[96,2048]{1,0:T(8,128)(2,1)S(1)}) custom-call(bf16[384,512]{1,0:T(8,128)(2,1)S(1)} %get-tuple-element.55.a_ref, bf16[384,512]{1,0:T(8,128)(2,1)S(1)} %collective-permute-done.1.b_ref, bf16[512,8192]{1,0:T(8,128)(2,1)} %wa_ref.7, ...), custom_call_target="tpu_custom_call" | custom-call | flops 1610612736 | bytes 5767168 | tf_op jit(solution)/shard_map/project/pallas_call | solution.py:260
  36.4 0.6 collective-permute-start.6
  37.0 2.7 %collective-permute-start.9 = (bf16[96,2048]{1,0:T(8,128)(2,1)S(1)}, bf16[96,2048]{1,0:T(8,128)(2,1)S(1)}, u32[]{:S(2)}, u32[]{:S(2)}) collective-permute-start(bf16[96,2048]{1,0:T(8,128)(2,1)S(1)} %get-tuple-element.54), channel_id=1, source_target_pairs={{0,12},{1,13},{2,14},{3,15},{4,0},{5,1},{6,2},{7,3},{8,4},{9,5},{1... | collective-permute-start | bytes 1179656 | tf_op jit(solution)/shard_map/ppermute | solution.py:285
  39.7 3.2 %project.7 = (bf16[192,1536]{1,0:T(8,128)(2,1)S(1)}, bf16[192,1536]{1,0:T(8,128)(2,1)S(1)}) custom-call(bf16[384,512]{1,0:T(8,128)(2,1)S(1)} %get-tuple-element.55.a_ref, bf16[384,512]{1,0:T(8,128)(2,1)S(1)} %collective-permute-done.1.b_ref, bf16[512,8192]{1,0:T(8,128)(2,1)} %wa_ref.7, bf16[512,8192]{1,0:T(8,128)(2,1)} %collective-permute-done.2.wb_ref), custom_call_target="tpu_custom_call" | custom-call | flops 1207959552 | bytes 4325376 | tf_op jit(solution)/shard_map/project/pallas_call | solution.py:260
  42.9 4.7 %collective-permute-done.5 = bf16[192,2560]{1,0:T(8,128)(2,1)S(1)} collective-permute-done((bf16[192,2560]{1,0:T(8,128)(2,1)S(1)}, bf16[192,2560]{1,0:T(8,128)(2,1)S(1)}, u32[]{:S(2)}, u32[]{:S(2)}) %collective-permute-start.5) | collective-permute-done | bytes 983072 | tf_op jit(solution)/shard_map/ppermute | solution.py:285
  47.6 2.1 %collective-permute-done.4 = bf16[96,2048]{1,0:T(8,128)(2,1)S(1)} collective-permute-done((bf16[96,2048]{1,0:T(8,128)(2,1)S(1)}, bf16[96,2048]{1,0:T(8,128)(2,1)S(1)}, u32[]{:S(2)}, u32[]{:S(2)}) %collective-permute-start.4) | collective-permute-done | bytes 393248 | tf_op jit(solution)/shard_map/ppermute | solution.py:285
  49.8 1.0 %collective-permute-start.7 = (bf16[96,2048]{1,0:T(8,128)(2,1)S(1)}, bf16[96,2048]{1,0:T(8,128)(2,1)S(1)}, u32[]{:S(2)}, u32[]{:S(2)}) collective-permute-start(bf16[96,2048]{1,0:T(8,128)(2,1)S(1)} %add_convert_fusion.1), channel_id=1, source_target_pairs={{0,12},{1,13},{2,14},{3,15},{4,0},{5,1},{6,2},{7,3},{8,4},{9,5},{1... | collective-permute-start | bytes 1179656 | tf_op jit(solution)/shard_map/ppermute | solution.py:285
  50.9 1.1 %collective-permute-start.8 = (bf16[96,2048]{1,0:T(8,128)(2,1)S(1)}, bf16[96,2048]{1,0:T(8,128)(2,1)S(1)}, u32[]{:S(2)}, u32[]{:S(2)}) collective-permute-start(bf16[96,2048]{1,0:T(8,128)(2,1)S(1)} %add_convert_fusion), channel_id=1, source_target_pairs={{0,4},{1,5},{2,6},{3,7},{4,8},{5,9},{6,10},{7,11},{8,12},{9,13},{1... | collective-permute-start | bytes 1179656 | tf_op jit(solution)/shard_map/ppermute | solution.py:285
  52.0 1.0 %collective-permute-start.10 = (bf16[192,1536]{1,0:T(8,128)(2,1)S(1)}, bf16[192,1536]{1,0:T(8,128)(2,1)S(1)}, u32[]{:S(2)}, u32[]{:S(2)}) collective-permute-start(bf16[192,1536]{1,0:T(8,128)(2,1)S(1)} %get-tuple-element.58), channel_id=1, source_target_pairs={{0,2},{1,3},{2,0},{3,1},{4,6},{5,7},{6,4},{7,5},{8,10},{9,11},{10,... | collective-permute-start | bytes 1769480 | tf_op jit(solution)/shard_map/ppermute | solution.py:285
  53.4 4.7 %collective-permute-done.6 = bf16[96,2048]{1,0:T(8,128)(2,1)S(1)} collective-permute-done((bf16[96,2048]{1,0:T(8,128)(2,1)S(1)}, bf16[96,2048]{1,0:T(8,128)(2,1)S(1)}, u32[]{:S(2)}, u32[]{:S(2)}) %collective-permute-start.6) | collective-permute-done | bytes 393248 | tf_op jit(solution)/shard_map/ppermute | solution.py:285
  58.1 0.9 collective-permute-done.7
  59.2 5.9 %collective-permute-done.8 = bf16[96,2048]{1,0:T(8,128)(2,1)S(1)} collective-permute-done((bf16[96,2048]{1,0:T(8,128)(2,1)S(1)}, bf16[96,2048]{1,0:T(8,128)(2,1)S(1)}, u32[]{:S(2)}, u32[]{:S(2)}) %collective-permute-start.8) | collective-permute-done | bytes 393248 | tf_op jit(solution)/shard_map/ppermute | solution.py:285
  65.2 0.6 collective-permute-done.10
  66.1 1.5 %collective-permute-start.17 = (bf16[48,2048]{1,0:T(8,128)(2,1)S(1)}, bf16[48,2048]{1,0:T(8,128)(2,1)S(1)}, u32[]{:S(2)}, u32[]{:S(2)}) collective-permute-start(bf16[48,2048]{1,0:T(8,128)(2,1)S(1)} %slice.99), channel_id=1, source_target_pairs={{0,2},{1,3},{2,0},{3,1},{4,6},{5,7},{6,4},{7,5},{8,10},{9,11},{10,... | collective-permute-start | bytes 589832 | tf_op jit(solution)/shard_map/ppermute | solution.py:285
  67.8 3.2 %collective-permute-start.14 = (bf16[48,2048]{1,0:T(8,128)(2,1)S(1)}, bf16[48,2048]{1,0:T(8,128)(2,1)S(1)}, u32[]{:S(2)}, u32[]{:S(2)}) collective-permute-start(bf16[48,2048]{1,0:T(8,128)(2,1)S(1)} %get-tuple-element.63), channel_id=1, source_target_pairs={{0,12},{1,13},{2,14},{3,15},{4,0},{5,1},{6,2},{7,3},{8,4},{9,5},{1... | collective-permute-start | bytes 589832 | tf_op jit(solution)/shard_map/ppermute | solution.py:285
  71.0 1.5 %collective-permute-start.12 = (bf16[48,2048]{1,0:T(8,128)(2,1)S(1)}, bf16[48,2048]{1,0:T(8,128)(2,1)S(1)}, u32[]{:S(2)}, u32[]{:S(2)}) collective-permute-start(bf16[48,2048]{1,0:T(8,128)(2,1)S(1)} %get-tuple-element.62), channel_id=1, source_target_pairs={{0,12},{1,13},{2,14},{3,15},{4,0},{5,1},{6,2},{7,3},{8,4},{9,5},{1... | collective-permute-start | bytes 589832 | tf_op jit(solution)/shard_map/ppermute | solution.py:285
  73.1 0.7 collective-permute-start.18
  73.7 3.4 %collective-permute-done.12 = bf16[48,2048]{1,0:T(8,128)(2,1)S(1)} collective-permute-done((bf16[48,2048]{1,0:T(8,128)(2,1)S(1)}, bf16[48,2048]{1,0:T(8,128)(2,1)S(1)}, u32[]{:S(2)}, u32[]{:S(2)}) %collective-permute-start.12) | collective-permute-done | bytes 196640 | tf_op jit(solution)/shard_map/ppermute | solution.py:285
  77.2 3.7 %collective-permute-start.13 = (bf16[48,2048]{1,0:T(8,128)(2,1)S(1)}, bf16[48,2048]{1,0:T(8,128)(2,1)S(1)}, u32[]{:S(2)}, u32[]{:S(2)}) collective-permute-start(bf16[48,2048]{1,0:T(8,128)(2,1)S(1)} %fusion.1), channel_id=1, source_target_pairs={{0,12},{1,13},{2,14},{3,15},{4,0},{5,1},{6,2},{7,3},{8,4},{9,5},{1... | collective-permute-start | bytes 589832 | tf_op jit(solution)/shard_map/ppermute | solution.py:285
  81.0 3.0 %collective-permute-done.13 = bf16[48,2048]{1,0:T(8,128)(2,1)S(1)} collective-permute-done((bf16[48,2048]{1,0:T(8,128)(2,1)S(1)}, bf16[48,2048]{1,0:T(8,128)(2,1)S(1)}, u32[]{:S(2)}, u32[]{:S(2)}) %collective-permute-start.13) | collective-permute-done | bytes 196640 | tf_op jit(solution)/shard_map/ppermute | solution.py:285
  84.2 3.7 %collective-permute-done.16 = bf16[48,2048]{1,0:T(8,128)(2,1)S(1)} collective-permute-done((bf16[48,2048]{1,0:T(8,128)(2,1)S(1)}, bf16[48,2048]{1,0:T(8,128)(2,1)S(1)}, u32[]{:S(2)}, u32[]{:S(2)}) %collective-permute-start.16) | collective-permute-done | bytes 196640 | tf_op jit(solution)/shard_map/ppermute | solution.py:285
  88.0 1.0 %fusion = bf16[48,8192]{1,0:T(8,128)(2,1)} fusion(f32[48,2048]{1,0:T(8,128)S(1)} %slice_add_fusion, f32[48,2048]{1,0:T(8,128)S(1)} %slice_add_fusion.1, f32[48,2048]{1,0:T(8,128)S(1)} %fusion.3, f32[48,2048]{1,0:T(8,128)S(1)} %fusion.2, bf16[48,8192]{1,0:T(8,128)(2,1)S(1)} %copy-done.1), kind=kLoop, calls=%fused_computation.2 | loop fusion | flops 2359296 | bytes 3145728 | tf_op jit(solution)/shard_map/convert_element_type | solution.py:322
  (38 shorter events, 2.4 us)
Async XLA Ops:
  0.0 18.9 %collective-permute-start.2 = (bf16[512,8192]{1,0:T(8,128)(2,1)}, bf16[512,8192]{1,0:T(8,128)(2,1)}, u32[]{:S(2)}, u32[]{:S(2)}) collective-permute-start(bf16[512,8192]{1,0:T(8,128)(2,1)} %wa_ref.7), channel_id=1, source_target_pairs={{0,1},{1,0},{2,3},{3,2},{4,5},{5,4},{6,7},{7,6},{8,9},{9,8},{10,11... | collective-permute-start | bytes 25165832 | tf_op jit(solution)/shard_map/ppermute | solution.py:285
  1.3 12.2 %collective-permute-start = (bf16[144,512]{1,0:T(8,128)(2,1)S(1)}, bf16[144,512]{1,0:T(8,128)(2,1)S(1)}, u32[]{:S(2)}, u32[]{:S(2)}) collective-permute-start(bf16[144,512]{1,0:T(8,128)(2,1)S(1)} %rim.1), channel_id=1, source_target_pairs={{0,16},{16,32},{32,48},{48,64},{64,80},{80,96},{96,112},{112,128},... | collective-permute-start | bytes 442376 | tf_op jit(solution)/shard_map/ppermute | solution.py:305
  5.1 8.4 %copy-start = (s32[256]{0:T(256)S(1)}, s32[256]{0:T(256)}, u32[]{:S(2)}) copy-start(s32[256]{0:T(256)} %constant.12.clone.order_ref) | copy-start | bytes 3076
  17.1 1.8 %collective-permute-start.1 = (bf16[384,512]{1,0:T(8,128)(2,1)S(1)}, bf16[384,512]{1,0:T(8,128)(2,1)S(1)}, u32[]{:S(2)}, u32[]{:S(2)}) collective-permute-start(bf16[384,512]{1,0:T(8,128)(2,1)S(1)} %get-tuple-element.39), channel_id=1, source_target_pairs={{0,1},{1,0},{2,3},{3,2},{4,5},{5,4},{6,7},{7,6},{8,9},{9,8},{10,11... | collective-permute-start | bytes 1179656 | tf_op jit(solution)/shard_map/ppermute | solution.py:285
  23.4 24.2 %collective-permute-start.5 = (bf16[192,2560]{1,0:T(8,128)(2,1)S(1)}, bf16[192,2560]{1,0:T(8,128)(2,1)S(1)}, u32[]{:S(2)}, u32[]{:S(2)}) collective-permute-start(bf16[192,2560]{1,0:T(8,128)(2,1)S(1)} %get-tuple-element.46), channel_id=1, source_target_pairs={{0,2},{1,3},{2,0},{3,1},{4,6},{5,7},{6,4},{7,5},{8,10},{9,11},{10,... | collective-permute-start | bytes 2949128 | tf_op jit(solution)/shard_map/ppermute | solution.py:285
  29.4 18.2 %collective-permute-start.3 = (bf16[96,2048]{1,0:T(8,128)(2,1)S(1)}, bf16[96,2048]{1,0:T(8,128)(2,1)S(1)}, u32[]{:S(2)}, u32[]{:S(2)}) collective-permute-start(bf16[96,2048]{1,0:T(8,128)(2,1)S(1)} %get-tuple-element.42), channel_id=1, source_target_pairs={{0,12},{1,13},{2,14},{3,15},{4,0},{5,1},{6,2},{7,3},{8,4},{9,5},{1... | collective-permute-start | bytes 1179656 | tf_op jit(solution)/shard_map/ppermute | solution.py:285
  36.3 13.3 %collective-permute-start.4 = (bf16[96,2048]{1,0:T(8,128)(2,1)S(1)}, bf16[96,2048]{1,0:T(8,128)(2,1)S(1)}, u32[]{:S(2)}, u32[]{:S(2)}) collective-permute-start(bf16[96,2048]{1,0:T(8,128)(2,1)S(1)} %get-tuple-element.45), channel_id=1, source_target_pairs={{0,4},{1,5},{2,6},{3,7},{4,8},{5,9},{6,10},{7,11},{8,12},{9,13},{1... | collective-permute-start | bytes 1179656 | tf_op jit(solution)/shard_map/ppermute | solution.py:285
  36.4 21.7 %collective-permute-start.6 = (bf16[96,2048]{1,0:T(8,128)(2,1)S(1)}, bf16[96,2048]{1,0:T(8,128)(2,1)S(1)}, u32[]{:S(2)}, u32[]{:S(2)}) collective-permute-start(bf16[96,2048]{1,0:T(8,128)(2,1)S(1)} %get-tuple-element.48), channel_id=1, source_target_pairs={{0,4},{1,5},{2,6},{3,7},{4,8},{5,9},{6,10},{7,11},{8,12},{9,13},{1... | collective-permute-start | bytes 1179656 | tf_op jit(solution)/shard_map/ppermute | solution.py:285
  37.0 22.1 %collective-permute-start.9 = (bf16[96,2048]{1,0:T(8,128)(2,1)S(1)}, bf16[96,2048]{1,0:T(8,128)(2,1)S(1)}, u32[]{:S(2)}, u32[]{:S(2)}) collective-permute-start(bf16[96,2048]{1,0:T(8,128)(2,1)S(1)} %get-tuple-element.54), channel_id=1, source_target_pairs={{0,12},{1,13},{2,14},{3,15},{4,0},{5,1},{6,2},{7,3},{8,4},{9,5},{1... | collective-permute-start | bytes 1179656 | tf_op jit(solution)/shard_map/ppermute | solution.py:285
  49.8 9.2 %collective-permute-start.7 = (bf16[96,2048]{1,0:T(8,128)(2,1)S(1)}, bf16[96,2048]{1,0:T(8,128)(2,1)S(1)}, u32[]{:S(2)}, u32[]{:S(2)}) collective-permute-start(bf16[96,2048]{1,0:T(8,128)(2,1)S(1)} %add_convert_fusion.1), channel_id=1, source_target_pairs={{0,12},{1,13},{2,14},{3,15},{4,0},{5,1},{6,2},{7,3},{8,4},{9,5},{1... | collective-permute-start | bytes 1179656 | tf_op jit(solution)/shard_map/ppermute | solution.py:285
  50.9 14.2 %collective-permute-start.8 = (bf16[96,2048]{1,0:T(8,128)(2,1)S(1)}, bf16[96,2048]{1,0:T(8,128)(2,1)S(1)}, u32[]{:S(2)}, u32[]{:S(2)}) collective-permute-start(bf16[96,2048]{1,0:T(8,128)(2,1)S(1)} %add_convert_fusion), channel_id=1, source_target_pairs={{0,4},{1,5},{2,6},{3,7},{4,8},{5,9},{6,10},{7,11},{8,12},{9,13},{1... | collective-permute-start | bytes 1179656 | tf_op jit(solution)/shard_map/ppermute | solution.py:285
  52.0 13.8 %collective-permute-start.10 = (bf16[192,1536]{1,0:T(8,128)(2,1)S(1)}, bf16[192,1536]{1,0:T(8,128)(2,1)S(1)}, u32[]{:S(2)}, u32[]{:S(2)}) collective-permute-start(bf16[192,1536]{1,0:T(8,128)(2,1)S(1)} %get-tuple-element.58), channel_id=1, source_target_pairs={{0,2},{1,3},{2,0},{3,1},{4,6},{5,7},{6,4},{7,5},{8,10},{9,11},{10,... | collective-permute-start | bytes 1769480 | tf_op jit(solution)/shard_map/ppermute | solution.py:285
  66.1 6.9 %collective-permute-start.17 = (bf16[48,2048]{1,0:T(8,128)(2,1)S(1)}, bf16[48,2048]{1,0:T(8,128)(2,1)S(1)}, u32[]{:S(2)}, u32[]{:S(2)}) collective-permute-start(bf16[48,2048]{1,0:T(8,128)(2,1)S(1)} %slice.99), channel_id=1, source_target_pairs={{0,2},{1,3},{2,0},{3,1},{4,6},{5,7},{6,4},{7,5},{8,10},{9,11},{10,... | collective-permute-start | bytes 589832 | tf_op jit(solution)/shard_map/ppermute | solution.py:285
  67.7 13.4 %collective-permute-start.11 = (bf16[48,2048]{1,0:T(8,128)(2,1)S(1)}, bf16[48,2048]{1,0:T(8,128)(2,1)S(1)}, u32[]{:S(2)}, u32[]{:S(2)}) collective-permute-start(bf16[48,2048]{1,0:T(8,128)(2,1)S(1)} %get-tuple-element.61), channel_id=1, source_target_pairs={{0,4},{1,5},{2,6},{3,7},{4,8},{5,9},{6,10},{7,11},{8,12},{9,13},{1... | collective-permute-start | bytes 589832 | tf_op jit(solution)/shard_map/ppermute | solution.py:285
  67.8 16.4 %collective-permute-start.14 = (bf16[48,2048]{1,0:T(8,128)(2,1)S(1)}, bf16[48,2048]{1,0:T(8,128)(2,1)S(1)}, u32[]{:S(2)}, u32[]{:S(2)}) collective-permute-start(bf16[48,2048]{1,0:T(8,128)(2,1)S(1)} %get-tuple-element.63), channel_id=1, source_target_pairs={{0,12},{1,13},{2,14},{3,15},{4,0},{5,1},{6,2},{7,3},{8,4},{9,5},{1... | collective-permute-start | bytes 589832 | tf_op jit(solution)/shard_map/ppermute | solution.py:285
  71.0 6.2 %collective-permute-start.12 = (bf16[48,2048]{1,0:T(8,128)(2,1)S(1)}, bf16[48,2048]{1,0:T(8,128)(2,1)S(1)}, u32[]{:S(2)}, u32[]{:S(2)}) collective-permute-start(bf16[48,2048]{1,0:T(8,128)(2,1)S(1)} %get-tuple-element.62), channel_id=1, source_target_pairs={{0,12},{1,13},{2,14},{3,15},{4,0},{5,1},{6,2},{7,3},{8,4},{9,5},{1... | collective-permute-start | bytes 589832 | tf_op jit(solution)/shard_map/ppermute | solution.py:285
  72.4 8.4 %collective-permute-start.15 = (bf16[48,2048]{1,0:T(8,128)(2,1)S(1)}, bf16[48,2048]{1,0:T(8,128)(2,1)S(1)}, u32[]{:S(2)}, u32[]{:S(2)}) collective-permute-start(bf16[48,2048]{1,0:T(8,128)(2,1)S(1)} %get-tuple-element.64), channel_id=1, source_target_pairs={{0,4},{1,5},{2,6},{3,7},{4,8},{5,9},{6,10},{7,11},{8,12},{9,13},{1... | collective-permute-start | bytes 589832 | tf_op jit(solution)/shard_map/ppermute | solution.py:285
  73.1 11.1 %collective-permute-start.18 = (bf16[48,2048]{1,0:T(8,128)(2,1)S(1)}, bf16[48,2048]{1,0:T(8,128)(2,1)S(1)}, u32[]{:S(2)}, u32[]{:S(2)}) collective-permute-start(bf16[48,2048]{1,0:T(8,128)(2,1)S(1)} %slice.98), channel_id=1, source_target_pairs={{0,2},{1,3},{2,0},{3,1},{4,6},{5,7},{6,4},{7,5},{8,10},{9,11},{10,... | collective-permute-start | bytes 589832 | tf_op jit(solution)/shard_map/ppermute | solution.py:285
  77.2 6.8 %collective-permute-start.13 = (bf16[48,2048]{1,0:T(8,128)(2,1)S(1)}, bf16[48,2048]{1,0:T(8,128)(2,1)S(1)}, u32[]{:S(2)}, u32[]{:S(2)}) collective-permute-start(bf16[48,2048]{1,0:T(8,128)(2,1)S(1)} %fusion.1), channel_id=1, source_target_pairs={{0,12},{1,13},{2,14},{3,15},{4,0},{5,1},{6,2},{7,3},{8,4},{9,5},{1... | collective-permute-start | bytes 589832 | tf_op jit(solution)/shard_map/ppermute | solution.py:285
  80.9 7.0 %copy-start.1 = (bf16[48,8192]{1,0:T(8,128)(2,1)S(1)}, bf16[48,8192]{1,0:T(8,128)(2,1)}, u32[]{:S(2)}) copy-start(bf16[48,8192]{1,0:T(8,128)(2,1)} %param.18) | copy-start | bytes 2359300
  80.9 7.0 %collective-permute-start.16 = (bf16[48,2048]{1,0:T(8,128)(2,1)S(1)}, bf16[48,2048]{1,0:T(8,128)(2,1)S(1)}, u32[]{:S(2)}, u32[]{:S(2)}) collective-permute-start(bf16[48,2048]{1,0:T(8,128)(2,1)S(1)} %fusion.4), channel_id=1, source_target_pairs={{0,4},{1,5},{2,6},{3,7},{4,8},{5,9},{6,10},{7,11},{8,12},{9,13},{1... | collective-permute-start | bytes 589832 | tf_op jit(solution)/shard_map/ppermute | solution.py:285

commit v5 on v4

--- a/solution.py
+++ b/solution.py
@@ -231,43 +231,129 @@
     )
 
 
-def project_kernel(first, count, tile, pieces, a_ref, b_ref, wa_ref, wb_ref, *out_refs):
-    depth = wa_ref.shape[0]
-
-    def step(wa, wb, *outs):
-        acc = jnp.dot(a_ref[...], wa[...], preferred_element_type=jnp.float32)
-        acc = acc + jnp.dot(b_ref[...], wb[...], preferred_element_type=jnp.float32)
-        acc = acc.astype(jnp.bfloat16)
-        for ref, spans in zip(outs, pieces):
-            at = 0
-            for start, stop in spans:
-                ref[at : at + stop - start] = acc[start:stop]
-                at += stop - start
-
-    rhs = pl.BlockSpec((depth, tile), lambda j: (0, j))
-    pltpu.emit_pipeline(
-        step,
+def scatter_rows(acc, refs, pieces):
+    acc = acc.astype(jnp.bfloat16)
+    for ref, spans in zip(refs, pieces):
+        at = 0
+        for start, stop in spans:
+            ref[at : at + stop - start] = acc[start:stop]
+            at += stop - start
+
+
+def both_products(a_ref, b_ref, wa_ref, wb_ref):
+    acc = jnp.dot(a_ref[...], wa_ref[...], preferred_element_type=jnp.float32)
+    return acc + jnp.dot(b_ref[...], wb_ref[...], preferred_element_type=jnp.float32)
+
+
+def own_kernel(a_ref, wa_ref, part_ref):
+    part_ref[...] = jnp.dot(a_ref[...], wa_ref[...], preferred_element_type=jnp.float32)
+
+
+def rest_kernel(pieces, b_ref, wb_ref, part_ref, *out_refs):
+    acc = part_ref[...] + jnp.dot(b_ref[...], wb_ref[...], preferred_element_type=jnp.float32)
+    scatter_rows(acc, out_refs, pieces)
+
+
+def project_kernel(pieces, half, a_ref, b_ref, wa_ref, wb_ref, *out_refs):
+    acc = both_products(a_ref, b_ref, wa_ref, wb_ref)
+    if half is None:
+        scatter_rows(acc, out_refs, pieces)
+        return
+    j = pl.program_id(0)
+
+    @pl.when(j < half)
+    def _():
+        scatter_rows(acc, out_refs[: len(pieces)], pieces)
+
+    @pl.when(j >= half)
+    def _():
+        scatter_rows(acc, out_refs[len(pieces) :], pieces)
+
+
+def project_call(kernel, operands, specs, out_shape, out_specs, count, tile, depth, name):
+    rows = operands[0].shape[0]
+    return pl.pallas_call(
+        kernel,
         grid=(count // tile,),
-        in_specs=[rhs, rhs],
-        out_specs=[pl.BlockSpec((ref.shape[0], tile), lambda j: (0, j)) for ref in out_refs],
-    )(wa_ref.at[:, pl.ds(first, count)], wb_ref.at[:, pl.ds(first, count)], *out_refs)
-
-
-def project(mine, theirs, weight, weight_pair, first, count, tile, pieces):
-    rows, depth = mine.shape
-    sizes = [sum(stop - start for start, stop in spans) for spans in pieces]
-    anywhere = pl.BlockSpec(memory_space=pl.ANY)
-    return pl.pallas_call(
-        functools.partial(project_kernel, first, count, tile, pieces),
-        out_shape=[jax.ShapeDtypeStruct((n, count), jnp.bfloat16) for n in sizes],
-        in_specs=[pl.BlockSpec(memory_space=pltpu.VMEM)] * 2 + [pl.BlockSpec(memory_space=pltpu.HBM)] * 2,
-        out_specs=[anywhere] * len(sizes),
+        out_shape=out_shape,
+        in_specs=specs,
+        out_specs=out_specs,
         compiler_params=pltpu.CompilerParams(vmem_limit_bytes=VMEM_LIMIT),
         cost_estimate=pl.CostEstimate(
-            flops=4 * rows * depth * count, bytes_accessed=2 * (2 * depth + rows) * count, transcendentals=0
+            flops=2 * rows * depth * count, bytes_accessed=2 * (depth + rows) * count, transcendentals=0
         ),
-        name="project",
-    )(mine, theirs, stay(weight), stay(weight_pair))
+        name=name,
+    )(*operands)
+
+
+def weight_block(depth, first, tile):
+    return pl.BlockSpec((depth, tile), lambda j: (0, j + first // tile))
+
+
+def row_sizes(pieces):
+    return [sum(stop - start for start, stop in spans) for spans in pieces]
+
+
+def project_own(mine, weight, first, count, tile):
+    rows, depth = mine.shape
+    return project_call(
+        own_kernel,
+        (mine, stay(weight)),
+        [pl.BlockSpec((rows, depth), lambda j: (0, 0)), weight_block(depth, first, tile)],
+        jax.ShapeDtypeStruct((rows, count), jnp.float32),
+        pl.BlockSpec((rows, tile), lambda j: (0, j)),
+        count,
+        tile,
+        depth,
+        "project_own",
+    )
+
+
+def project_rest(theirs, weight_pair, part, first, tile, pieces):
+    rows, depth = theirs.shape
+    count = part.shape[1]
+    return project_call(
+        functools.partial(rest_kernel, pieces),
+        (theirs, stay(weight_pair), part),
+        [
+            pl.BlockSpec((rows, depth), lambda j: (0, 0)),
+            weight_block(depth, first, tile),
+            pl.BlockSpec((rows, tile), lambda j: (0, j)),
+        ],
+        [jax.ShapeDtypeStruct((n, count), jnp.bfloat16) for n in row_sizes(pieces)],
+        [pl.BlockSpec((n, tile), lambda j: (0, j)) for n in row_sizes(pieces)],
+        count,
+        tile,
+        depth,
+        "project_rest",
+    )
+
+
+def project(mine, theirs, weight, weight_pair, first, count, tile, pieces, halves=False):
+    rows, depth = mine.shape
+    lhs = pl.BlockSpec((rows, depth), lambda j: (0, 0))
+    rhs = weight_block(depth, first, tile)
+    sizes = row_sizes(pieces)
+    if halves:
+        half = count // tile // 2
+        shapes = [jax.ShapeDtypeStruct((n, count // 2), jnp.bfloat16) for n in sizes] * 2
+        out_specs = [pl.BlockSpec((n, tile), lambda j: (0, jnp.minimum(j, half - 1))) for n in sizes]
+        out_specs += [pl.BlockSpec((n, tile), lambda j: (0, jnp.maximum(j - half, 0))) for n in sizes]
+    else:
+        half = None
+        shapes = [jax.ShapeDtypeStruct((n, count), jnp.bfloat16) for n in sizes]
+        out_specs = [pl.BlockSpec((n, tile), lambda j: (0, j)) for n in sizes]
+    return project_call(
+        functools.partial(project_kernel, pieces, half),
+        (mine, theirs, stay(weight), stay(weight_pair)),
+        [lhs, lhs, rhs, rhs],
+        shapes,
+        out_specs,
+        count,
+        tile,
+        2 * depth,
+        "project",
+    )
 
 
 def moved(dy=0, dx=0, dc=0):
@@ -312,20 +398,22 @@
     half = rows // (2 * N_C)
     by_x = (((0, half),), ((half, 2 * half),))
     by_y = tuple(((s * piece, (s + 1) * piece), (half + s * piece, half + (s + 1) * piece)) for s in range(N_Y))
-    y_first = (width - sum(X_FIRST)) // 2
-
-    def multiply(after, first, count, pieces):
-        left = lax.optimization_barrier((keep, after))[0]
-        return project(left, theirs, out_weight, weight_pair, first, count, count // 2, pieces)
 
     def narrow(array):
         return array.astype(jnp.bfloat16)
 
-    a0_keep, a0_give = multiply(place, 0, X_FIRST[0], by_x)
+    edge = sum(X_FIRST)
+    a0_part = project_own(keep, out_weight, 0, X_FIRST[0], X_FIRST[0] // 2)
+    a0_keep, a0_give = project_rest(theirs, weight_pair, a0_part, 0, X_FIRST[0] // 2, by_x)
     a0_got = send(a0_give, dx=1)
-    b0 = multiply(a0_keep, sum(X_FIRST), y_first, by_y)
-    b1 = multiply(b0[0], sum(X_FIRST) + y_first, y_first, by_y)
-    a1_keep, a1_give = multiply(b1[0], X_FIRST[0], X_FIRST[1], by_x)
+    left = lax.optimization_barrier((keep, a0_keep))[0]
+    tile = (width - edge) // 4
+    b_all = project(left, theirs, out_weight, weight_pair, edge, width - edge, tile, by_y, halves=True)
+    b0, b1 = b_all[:N_Y], b_all[N_Y:]
+    left = lax.optimization_barrier((keep, b0[0]))[0]
+    a1_keep, a1_give = project(
+        left, theirs, out_weight, weight_pair, X_FIRST[0], X_FIRST[1], math.gcd(*X_FIRST), by_x
+    )
 
     b1_far = send(b1[2], dy=1)
     b0_far = send(b0[2], dy=-1)
@@ -356,7 +444,7 @@
     low_up = send(low_send[1], dy=1)
     high_down = send(high_send[3], dy=-1)
 
-    b0_got, b1_give = lax.optimization_barrier((b0_got, b1_give))
+    low_far, high_far, b0_got, b1_give = lax.optimization_barrier((low_far, high_far, b0_got, b1_give))
     low_down = send(narrow(add(low[3], low_far)), dy=-1)
     high_up = send(narrow(add(high[1], high_far)), dy=1)
     b1_got = send(b1_give, dx=1)

time: 89.2 us -> 86.2 us (0.966)
  waiting for transfers between devices: 35.1 us -> 31.3 us
    ppermute x18, waiting for transfers between devices: 30.7 us -> 26.9 us  [send(): return lax.ppermute(array, 'tp', moved(**step))]
  transfers between devices with their start and end apart: 19 -> 19, of which waited for: 11 -> 12; matrix products, arithmetic and copies ran while one was open for 1% -> 1% of each run, Pallas kernels for 22% -> 26%
where the time goes in v5:
time: 86.2 us; the launch traced here: 85.8 us
  waiting for transfers between devices  31.3 us (36%)
  starting transfers between devices  26.9 us (31%)
  Pallas kernels  24.9 us (29%)
  other arithmetic  2.33 us (3%)
    ppermute x18, waiting for transfers between devices, send(): return lax.ppermute(array, 'tp', moved(**step))  26.9 us
    ppermute x18, starting transfers between devices, send(): return lax.ppermute(array, 'tp', moved(**step))  23.1 us
    pallas_call x4, Pallas kernels, project_call(): pl.pallas_call(kernel, grid=(count // tile,), out_shape=out_shape, in_spe...  16.1 us
    ppermute x1, waiting for transfers between devices, body(): halo = lax.ppermute(rim, 'ctx', [(i, i + 1) for i in range(peers - 1)])  4.4 us
    pallas_call x1, Pallas kernels, gate_late(): pl.pallas_call(functools.partial(late_kernel, EARLY), grid=(channels // W...  3.95 us
    ppermute x1, starting transfers between devices, body(): halo = lax.ppermute(rim, 'ctx', [(i, i + 1) for i in range(peers - 1)])  3.83 us
    pallas_call x1, Pallas kernels, gate_early(): pl.pallas_call(early_kernel, grid_spec=pltpu.PrefetchScalarGridSpec(num_s...  3.58 us
  transfers between devices with their start and end apart: 19, of which 12 were waited for; matrix products, arithmetic and copies ran while one was open for 1% of the time, Pallas kernels for 26%

profile of v5, /device:TPU:4, one launch (start us, length us, event | category | flops | bytes accessed | tf_op | source)
XLA Modules:
  0.0 85.8 jit_solution(10420549372828527486)
XLA Ops:
  0.0 1.2 %rim.1 = bf16[144,512]{1,0:T(8,128)(2,1)S(1)} custom-call(bf16[768,512]{1,0:T(8,128)(2,1)} %q_ref.5, bf16[768,512]{1,0:T(8,128)(2,1)} %k_ref.5, bf16[768,512]{1,0:T(8,128)(2,1)} %v_ref.5, bf16[3,512]{1,0:T(4,128)(2,1)} %taps_ref.5), custom_call_target="tpu_custom_call" | custom-call | flops 1000000000 | bytes 1000000 | tf_op jit(solution)/shard_map/rim/pallas_call | solution.py:160
  1.3 3.8 %collective-permute-start = (bf16[144,512]{1,0:T(8,128)(2,1)S(1)}, bf16[144,512]{1,0:T(8,128)(2,1)S(1)}, u32[]{:S(2)}, u32[]{:S(2)}) collective-permute-start(bf16[144,512]{1,0:T(8,128)(2,1)S(1)} %rim.1), channel_id=1, source_target_pairs={{0,16},{16,32},{32,48},{48,64},{64,80},{80,96},{96,112},{112,128},... | collective-permute-start | bytes 442376 | tf_op jit(solution)/shard_map/ppermute | solution.py:391
  5.1 4.0 %gate_late.1.late_ref = bf16[512,512]{1,0:T(8,128)(2,1)S(1)} custom-call(bf16[768,512]{1,0:T(8,128)(2,1)} %q_ref.5, bf16[768,512]{1,0:T(8,128)(2,1)} %k_ref.5, bf16[768,512]{1,0:T(8,128)(2,1)} %v_ref.5, bf16[3,512]{1,0:T(4,128)(2,1)} %taps_ref.5, bf16[512,128]{1,0:T(8,128)(2,1)} %filt_ref.3, f32[1,512]{1,0:T(1,128)} %bitcast.2, ...), custom_call_target="tpu_custom_call" | custom-call | flops 4000000000 | bytes 3000000 | tf_op jit(solution)/shard_map/gate_late/pallas_call | solution.py:190
  9.1 4.4 %collective-permute-done.halo_ref = bf16[144,512]{1,0:T(8,128)(2,1)S(1)} collective-permute-done((bf16[144,512]{1,0:T(8,128)(2,1)S(1)}, bf16[144,512]{1,0:T(8,128)(2,1)S(1)}, u32[]{:S(2)}, u32[]{:S(2)}) %collective-permute-start) | collective-permute-done | bytes 147488 | tf_op jit(solution)/shard_map/ppermute | solution.py:391
  13.5 3.6 %gate_early.1 = (bf16[384,512]{1,0:T(8,128)(2,1)S(1)}, bf16[384,512]{1,0:T(8,128)(2,1)S(1)}) custom-call(s32[1]{0:T(128)} %bitcast.place_ref, s32[256]{0:T(256)S(1)} %copy-done, bf16[768,512]{1,0:T(8,128)(2,1)} %q_ref.5, bf16[768,512]{1,0:T(8,128)(2,1)} %k_ref.5, bf16[768,512]{1,0:T(8,128)(2,1)} %v_ref.5, ...), custom_call_target="tpu_custom_call" | custom-call | flops 2000000000 | bytes 3000000 | tf_op jit(solution)/shard_map/gate_early/pallas_call | solution.py:206
  17.2 2.9 %project_own.1.part_ref = f32[384,2560]{1,0:T(8,128)S(1)} custom-call(bf16[384,512]{1,0:T(8,128)(2,1)S(1)} %get-tuple-element.53.a_ref, bf16[512,8192]{1,0:T(8,128)(2,1)} %wa_ref.5), custom_call_target="tpu_custom_call" | custom-call | flops 1006632960 | bytes 4587520 | tf_op jit(solution)/shard_map/project_own/pallas_call | solution.py:275
  20.1 2.8 %project_rest.1 = (bf16[192,2560]{1,0:T(8,128)(2,1)S(1)}, bf16[192,2560]{1,0:T(8,128)(2,1)S(1)}) custom-call(bf16[384,512]{1,0:T(8,128)(2,1)S(1)} %collective-permute-done.1.b_ref, bf16[512,8192]{1,0:T(8,128)(2,1)} %collective-permute-done.2.wb_ref, f32[384,2560]{1,0:T(8,128)S(1)} %project_own.1.part_ref), custom_call_target="tpu_custom_call" | custom-call | flops 1006632960 | bytes 4587520 | tf_op jit(solution)/shard_map/project_rest/pallas_call | solution.py:275
  23.0 2.2 %collective-permute-start.5 = (bf16[192,2560]{1,0:T(8,128)(2,1)S(1)}, bf16[192,2560]{1,0:T(8,128)(2,1)S(1)}, u32[]{:S(2)}, u32[]{:S(2)}) collective-permute-start(bf16[192,2560]{1,0:T(8,128)(2,1)S(1)} %get-tuple-element.43), channel_id=1, source_target_pairs={{0,2},{1,3},{2,0},{3,1},{4,6},{5,7},{6,4},{7,5},{8,10},{9,11},{10,... | collective-permute-start | bytes 2949128 | tf_op jit(solution)/shard_map/ppermute | solution.py:371
  25.2 6.7 %project.2 = (bf16[96,2048]{1,0:T(8,128)(2,1)S(1)}, bf16[96,2048]{1,0:T(8,128)(2,1)S(1)}, bf16[96,2048]{1,0:T(8,128)(2,1)S(1)}, bf16[96,2048]{1,0:T(8,128)(2,1)S...) custom-call(bf16[384,512]{1,0:T(8,128)(2,1)S(1)} %get-tuple-element., ...), custom_call_target="tpu_custom_call" | custom-call | flops 3221225472 | bytes 11534336 | tf_op jit(solution)/shard_map/project/pallas_call | solution.py:275
  31.9 3.1 %collective-permute-start.3 = (bf16[96,2048]{1,0:T(8,128)(2,1)S(1)}, bf16[96,2048]{1,0:T(8,128)(2,1)S(1)}, u32[]{:S(2)}, u32[]{:S(2)}) collective-permute-start(bf16[96,2048]{1,0:T(8,128)(2,1)S(1)} %get-tuple-element.41), channel_id=1, source_target_pairs={{0,12},{1,13},{2,14},{3,15},{4,0},{5,1},{6,2},{7,3},{8,4},{9,5},{1... | collective-permute-start | bytes 1179656 | tf_op jit(solution)/shard_map/ppermute | solution.py:371
  35.6 2.7 %collective-permute-start.9 = (bf16[96,2048]{1,0:T(8,128)(2,1)S(1)}, bf16[96,2048]{1,0:T(8,128)(2,1)S(1)}, u32[]{:S(2)}, u32[]{:S(2)}) collective-permute-start(bf16[96,2048]{1,0:T(8,128)(2,1)S(1)} %get-tuple-element.52), channel_id=1, source_target_pairs={{0,12},{1,13},{2,14},{3,15},{4,0},{5,1},{6,2},{7,3},{8,4},{9,5},{1... | collective-permute-start | bytes 1179656 | tf_op jit(solution)/shard_map/ppermute | solution.py:371
  38.2 3.6 %project.3 = (bf16[192,1536]{1,0:T(8,128)(2,1)S(1)}, bf16[192,1536]{1,0:T(8,128)(2,1)S(1)}) custom-call(bf16[384,512]{1,0:T(8,128)(2,1)S(1)} %get-tuple-element.53.a_ref, bf16[384,512]{1,0:T(8,128)(2,1)S(1)} %collective-permute-done.1.b_ref, bf16[512,8192]{1,0:T(8,128)(2,1)} %wa_ref.5, bf16[512,8192]{1,0:T(8,128)(2,1)} %collective-permute-done.2.wb_ref), custom_call_target="tpu_custom_call" | custom-call | flops 1207959552 | bytes 4325376 | tf_op jit(solution)/shard_map/project/pallas_call | solution.py:275
  41.9 2.6 %collective-permute-done.3 = bf16[96,2048]{1,0:T(8,128)(2,1)S(1)} collective-permute-done((bf16[96,2048]{1,0:T(8,128)(2,1)S(1)}, bf16[96,2048]{1,0:T(8,128)(2,1)S(1)}, u32[]{:S(2)}, u32[]{:S(2)}) %collective-permute-start.3) | collective-permute-done | bytes 393248 | tf_op jit(solution)/shard_map/ppermute | solution.py:371
  44.4 3.7 %collective-permute-done.4 = bf16[96,2048]{1,0:T(8,128)(2,1)S(1)} collective-permute-done((bf16[96,2048]{1,0:T(8,128)(2,1)S(1)}, bf16[96,2048]{1,0:T(8,128)(2,1)S(1)}, u32[]{:S(2)}, u32[]{:S(2)}) %collective-permute-start.4) | collective-permute-done | bytes 393248 | tf_op jit(solution)/shard_map/ppermute | solution.py:371
  48.3 2.5 %collective-permute-start.7 = (bf16[96,2048]{1,0:T(8,128)(2,1)S(1)}, bf16[96,2048]{1,0:T(8,128)(2,1)S(1)}, u32[]{:S(2)}, u32[]{:S(2)}) collective-permute-start(bf16[96,2048]{1,0:T(8,128)(2,1)S(1)} %add_convert_fusion.1), channel_id=1, source_target_pairs={{0,12},{1,13},{2,14},{3,15},{4,0},{5,1},{6,2},{7,3},{8,4},{9,5},{1... | collective-permute-start | bytes 1179656 | tf_op jit(solution)/shard_map/ppermute | solution.py:371
  50.8 1.7 %collective-permute-start.10 = (bf16[192,1536]{1,0:T(8,128)(2,1)S(1)}, bf16[192,1536]{1,0:T(8,128)(2,1)S(1)}, u32[]{:S(2)}, u32[]{:S(2)}) collective-permute-start(bf16[192,1536]{1,0:T(8,128)(2,1)S(1)} %get-tuple-element.56), channel_id=1, source_target_pairs={{0,2},{1,3},{2,0},{3,1},{4,6},{5,7},{6,4},{7,5},{8,10},{9,11},{10,... | collective-permute-start | bytes 1769480 | tf_op jit(solution)/shard_map/ppermute | solution.py:371
  53.3 2.3 %collective-permute-done.6 = bf16[96,2048]{1,0:T(8,128)(2,1)S(1)} collective-permute-done((bf16[96,2048]{1,0:T(8,128)(2,1)S(1)}, bf16[96,2048]{1,0:T(8,128)(2,1)S(1)}, u32[]{:S(2)}, u32[]{:S(2)}) %collective-permute-start.6) | collective-permute-done | bytes 393248 | tf_op jit(solution)/shard_map/ppermute | solution.py:371
  55.5 5.0 %collective-permute-done.7 = bf16[96,2048]{1,0:T(8,128)(2,1)S(1)} collective-permute-done((bf16[96,2048]{1,0:T(8,128)(2,1)S(1)}, bf16[96,2048]{1,0:T(8,128)(2,1)S(1)}, u32[]{:S(2)}, u32[]{:S(2)}) %collective-permute-start.7) | collective-permute-done | bytes 393248 | tf_op jit(solution)/shard_map/ppermute | solution.py:371
  60.7 3.8 %collective-permute-done.8 = bf16[96,2048]{1,0:T(8,128)(2,1)S(1)} collective-permute-done((bf16[96,2048]{1,0:T(8,128)(2,1)S(1)}, bf16[96,2048]{1,0:T(8,128)(2,1)S(1)}, u32[]{:S(2)}, u32[]{:S(2)}) %collective-permute-start.8) | collective-permute-done | bytes 393248 | tf_op jit(solution)/shard_map/ppermute | solution.py:371
  64.7 0.9 %collective-permute-done.10 = bf16[192,1536]{1,0:T(8,128)(2,1)S(1)} collective-permute-done((bf16[192,1536]{1,0:T(8,128)(2,1)S(1)}, bf16[192,1536]{1,0:T(8,128)(2,1)S(1)}, u32[]{:S(2)}, u32[]{:S(2)}) %collective-permute-start.10) | collective-permute-done | bytes 589856 | tf_op jit(solution)/shard_map/ppermute | solution.py:371
  65.9 1.6 %collective-permute-start.14 = (bf16[48,2048]{1,0:T(8,128)(2,1)S(1)}, bf16[48,2048]{1,0:T(8,128)(2,1)S(1)}, u32[]{:S(2)}, u32[]{:S(2)}) collective-permute-start(bf16[48,2048]{1,0:T(8,128)(2,1)S(1)} %slice.99), channel_id=1, source_target_pairs={{0,2},{1,3},{2,0},{3,1},{4,6},{5,7},{6,4},{7,5},{8,10},{9,11},{10,... | collective-permute-start | bytes 589832 | tf_op jit(solution)/shard_map/ppermute | solution.py:371
  67.5 0.7 collective-permute-start.12
  68.2 1.3 %collective-permute-start.13 = (bf16[48,2048]{1,0:T(8,128)(2,1)S(1)}, bf16[48,2048]{1,0:T(8,128)(2,1)S(1)}, u32[]{:S(2)}, u32[]{:S(2)}) collective-permute-start(bf16[48,2048]{1,0:T(8,128)(2,1)S(1)} %get-tuple-element.61), channel_id=1, source_target_pairs={{0,4},{1,5},{2,6},{3,7},{4,8},{5,9},{6,10},{7,11},{8,12},{9,13},{1... | collective-permute-start | bytes 589832 | tf_op jit(solution)/shard_map/ppermute | solution.py:371
  69.6 3.3 %collective-permute-start.16 = (bf16[48,2048]{1,0:T(8,128)(2,1)S(1)}, bf16[48,2048]{1,0:T(8,128)(2,1)S(1)}, u32[]{:S(2)}, u32[]{:S(2)}) collective-permute-start(bf16[48,2048]{1,0:T(8,128)(2,1)S(1)} %get-tuple-element.65), channel_id=1, source_target_pairs={{0,12},{1,13},{2,14},{3,15},{4,0},{5,1},{6,2},{7,3},{8,4},{9,5},{1... | collective-permute-start | bytes 589832 | tf_op jit(solution)/shard_map/ppermute | solution.py:371
  72.9 1.7 %collective-permute-done.12 = bf16[48,2048]{1,0:T(8,128)(2,1)S(1)} collective-permute-done((bf16[48,2048]{1,0:T(8,128)(2,1)S(1)}, bf16[48,2048]{1,0:T(8,128)(2,1)S(1)}, u32[]{:S(2)}, u32[]{:S(2)}) %collective-permute-start.12) | collective-permute-done | bytes 196640 | tf_op jit(solution)/shard_map/ppermute | solution.py:371
  74.6 1.9 %collective-permute-done.13 = bf16[48,2048]{1,0:T(8,128)(2,1)S(1)} collective-permute-done((bf16[48,2048]{1,0:T(8,128)(2,1)S(1)}, bf16[48,2048]{1,0:T(8,128)(2,1)S(1)}, u32[]{:S(2)}, u32[]{:S(2)}) %collective-permute-start.13) | collective-permute-done | bytes 196640 | tf_op jit(solution)/shard_map/ppermute | solution.py:371
  76.8 2.1 %collective-permute-start.17 = (bf16[48,2048]{1,0:T(8,128)(2,1)S(1)}, bf16[48,2048]{1,0:T(8,128)(2,1)S(1)}, u32[]{:S(2)}, u32[]{:S(2)}) collective-permute-start(bf16[48,2048]{1,0:T(8,128)(2,1)S(1)} %fusion.4), channel_id=1, source_target_pairs={{0,4},{1,5},{2,6},{3,7},{4,8},{5,9},{6,10},{7,11},{8,12},{9,13},{1... | collective-permute-start | bytes 589832 | tf_op jit(solution)/shard_map/ppermute | solution.py:371
  78.9 0.8 collective-permute-start.18
  79.7 0.8 collective-permute-done.11
  80.5 1.8 %collective-permute-done.15 = bf16[48,2048]{1,0:T(8,128)(2,1)S(1)} collective-permute-done((bf16[48,2048]{1,0:T(8,128)(2,1)S(1)}, bf16[48,2048]{1,0:T(8,128)(2,1)S(1)}, u32[]{:S(2)}, u32[]{:S(2)}) %collective-permute-start.15) | collective-permute-done | bytes 196640 | tf_op jit(solution)/shard_map/ppermute | solution.py:371
  82.4 2.2 %collective-permute-done.18 = bf16[48,2048]{1,0:T(8,128)(2,1)S(1)} collective-permute-done((bf16[48,2048]{1,0:T(8,128)(2,1)S(1)}, bf16[48,2048]{1,0:T(8,128)(2,1)S(1)}, u32[]{:S(2)}, u32[]{:S(2)}) %collective-permute-start.18) | collective-permute-done | bytes 196640 | tf_op jit(solution)/shard_map/ppermute | solution.py:371
  84.8 1.0 %fusion = bf16[48,8192]{1,0:T(8,128)(2,1)} fusion(f32[48,2048]{1,0:T(8,128)S(1)} %slice_add_fusion, f32[48,2048]{1,0:T(8,128)S(1)} %slice_add_fusion.1, f32[48,2048]{1,0:T(8,128)S(1)} %fusion.3, f32[48,2048]{1,0:T(8,128)S(1)} %fusion.2, bf16[48,8192]{1,0:T(8,128)(2,1)S(1)} %copy-done.1), kind=kLoop, calls=%fused_computation.2 | loop fusion | flops 2359296 | bytes 3145728 | tf_op jit(solution)/shard_map/convert_element_type | solution.py:403
  (38 shorter events, 2.5 us)
Async XLA Ops:
  0.0 20.1 %collective-permute-start.2 = (bf16[512,8192]{1,0:T(8,128)(2,1)}, bf16[512,8192]{1,0:T(8,128)(2,1)}, u32[]{:S(2)}, u32[]{:S(2)}) collective-permute-start(bf16[512,8192]{1,0:T(8,128)(2,1)} %wa_ref.5), channel_id=1, source_target_pairs={{0,1},{1,0},{2,3},{3,2},{4,5},{5,4},{6,7},{7,6},{8,9},{9,8},{10,11... | collective-permute-start | bytes 25165832 | tf_op jit(solution)/shard_map/ppermute | solution.py:371
  1.3 12.2 %collective-permute-start = (bf16[144,512]{1,0:T(8,128)(2,1)S(1)}, bf16[144,512]{1,0:T(8,128)(2,1)S(1)}, u32[]{:S(2)}, u32[]{:S(2)}) collective-permute-start(bf16[144,512]{1,0:T(8,128)(2,1)S(1)} %rim.1), channel_id=1, source_target_pairs={{0,16},{16,32},{32,48},{48,64},{64,80},{80,96},{96,112},{112,128},... | collective-permute-start | bytes 442376 | tf_op jit(solution)/shard_map/ppermute | solution.py:391
  5.1 8.4 %copy-start = (s32[256]{0:T(256)S(1)}, s32[256]{0:T(256)}, u32[]{:S(2)}) copy-start(s32[256]{0:T(256)} %constant.12.clone.order_ref) | copy-start | bytes 3076
  17.1 3.1 %collective-permute-start.1 = (bf16[384,512]{1,0:T(8,128)(2,1)S(1)}, bf16[384,512]{1,0:T(8,128)(2,1)S(1)}, u32[]{:S(2)}, u32[]{:S(2)}) collective-permute-start(bf16[384,512]{1,0:T(8,128)(2,1)S(1)} %get-tuple-element.37), channel_id=1, source_target_pairs={{0,1},{1,0},{2,3},{3,2},{4,5},{5,4},{6,7},{7,6},{8,9},{9,8},{10,11... | collective-permute-start | bytes 1179656 | tf_op jit(solution)/shard_map/ppermute | solution.py:371
  23.0 25.2 %collective-permute-start.5 = (bf16[192,2560]{1,0:T(8,128)(2,1)S(1)}, bf16[192,2560]{1,0:T(8,128)(2,1)S(1)}, u32[]{:S(2)}, u32[]{:S(2)}) collective-permute-start(bf16[192,2560]{1,0:T(8,128)(2,1)S(1)} %get-tuple-element.43), channel_id=1, source_target_pairs={{0,2},{1,3},{2,0},{3,1},{4,6},{5,7},{6,4},{7,5},{8,10},{9,11},{10,... | collective-permute-start | bytes 2949128 | tf_op jit(solution)/shard_map/ppermute | solution.py:371
  31.9 12.6 %collective-permute-start.3 = (bf16[96,2048]{1,0:T(8,128)(2,1)S(1)}, bf16[96,2048]{1,0:T(8,128)(2,1)S(1)}, u32[]{:S(2)}, u32[]{:S(2)}) collective-permute-start(bf16[96,2048]{1,0:T(8,128)(2,1)S(1)} %get-tuple-element.41), channel_id=1, source_target_pairs={{0,12},{1,13},{2,14},{3,15},{4,0},{5,1},{6,2},{7,3},{8,4},{9,5},{1... | collective-permute-start | bytes 1179656 | tf_op jit(solution)/shard_map/ppermute | solution.py:371
  35.0 13.2 %collective-permute-start.4 = (bf16[96,2048]{1,0:T(8,128)(2,1)S(1)}, bf16[96,2048]{1,0:T(8,128)(2,1)S(1)}, u32[]{:S(2)}, u32[]{:S(2)}) collective-permute-start(bf16[96,2048]{1,0:T(8,128)(2,1)S(1)} %get-tuple-element.42), channel_id=1, source_target_pairs={{0,4},{1,5},{2,6},{3,7},{4,8},{5,9},{6,10},{7,11},{8,12},{9,13},{1... | collective-permute-start | bytes 1179656 | tf_op jit(solution)/shard_map/ppermute | solution.py:371
  35.0 20.6 %collective-permute-start.6 = (bf16[96,2048]{1,0:T(8,128)(2,1)S(1)}, bf16[96,2048]{1,0:T(8,128)(2,1)S(1)}, u32[]{:S(2)}, u32[]{:S(2)}) collective-permute-start(bf16[96,2048]{1,0:T(8,128)(2,1)S(1)} %get-tuple-element.46), channel_id=1, source_target_pairs={{0,4},{1,5},{2,6},{3,7},{4,8},{5,9},{6,10},{7,11},{8,12},{9,13},{1... | collective-permute-start | bytes 1179656 | tf_op jit(solution)/shard_map/ppermute | solution.py:371
  35.6 25.2 %collective-permute-start.9 = (bf16[96,2048]{1,0:T(8,128)(2,1)S(1)}, bf16[96,2048]{1,0:T(8,128)(2,1)S(1)}, u32[]{:S(2)}, u32[]{:S(2)}) collective-permute-start(bf16[96,2048]{1,0:T(8,128)(2,1)S(1)} %get-tuple-element.52), channel_id=1, source_target_pairs={{0,12},{1,13},{2,14},{3,15},{4,0},{5,1},{6,2},{7,3},{8,4},{9,5},{1... | collective-permute-start | bytes 1179656 | tf_op jit(solution)/shard_map/ppermute | solution.py:371
  48.3 12.3 %collective-permute-start.7 = (bf16[96,2048]{1,0:T(8,128)(2,1)S(1)}, bf16[96,2048]{1,0:T(8,128)(2,1)S(1)}, u32[]{:S(2)}, u32[]{:S(2)}) collective-permute-start(bf16[96,2048]{1,0:T(8,128)(2,1)S(1)} %add_convert_fusion.1), channel_id=1, source_target_pairs={{0,12},{1,13},{2,14},{3,15},{4,0},{5,1},{6,2},{7,3},{8,4},{9,5},{1... | collective-permute-start | bytes 1179656 | tf_op jit(solution)/shard_map/ppermute | solution.py:371
  50.8 14.9 %collective-permute-start.10 = (bf16[192,1536]{1,0:T(8,128)(2,1)S(1)}, bf16[192,1536]{1,0:T(8,128)(2,1)S(1)}, u32[]{:S(2)}, u32[]{:S(2)}) collective-permute-start(bf16[192,1536]{1,0:T(8,128)(2,1)S(1)} %get-tuple-element.56), channel_id=1, source_target_pairs={{0,2},{1,3},{2,0},{3,1},{4,6},{5,7},{6,4},{7,5},{8,10},{9,11},{10,... | collective-permute-start | bytes 1769480 | tf_op jit(solution)/shard_map/ppermute | solution.py:371
  52.9 11.6 %collective-permute-start.8 = (bf16[96,2048]{1,0:T(8,128)(2,1)S(1)}, bf16[96,2048]{1,0:T(8,128)(2,1)S(1)}, u32[]{:S(2)}, u32[]{:S(2)}) collective-permute-start(bf16[96,2048]{1,0:T(8,128)(2,1)S(1)} %add_convert_fusion), channel_id=1, source_target_pairs={{0,4},{1,5},{2,6},{3,7},{4,8},{5,9},{6,10},{7,11},{8,12},{9,13},{1... | collective-permute-start | bytes 1179656 | tf_op jit(solution)/shard_map/ppermute | solution.py:371
  65.9 7.0 %collective-permute-start.14 = (bf16[48,2048]{1,0:T(8,128)(2,1)S(1)}, bf16[48,2048]{1,0:T(8,128)(2,1)S(1)}, u32[]{:S(2)}, u32[]{:S(2)}) collective-permute-start(bf16[48,2048]{1,0:T(8,128)(2,1)S(1)} %slice.99), channel_id=1, source_target_pairs={{0,2},{1,3},{2,0},{3,1},{4,6},{5,7},{6,4},{7,5},{8,10},{9,11},{10,... | collective-permute-start | bytes 589832 | tf_op jit(solution)/shard_map/ppermute | solution.py:371
  67.5 7.1 %collective-permute-start.12 = (bf16[48,2048]{1,0:T(8,128)(2,1)S(1)}, bf16[48,2048]{1,0:T(8,128)(2,1)S(1)}, u32[]{:S(2)}, u32[]{:S(2)}) collective-permute-start(bf16[48,2048]{1,0:T(8,128)(2,1)S(1)} %get-tuple-element.60), channel_id=1, source_target_pairs={{0,12},{1,13},{2,14},{3,15},{4,0},{5,1},{6,2},{7,3},{8,4},{9,5},{1... | collective-permute-start | bytes 589832 | tf_op jit(solution)/shard_map/ppermute | solution.py:371
  68.2 8.3 %collective-permute-start.13 = (bf16[48,2048]{1,0:T(8,128)(2,1)S(1)}, bf16[48,2048]{1,0:T(8,128)(2,1)S(1)}, u32[]{:S(2)}, u32[]{:S(2)}) collective-permute-start(bf16[48,2048]{1,0:T(8,128)(2,1)S(1)} %get-tuple-element.61), channel_id=1, source_target_pairs={{0,4},{1,5},{2,6},{3,7},{4,8},{5,9},{6,10},{7,11},{8,12},{9,13},{1... | collective-permute-start | bytes 589832 | tf_op jit(solution)/shard_map/ppermute | solution.py:371
  69.5 11.0 %collective-permute-start.11 = (bf16[48,2048]{1,0:T(8,128)(2,1)S(1)}, bf16[48,2048]{1,0:T(8,128)(2,1)S(1)}, u32[]{:S(2)}, u32[]{:S(2)}) collective-permute-start(bf16[48,2048]{1,0:T(8,128)(2,1)S(1)} %get-tuple-element.59), channel_id=1, source_target_pairs={{0,4},{1,5},{2,6},{3,7},{4,8},{5,9},{6,10},{7,11},{8,12},{9,13},{1... | collective-permute-start | bytes 589832 | tf_op jit(solution)/shard_map/ppermute | solution.py:371
  69.6 15.1 %collective-permute-start.16 = (bf16[48,2048]{1,0:T(8,128)(2,1)S(1)}, bf16[48,2048]{1,0:T(8,128)(2,1)S(1)}, u32[]{:S(2)}, u32[]{:S(2)}) collective-permute-start(bf16[48,2048]{1,0:T(8,128)(2,1)S(1)} %get-tuple-element.65), channel_id=1, source_target_pairs={{0,12},{1,13},{2,14},{3,15},{4,0},{5,1},{6,2},{7,3},{8,4},{9,5},{1... | collective-permute-start | bytes 589832 | tf_op jit(solution)/shard_map/ppermute | solution.py:371
  76.6 5.7 %collective-permute-start.15 = (bf16[48,2048]{1,0:T(8,128)(2,1)S(1)}, bf16[48,2048]{1,0:T(8,128)(2,1)S(1)}, u32[]{:S(2)}, u32[]{:S(2)}) collective-permute-start(bf16[48,2048]{1,0:T(8,128)(2,1)S(1)} %fusion.1), channel_id=1, source_target_pairs={{0,12},{1,13},{2,14},{3,15},{4,0},{5,1},{6,2},{7,3},{8,4},{9,5},{1... | collective-permute-start | bytes 589832 | tf_op jit(solution)/shard_map/ppermute | solution.py:371
  76.8 7.9 %collective-permute-start.17 = (bf16[48,2048]{1,0:T(8,128)(2,1)S(1)}, bf16[48,2048]{1,0:T(8,128)(2,1)S(1)}, u32[]{:S(2)}, u32[]{:S(2)}) collective-permute-start(bf16[48,2048]{1,0:T(8,128)(2,1)S(1)} %fusion.4), channel_id=1, source_target_pairs={{0,4},{1,5},{2,6},{3,7},{4,8},{5,9},{6,10},{7,11},{8,12},{9,13},{1... | collective-permute-start | bytes 589832 | tf_op jit(solution)/shard_map/ppermute | solution.py:371
  78.9 5.9 %copy-start.1 = (bf16[48,8192]{1,0:T(8,128)(2,1)S(1)}, bf16[48,8192]{1,0:T(8,128)(2,1)}, u32[]{:S(2)}) copy-start(bf16[48,8192]{1,0:T(8,128)(2,1)} %param.18) | copy-start | bytes 2359300
  78.9 5.8 %collective-permute-start.18 = (bf16[48,2048]{1,0:T(8,128)(2,1)S(1)}, bf16[48,2048]{1,0:T(8,128)(2,1)S(1)}, u32[]{:S(2)}, u32[]{:S(2)}) collective-permute-start(bf16[48,2048]{1,0:T(8,128)(2,1)S(1)} %slice.98), channel_id=1, source_target_pairs={{0,2},{1,3},{2,0},{3,1},{4,6},{5,7},{6,4},{7,5},{8,10},{9,11},{10,... | collective-permute-start | bytes 589832 | tf_op jit(solution)/shard_map/ppermute | solution.py:371

commit v6 on v5

--- a/solution.py
+++ b/solution.py
@@ -378,7 +378,7 @@
     return total
 
 
-X_FIRST = (2560, 1536)
+X_FIRST = (2304, 1280)
 
 
 def body(queries, keys_in, values_in, short_taps, filters, skip_gain, out_weight, residual):
@@ -402,17 +402,18 @@
     def narrow(array):
         return array.astype(jnp.bfloat16)
 
-    edge = sum(X_FIRST)
-    a0_part = project_own(keep, out_weight, 0, X_FIRST[0], X_FIRST[0] // 2)
-    a0_keep, a0_give = project_rest(theirs, weight_pair, a0_part, 0, X_FIRST[0] // 2, by_x)
+    y_first = width - sum(X_FIRST)
+    tile = y_first // 4
+    a0_part = project_own(keep, out_weight, y_first, X_FIRST[0], tile)
+    a0_keep, a0_give = project_rest(theirs, weight_pair, a0_part, y_first, tile, by_x)
     a0_got = send(a0_give, dx=1)
     left = lax.optimization_barrier((keep, a0_keep))[0]
-    tile = (width - edge) // 4
-    b_all = project(left, theirs, out_weight, weight_pair, edge, width - edge, tile, by_y, halves=True)
+    b_all = project(left, theirs, out_weight, weight_pair, 0, y_first, tile, by_y, halves=True)
     b0, b1 = b_all[:N_Y], b_all[N_Y:]
     left = lax.optimization_barrier((keep, b0[0]))[0]
+    last = width - X_FIRST[1]
     a1_keep, a1_give = project(
-        left, theirs, out_weight, weight_pair, X_FIRST[0], X_FIRST[1], math.gcd(*X_FIRST), by_x
+        left, theirs, out_weight, weight_pair, last, X_FIRST[1], math.gcd(last, X_FIRST[1]), by_x
     )
 
     b1_far = send(b1[2], dy=1)
@@ -433,28 +434,27 @@
         for s in range(N_Y)
     ]
     low_send, high_send = [narrow(part) for part in low], [narrow(part) for part in high]
-    low_send, high_send = lax.optimization_barrier((low_send, high_send))
+    low_send, high_send, b0_up, b1_down = lax.optimization_barrier((low_send, high_send, b0_up, b1_down))
     low_far = send(low_send[2], dy=-1)
     high_far = send(high_send[2], dy=1)
 
     b0_sum, b1_sum = add(b0[0], b0_up, b0_down), add(b1[0], b1_up, b1_down)
     b0_give, b1_give = narrow(b0_sum[piece:]), narrow(b1_sum[piece:])
-    b0_give, b1_give, low_send[1], high_send[3] = lax.optimization_barrier((b0_give, b1_give, low_send[1], high_send[3]))
     b0_got = send(b0_give, dx=1)
     low_up = send(low_send[1], dy=1)
     high_down = send(high_send[3], dy=-1)
 
-    low_far, high_far, b0_got, b1_give = lax.optimization_barrier((low_far, high_far, b0_got, b1_give))
+    low_far, high_far, b1_give = lax.optimization_barrier((low_far, high_far, b1_give))
     low_down = send(narrow(add(low[3], low_far)), dy=-1)
     high_up = send(narrow(add(high[1], high_far)), dy=1)
     b1_got = send(b1_give, dx=1)
 
     summed = jnp.concatenate(
         [
+            add(b0_sum[:piece], b0_got),
+            add(b1_sum[:piece], b1_got),
             add(low[0], low_up, low_down),
             add(high[0], high_down, high_up),
-            add(b0_sum[:piece], b0_got),
-            add(b1_sum[:piece], b1_got),
         ],
         axis=1,
     )

time: 86.2 us -> 83 us (0.963)
  starting transfers between devices: 26.9 us -> 23.6 us
  Pallas kernels: 24.9 us -> 26.3 us
  waiting for transfers between devices: 31.3 us -> 30.1 us
    ppermute x18, starting transfers between devices: 23.1 us -> 19.8 us  [send(): return lax.ppermute(array, 'tp', moved(**step))]
    pallas_call x4, Pallas kernels: 16.1 us -> 17.5 us  [project_call(): pl.pallas_call(kernel, grid=(count // tile,), out_shape=out_shape, in_spe...]
    ppermute x18, waiting for transfers between devices: 26.9 us -> 25.7 us  [send(): return lax.ppermute(array, 'tp', moved(**step))]
  transfers between devices with their start and end apart: 19 -> 19, of which waited for: 12 -> 11; matrix products, arithmetic and copies ran while one was open for 1% -> 2% of each run, Pallas kernels for 26% -> 28%
where the time goes in v6:
time: 83 us; the launch traced here: 82.7 us
  waiting for transfers between devices  30.1 us (36%)
  Pallas kernels  26.3 us (32%)
  starting transfers between devices  23.6 us (28%)
  other arithmetic  2.15 us (3%)
    ppermute x18, waiting for transfers between devices, send(): return lax.ppermute(array, 'tp', moved(**step))  25.7 us
    ppermute x18, starting transfers between devices, send(): return lax.ppermute(array, 'tp', moved(**step))  19.8 us
    pallas_call x4, Pallas kernels, project_call(): pl.pallas_call(kernel, grid=(count // tile,), out_shape=out_shape, in_spe...  17.5 us
    ppermute x1, waiting for transfers between devices, body(): halo = lax.ppermute(rim, 'ctx', [(i, i + 1) for i in range(peers - 1)])  4.4 us
    pallas_call x1, Pallas kernels, gate_late(): pl.pallas_call(functools.partial(late_kernel, EARLY), grid=(channels // W...  3.95 us
    ppermute x1, starting transfers between devices, body(): halo = lax.ppermute(rim, 'ctx', [(i, i + 1) for i in range(peers - 1)])  3.83 us
    pallas_call x1, Pallas kernels, gate_early(): pl.pallas_call(early_kernel, grid_spec=pltpu.PrefetchScalarGridSpec(num_s...  3.58 us
  transfers between devices with their start and end apart: 19, of which 11 were waited for; matrix products, arithmetic and copies ran while one was open for 2% of the time, Pallas kernels for 28%

profile of v6, /device:TPU:4, one launch (start us, length us, event | category | flops | bytes accessed | tf_op | source)
XLA Modules:
  0.0 82.7 jit_solution(756918648876858508)
XLA Ops:
  0.0 1.2 %rim.1 = bf16[144,512]{1,0:T(8,128)(2,1)S(1)} custom-call(bf16[768,512]{1,0:T(8,128)(2,1)} %q_ref.5, bf16[768,512]{1,0:T(8,128)(2,1)} %k_ref.5, bf16[768,512]{1,0:T(8,128)(2,1)} %v_ref.5, bf16[3,512]{1,0:T(4,128)(2,1)} %taps_ref.5), custom_call_target="tpu_custom_call" | custom-call | flops 1000000000 | bytes 1000000 | tf_op jit(solution)/shard_map/rim/pallas_call | solution.py:160
  1.3 3.8 %collective-permute-start = (bf16[144,512]{1,0:T(8,128)(2,1)S(1)}, bf16[144,512]{1,0:T(8,128)(2,1)S(1)}, u32[]{:S(2)}, u32[]{:S(2)}) collective-permute-start(bf16[144,512]{1,0:T(8,128)(2,1)S(1)} %rim.1), channel_id=1, source_target_pairs={{0,16},{16,32},{32,48},{48,64},{64,80},{80,96},{96,112},{112,128},... | collective-permute-start | bytes 442376 | tf_op jit(solution)/shard_map/ppermute | solution.py:391
  5.1 4.0 %gate_late.1.late_ref = bf16[512,512]{1,0:T(8,128)(2,1)S(1)} custom-call(bf16[768,512]{1,0:T(8,128)(2,1)} %q_ref.5, bf16[768,512]{1,0:T(8,128)(2,1)} %k_ref.5, bf16[768,512]{1,0:T(8,128)(2,1)} %v_ref.5, bf16[3,512]{1,0:T(4,128)(2,1)} %taps_ref.5, bf16[512,128]{1,0:T(8,128)(2,1)} %filt_ref.3, f32[1,512]{1,0:T(1,128)} %bitcast.2, ...), custom_call_target="tpu_custom_call" | custom-call | flops 4000000000 | bytes 3000000 | tf_op jit(solution)/shard_map/gate_late/pallas_call | solution.py:190
  9.1 4.4 %collective-permute-done.halo_ref = bf16[144,512]{1,0:T(8,128)(2,1)S(1)} collective-permute-done((bf16[144,512]{1,0:T(8,128)(2,1)S(1)}, bf16[144,512]{1,0:T(8,128)(2,1)S(1)}, u32[]{:S(2)}, u32[]{:S(2)}) %collective-permute-start) | collective-permute-done | bytes 147488 | tf_op jit(solution)/shard_map/ppermute | solution.py:391
  13.5 3.6 %gate_early.1 = (bf16[384,512]{1,0:T(8,128)(2,1)S(1)}, bf16[384,512]{1,0:T(8,128)(2,1)S(1)}) custom-call(s32[1]{0:T(128)} %bitcast.place_ref, s32[256]{0:T(256)S(1)} %copy-done, bf16[768,512]{1,0:T(8,128)(2,1)} %q_ref.5, bf16[768,512]{1,0:T(8,128)(2,1)} %k_ref.5, bf16[768,512]{1,0:T(8,128)(2,1)} %v_ref.5, ...), custom_call_target="tpu_custom_call" | custom-call | flops 2000000000 | bytes 3000000 | tf_op jit(solution)/shard_map/gate_early/pallas_call | solution.py:206
  17.2 2.9 %project_own.1.part_ref = f32[384,2304]{1,0:T(8,128)S(1)} custom-call(bf16[384,512]{1,0:T(8,128)(2,1)S(1)} %get-tuple-element.43.a_ref, bf16[512,8192]{1,0:T(8,128)(2,1)} %wa_ref.5), custom_call_target="tpu_custom_call" | custom-call | flops 905969664 | bytes 4128768 | tf_op jit(solution)/shard_map/project_own/pallas_call | solution.py:275
  20.1 2.8 %project_rest.1 = (bf16[192,2304]{1,0:T(8,128)(2,1)S(1)}, bf16[192,2304]{1,0:T(8,128)(2,1)S(1)}) custom-call(bf16[384,512]{1,0:T(8,128)(2,1)S(1)} %collective-permute-done.1.b_ref, bf16[512,8192]{1,0:T(8,128)(2,1)} %collective-permute-done.2.wb_ref, f32[384,2304]{1,0:T(8,128)S(1)} %project_own.1.part_ref), custom_call_target="tpu_custom_call" | custom-call | flops 905969664 | bytes 4128768 | tf_op jit(solution)/shard_map/project_rest/pallas_call | solution.py:275
  22.9 2.2 %collective-permute-start.5 = (bf16[192,2304]{1,0:T(8,128)(2,1)S(1)}, bf16[192,2304]{1,0:T(8,128)(2,1)S(1)}, u32[]{:S(2)}, u32[]{:S(2)}) collective-permute-start(bf16[192,2304]{1,0:T(8,128)(2,1)S(1)} %get-tuple-element.41), channel_id=1, source_target_pairs={{0,2},{1,3},{2,0},{3,1},{4,6},{5,7},{6,4},{7,5},{8,10},{9,11},{10,... | collective-permute-start | bytes 2654216 | tf_op jit(solution)/shard_map/ppermute | solution.py:371
  25.0 7.5 %project.2 = (bf16[96,2304]{1,0:T(8,128)(2,1)S(1)}, bf16[96,2304]{1,0:T(8,128)(2,1)S(1)}, bf16[96,2304]{1,0:T(8,128)(2,1)S(1)}, bf16[96,2304]{1,0:T(8,128)(2,1)S...) custom-call(bf16[384,512]{1,0:T(8,128)(2,1)S(1)} %get-tuple-element., ...), custom_call_target="tpu_custom_call" | custom-call | flops 3623878656 | bytes 12976128 | tf_op jit(solution)/shard_map/project/pallas_call | solution.py:275
  32.6 3.1 %collective-permute-start.3 = (bf16[96,2304]{1,0:T(8,128)(2,1)S(1)}, bf16[96,2304]{1,0:T(8,128)(2,1)S(1)}, u32[]{:S(2)}, u32[]{:S(2)}) collective-permute-start(bf16[96,2304]{1,0:T(8,128)(2,1)S(1)} %get-tuple-element.39), channel_id=1, source_target_pairs={{0,12},{1,13},{2,14},{3,15},{4,0},{5,1},{6,2},{7,3},{8,4},{9,5},{1... | collective-permute-start | bytes 1327112 | tf_op jit(solution)/shard_map/ppermute | solution.py:371
  35.7 0.6 collective-permute-start.7
  36.3 2.7 %collective-permute-start.8 = (bf16[96,2304]{1,0:T(8,128)(2,1)S(1)}, bf16[96,2304]{1,0:T(8,128)(2,1)S(1)}, u32[]{:S(2)}, u32[]{:S(2)}) collective-permute-start(bf16[96,2304]{1,0:T(8,128)(2,1)S(1)} %get-tuple-element.48), channel_id=1, source_target_pairs={{0,12},{1,13},{2,14},{3,15},{4,0},{5,1},{6,2},{7,3},{8,4},{9,5},{1... | collective-permute-start | bytes 1327112 | tf_op jit(solution)/shard_map/ppermute | solution.py:371
  39.0 4.3 %project.3 = (bf16[192,1280]{1,0:T(8,128)(2,1)S(1)}, bf16[192,1280]{1,0:T(8,128)(2,1)S(1)}) custom-call(bf16[384,512]{1,0:T(8,128)(2,1)S(1)} %get-tuple-element.43.a_ref, bf16[384,512]{1,0:T(8,128)(2,1)S(1)} %collective-permute-done.1.b_ref, bf16[512,8192]{1,0:T(8,128)(2,1)} %wa_ref.5, bf16[512,8192]{1,0:T(8,128)(2,1)} %collective-permute-done.2.wb_ref), custom_call_target="tpu_custom_call" | custom-call | flops 1006632960 | bytes 3604480 | tf_op jit(solution)/shard_map/project/pallas_call | solution.py:275
  43.3 2.1 %collective-permute-done.5 = bf16[192,2304]{1,0:T(8,128)(2,1)S(1)} collective-permute-done((bf16[192,2304]{1,0:T(8,128)(2,1)S(1)}, bf16[192,2304]{1,0:T(8,128)(2,1)S(1)}, u32[]{:S(2)}, u32[]{:S(2)}) %collective-permute-start.5) | collective-permute-done | bytes 884768 | tf_op jit(solution)/shard_map/ppermute | solution.py:371
  45.3 0.9 %collective-permute-done.3 = bf16[96,2304]{1,0:T(8,128)(2,1)S(1)} collective-permute-done((bf16[96,2304]{1,0:T(8,128)(2,1)S(1)}, bf16[96,2304]{1,0:T(8,128)(2,1)S(1)}, u32[]{:S(2)}, u32[]{:S(2)}) %collective-permute-start.3) | collective-permute-done | bytes 442400 | tf_op jit(solution)/shard_map/ppermute | solution.py:371
  46.2 3.7 %collective-permute-done.4 = bf16[96,2304]{1,0:T(8,128)(2,1)S(1)} collective-permute-done((bf16[96,2304]{1,0:T(8,128)(2,1)S(1)}, bf16[96,2304]{1,0:T(8,128)(2,1)S(1)}, u32[]{:S(2)}, u32[]{:S(2)}) %collective-permute-start.4) | collective-permute-done | bytes 442400 | tf_op jit(solution)/shard_map/ppermute | solution.py:371
  50.3 2.1 %collective-permute-start.11 = (bf16[96,2304]{1,0:T(8,128)(2,1)S(1)}, bf16[96,2304]{1,0:T(8,128)(2,1)S(1)}, u32[]{:S(2)}, u32[]{:S(2)}) collective-permute-start(bf16[96,2304]{1,0:T(8,128)(2,1)S(1)} %add_convert_fusion), channel_id=1, source_target_pairs={{0,4},{1,5},{2,6},{3,7},{4,8},{5,9},{6,10},{7,11},{8,12},{9,13},{1... | collective-permute-start | bytes 1327112 | tf_op jit(solution)/shard_map/ppermute | solution.py:371
  52.3 0.2 fusion.6
  52.6 10.3 %collective-permute-done.6 = bf16[192,1280]{1,0:T(8,128)(2,1)S(1)} collective-permute-done((bf16[192,1280]{1,0:T(8,128)(2,1)S(1)}, bf16[192,1280]{1,0:T(8,128)(2,1)S(1)}, u32[]{:S(2)}, u32[]{:S(2)}) %collective-permute-start.6) | collective-permute-done | bytes 491552 | tf_op jit(solution)/shard_map/ppermute | solution.py:371
  63.1 1.9 %collective-permute-start.12 = (bf16[48,1792]{1,0:T(8,128)(2,1)S(1)}, bf16[48,1792]{1,0:T(8,128)(2,1)S(1)}, u32[]{:S(2)}, u32[]{:S(2)}) collective-permute-start(bf16[48,1792]{1,0:T(8,128)(2,1)S(1)} %get-tuple-element.56), channel_id=1, source_target_pairs={{0,12},{1,13},{2,14},{3,15},{4,0},{5,1},{6,2},{7,3},{8,4},{9,5},{1... | collective-permute-start | bytes 516104 | tf_op jit(solution)/shard_map/ppermute | solution.py:371
  65.0 0.2 collective-permute-start.13
  65.2 0.6 collective-permute-start.15
  65.8 3.1 %collective-permute-start.17 = (bf16[48,1792]{1,0:T(8,128)(2,1)S(1)}, bf16[48,1792]{1,0:T(8,128)(2,1)S(1)}, u32[]{:S(2)}, u32[]{:S(2)}) collective-permute-start(bf16[48,1792]{1,0:T(8,128)(2,1)S(1)} %get-tuple-element.61), channel_id=1, source_target_pairs={{0,12},{1,13},{2,14},{3,15},{4,0},{5,1},{6,2},{7,3},{8,4},{9,5},{1... | collective-permute-start | bytes 516104 | tf_op jit(solution)/shard_map/ppermute | solution.py:371
  69.3 0.7 collective-permute-start.10
  70.1 3.3 %collective-permute-done.13 = bf16[48,1792]{1,0:T(8,128)(2,1)S(1)} collective-permute-done((bf16[48,1792]{1,0:T(8,128)(2,1)S(1)}, bf16[48,1792]{1,0:T(8,128)(2,1)S(1)}, u32[]{:S(2)}, u32[]{:S(2)}) %collective-permute-start.13) | collective-permute-done | bytes 172064 | tf_op jit(solution)/shard_map/ppermute | solution.py:371
  73.6 2.1 %collective-permute-start.18 = (bf16[48,1792]{1,0:T(8,128)(2,1)S(1)}, bf16[48,1792]{1,0:T(8,128)(2,1)S(1)}, u32[]{:S(2)}, u32[]{:S(2)}) collective-permute-start(bf16[48,1792]{1,0:T(8,128)(2,1)S(1)} %fusion.4), channel_id=1, source_target_pairs={{0,4},{1,5},{2,6},{3,7},{4,8},{5,9},{6,10},{7,11},{8,12},{9,13},{1... | collective-permute-start | bytes 516104 | tf_op jit(solution)/shard_map/ppermute | solution.py:371
  75.7 0.3 collective-permute-start.14
  76.0 0.4 collective-permute-done.15
  76.4 2.5 %collective-permute-done.16 = bf16[48,1792]{1,0:T(8,128)(2,1)S(1)} collective-permute-done((bf16[48,1792]{1,0:T(8,128)(2,1)S(1)}, bf16[48,1792]{1,0:T(8,128)(2,1)S(1)}, u32[]{:S(2)}, u32[]{:S(2)}) %collective-permute-start.16) | collective-permute-done | bytes 172064 | tf_op jit(solution)/shard_map/ppermute | solution.py:371
  79.0 1.3 %collective-permute-done.18 = bf16[48,1792]{1,0:T(8,128)(2,1)S(1)} collective-permute-done((bf16[48,1792]{1,0:T(8,128)(2,1)S(1)}, bf16[48,1792]{1,0:T(8,128)(2,1)S(1)}, u32[]{:S(2)}, u32[]{:S(2)}) %collective-permute-start.18) | collective-permute-done | bytes 172064 | tf_op jit(solution)/shard_map/ppermute | solution.py:371
  80.3 1.3 %collective-permute-done.14 = bf16[48,2304]{1,0:T(8,128)(2,1)S(1)} collective-permute-done((bf16[48,2304]{1,0:T(8,128)(2,1)S(1)}, bf16[48,2304]{1,0:T(8,128)(2,1)S(1)}, u32[]{:S(2)}, u32[]{:S(2)}) %collective-permute-start.14) | collective-permute-done | bytes 221216 | tf_op jit(solution)/shard_map/ppermute | solution.py:371
  81.6 1.0 %fusion = bf16[48,8192]{1,0:T(8,128)(2,1)} fusion(f32[48,1792]{1,0:T(8,128)S(1)} %fusion.3, f32[48,1792]{1,0:T(8,128)S(1)} %fusion.2, f32[48,2304]{1,0:T(8,128)S(1)} %slice_add_fusion, f32[48,2304]{1,0:T(8,128)S(1)} %slice_add_fusion.1, bf16[48,8192]{1,0:T(8,128)(2,1)S(1)} %copy-done.1), kind=kLoop, calls=%fused_computation.2 | loop fusion | flops 2359296 | bytes 3145728 | tf_op jit(solution)/shard_map/convert_element_type | solution.py:403
  (38 shorter events, 1.5 us)
Async XLA Ops:
  0.0 20.1 %collective-permute-start.2 = (bf16[512,8192]{1,0:T(8,128)(2,1)}, bf16[512,8192]{1,0:T(8,128)(2,1)}, u32[]{:S(2)}, u32[]{:S(2)}) collective-permute-start(bf16[512,8192]{1,0:T(8,128)(2,1)} %wa_ref.5), channel_id=1, source_target_pairs={{0,1},{1,0},{2,3},{3,2},{4,5},{5,4},{6,7},{7,6},{8,9},{9,8},{10,11... | collective-permute-start | bytes 25165832 | tf_op jit(solution)/shard_map/ppermute | solution.py:371
  1.3 12.2 %collective-permute-start = (bf16[144,512]{1,0:T(8,128)(2,1)S(1)}, bf16[144,512]{1,0:T(8,128)(2,1)S(1)}, u32[]{:S(2)}, u32[]{:S(2)}) collective-permute-start(bf16[144,512]{1,0:T(8,128)(2,1)S(1)} %rim.1), channel_id=1, source_target_pairs={{0,16},{16,32},{32,48},{48,64},{64,80},{80,96},{96,112},{112,128},... | collective-permute-start | bytes 442376 | tf_op jit(solution)/shard_map/ppermute | solution.py:391
  5.1 8.4 %copy-start = (s32[256]{0:T(256)S(1)}, s32[256]{0:T(256)}, u32[]{:S(2)}) copy-start(s32[256]{0:T(256)} %constant.12.clone.order_ref) | copy-start | bytes 3076
  17.1 3.0 %collective-permute-start.1 = (bf16[384,512]{1,0:T(8,128)(2,1)S(1)}, bf16[384,512]{1,0:T(8,128)(2,1)S(1)}, u32[]{:S(2)}, u32[]{:S(2)}) collective-permute-start(bf16[384,512]{1,0:T(8,128)(2,1)S(1)} %get-tuple-element.35), channel_id=1, source_target_pairs={{0,1},{1,0},{2,3},{3,2},{4,5},{5,4},{6,7},{7,6},{8,9},{9,8},{10,11... | collective-permute-start | bytes 1179656 | tf_op jit(solution)/shard_map/ppermute | solution.py:371
  22.9 22.5 %collective-permute-start.5 = (bf16[192,2304]{1,0:T(8,128)(2,1)S(1)}, bf16[192,2304]{1,0:T(8,128)(2,1)S(1)}, u32[]{:S(2)}, u32[]{:S(2)}) collective-permute-start(bf16[192,2304]{1,0:T(8,128)(2,1)S(1)} %get-tuple-element.41), channel_id=1, source_target_pairs={{0,2},{1,3},{2,0},{3,1},{4,6},{5,7},{6,4},{7,5},{8,10},{9,11},{10,... | collective-permute-start | bytes 2654216 | tf_op jit(solution)/shard_map/ppermute | solution.py:371
  32.6 13.6 %collective-permute-start.3 = (bf16[96,2304]{1,0:T(8,128)(2,1)S(1)}, bf16[96,2304]{1,0:T(8,128)(2,1)S(1)}, u32[]{:S(2)}, u32[]{:S(2)}) collective-permute-start(bf16[96,2304]{1,0:T(8,128)(2,1)S(1)} %get-tuple-element.39), channel_id=1, source_target_pairs={{0,12},{1,13},{2,14},{3,15},{4,0},{5,1},{6,2},{7,3},{8,4},{9,5},{1... | collective-permute-start | bytes 1327112 | tf_op jit(solution)/shard_map/ppermute | solution.py:371
  35.7 14.3 %collective-permute-start.4 = (bf16[96,2304]{1,0:T(8,128)(2,1)S(1)}, bf16[96,2304]{1,0:T(8,128)(2,1)S(1)}, u32[]{:S(2)}, u32[]{:S(2)}) collective-permute-start(bf16[96,2304]{1,0:T(8,128)(2,1)S(1)} %get-tuple-element.40), channel_id=1, source_target_pairs={{0,4},{1,5},{2,6},{3,7},{4,8},{5,9},{6,10},{7,11},{8,12},{9,13},{1... | collective-permute-start | bytes 1327112 | tf_op jit(solution)/shard_map/ppermute | solution.py:371
  35.7 27.4 %collective-permute-start.7 = (bf16[96,2304]{1,0:T(8,128)(2,1)S(1)}, bf16[96,2304]{1,0:T(8,128)(2,1)S(1)}, u32[]{:S(2)}, u32[]{:S(2)}) collective-permute-start(bf16[96,2304]{1,0:T(8,128)(2,1)S(1)} %get-tuple-element.47), channel_id=1, source_target_pairs={{0,4},{1,5},{2,6},{3,7},{4,8},{5,9},{6,10},{7,11},{8,12},{9,13},{1... | collective-permute-start | bytes 1327112 | tf_op jit(solution)/shard_map/ppermute | solution.py:371
  36.3 26.8 %collective-permute-start.8 = (bf16[96,2304]{1,0:T(8,128)(2,1)S(1)}, bf16[96,2304]{1,0:T(8,128)(2,1)S(1)}, u32[]{:S(2)}, u32[]{:S(2)}) collective-permute-start(bf16[96,2304]{1,0:T(8,128)(2,1)S(1)} %get-tuple-element.48), channel_id=1, source_target_pairs={{0,12},{1,13},{2,14},{3,15},{4,0},{5,1},{6,2},{7,3},{8,4},{9,5},{1... | collective-permute-start | bytes 1327112 | tf_op jit(solution)/shard_map/ppermute | solution.py:371
  50.1 15.7 %collective-permute-start.9 = (bf16[96,2304]{1,0:T(8,128)(2,1)S(1)}, bf16[96,2304]{1,0:T(8,128)(2,1)S(1)}, u32[]{:S(2)}, u32[]{:S(2)}) collective-permute-start(bf16[96,2304]{1,0:T(8,128)(2,1)S(1)} %add_convert_fusion.1), channel_id=1, source_target_pairs={{0,12},{1,13},{2,14},{3,15},{4,0},{5,1},{6,2},{7,3},{8,4},{9,5},{1... | collective-permute-start | bytes 1327112 | tf_op jit(solution)/shard_map/ppermute | solution.py:371
  50.3 18.8 %collective-permute-start.11 = (bf16[96,2304]{1,0:T(8,128)(2,1)S(1)}, bf16[96,2304]{1,0:T(8,128)(2,1)S(1)}, u32[]{:S(2)}, u32[]{:S(2)}) collective-permute-start(bf16[96,2304]{1,0:T(8,128)(2,1)S(1)} %add_convert_fusion), channel_id=1, source_target_pairs={{0,4},{1,5},{2,6},{3,7},{4,8},{5,9},{6,10},{7,11},{8,12},{9,13},{1... | collective-permute-start | bytes 1327112 | tf_op jit(solution)/shard_map/ppermute | solution.py:371
  52.3 10.6 %collective-permute-start.6 = (bf16[192,1280]{1,0:T(8,128)(2,1)S(1)}, bf16[192,1280]{1,0:T(8,128)(2,1)S(1)}, u32[]{:S(2)}, u32[]{:S(2)}) collective-permute-start(bf16[192,1280]{1,0:T(8,128)(2,1)S(1)} %get-tuple-element.46), channel_id=1, source_target_pairs={{0,2},{1,3},{2,0},{3,1},{4,6},{5,7},{6,4},{7,5},{8,10},{9,11},{10,... | collective-permute-start | bytes 1474568 | tf_op jit(solution)/shard_map/ppermute | solution.py:371
  63.1 7.0 %collective-permute-start.12 = (bf16[48,1792]{1,0:T(8,128)(2,1)S(1)}, bf16[48,1792]{1,0:T(8,128)(2,1)S(1)}, u32[]{:S(2)}, u32[]{:S(2)}) collective-permute-start(bf16[48,1792]{1,0:T(8,128)(2,1)S(1)} %get-tuple-element.56), channel_id=1, source_target_pairs={{0,12},{1,13},{2,14},{3,15},{4,0},{5,1},{6,2},{7,3},{8,4},{9,5},{1... | collective-permute-start | bytes 516104 | tf_op jit(solution)/shard_map/ppermute | solution.py:371
  65.0 8.4 %collective-permute-start.13 = (bf16[48,1792]{1,0:T(8,128)(2,1)S(1)}, bf16[48,1792]{1,0:T(8,128)(2,1)S(1)}, u32[]{:S(2)}, u32[]{:S(2)}) collective-permute-start(bf16[48,1792]{1,0:T(8,128)(2,1)S(1)} %get-tuple-element.57), channel_id=1, source_target_pairs={{0,4},{1,5},{2,6},{3,7},{4,8},{5,9},{6,10},{7,11},{8,12},{9,13},{1... | collective-permute-start | bytes 516104 | tf_op jit(solution)/shard_map/ppermute | solution.py:371
  65.2 11.2 %collective-permute-start.15 = (bf16[48,1792]{1,0:T(8,128)(2,1)S(1)}, bf16[48,1792]{1,0:T(8,128)(2,1)S(1)}, u32[]{:S(2)}, u32[]{:S(2)}) collective-permute-start(bf16[48,1792]{1,0:T(8,128)(2,1)S(1)} %get-tuple-element.59), channel_id=1, source_target_pairs={{0,4},{1,5},{2,6},{3,7},{4,8},{5,9},{6,10},{7,11},{8,12},{9,13},{1... | collective-permute-start | bytes 516104 | tf_op jit(solution)/shard_map/ppermute | solution.py:371
  65.8 13.2 %collective-permute-start.17 = (bf16[48,1792]{1,0:T(8,128)(2,1)S(1)}, bf16[48,1792]{1,0:T(8,128)(2,1)S(1)}, u32[]{:S(2)}, u32[]{:S(2)}) collective-permute-start(bf16[48,1792]{1,0:T(8,128)(2,1)S(1)} %get-tuple-element.61), channel_id=1, source_target_pairs={{0,12},{1,13},{2,14},{3,15},{4,0},{5,1},{6,2},{7,3},{8,4},{9,5},{1... | collective-permute-start | bytes 516104 | tf_op jit(solution)/shard_map/ppermute | solution.py:371
  69.3 6.4 %collective-permute-start.10 = (bf16[48,2304]{1,0:T(8,128)(2,1)S(1)}, bf16[48,2304]{1,0:T(8,128)(2,1)S(1)}, u32[]{:S(2)}, u32[]{:S(2)}) collective-permute-start(bf16[48,2304]{1,0:T(8,128)(2,1)S(1)} %slice.99), channel_id=1, source_target_pairs={{0,2},{1,3},{2,0},{3,1},{4,6},{5,7},{6,4},{7,5},{8,10},{9,11},{10,... | collective-permute-start | bytes 663560 | tf_op jit(solution)/shard_map/ppermute | solution.py:371
  73.4 5.5 %collective-permute-start.16 = (bf16[48,1792]{1,0:T(8,128)(2,1)S(1)}, bf16[48,1792]{1,0:T(8,128)(2,1)S(1)}, u32[]{:S(2)}, u32[]{:S(2)}) collective-permute-start(bf16[48,1792]{1,0:T(8,128)(2,1)S(1)} %fusion.1), channel_id=1, source_target_pairs={{0,12},{1,13},{2,14},{3,15},{4,0},{5,1},{6,2},{7,3},{8,4},{9,5},{1... | collective-permute-start | bytes 516104 | tf_op jit(solution)/shard_map/ppermute | solution.py:371
  73.6 6.7 %collective-permute-start.18 = (bf16[48,1792]{1,0:T(8,128)(2,1)S(1)}, bf16[48,1792]{1,0:T(8,128)(2,1)S(1)}, u32[]{:S(2)}, u32[]{:S(2)}) collective-permute-start(bf16[48,1792]{1,0:T(8,128)(2,1)S(1)} %fusion.4), channel_id=1, source_target_pairs={{0,4},{1,5},{2,6},{3,7},{4,8},{5,9},{6,10},{7,11},{8,12},{9,13},{1... | collective-permute-start | bytes 516104 | tf_op jit(solution)/shard_map/ppermute | solution.py:371
  75.7 5.9 %collective-permute-start.14 = (bf16[48,2304]{1,0:T(8,128)(2,1)S(1)}, bf16[48,2304]{1,0:T(8,128)(2,1)S(1)}, u32[]{:S(2)}, u32[]{:S(2)}) collective-permute-start(bf16[48,2304]{1,0:T(8,128)(2,1)S(1)} %slice.98), channel_id=1, source_target_pairs={{0,2},{1,3},{2,0},{3,1},{4,6},{5,7},{6,4},{7,5},{8,10},{9,11},{10,... | collective-permute-start | bytes 663560 | tf_op jit(solution)/shard_map/ppermute | solution.py:371
  76.0 5.6 %copy-start.1 = (bf16[48,8192]{1,0:T(8,128)(2,1)S(1)}, bf16[48,8192]{1,0:T(8,128)(2,1)}, u32[]{:S(2)}) copy-start(bf16[48,8192]{1,0:T(8,128)(2,1)} %param.18) | copy-start | bytes 2359300

commit v7 on v6

--- a/solution.py
+++ b/solution.py
@@ -408,7 +408,7 @@
     a0_keep, a0_give = project_rest(theirs, weight_pair, a0_part, y_first, tile, by_x)
     a0_got = send(a0_give, dx=1)
     left = lax.optimization_barrier((keep, a0_keep))[0]
-    b_all = project(left, theirs, out_weight, weight_pair, 0, y_first, tile, by_y, halves=True)
+    b_all = project(left, theirs, out_weight, weight_pair, 0, y_first, y_first // 2, by_y, halves=True)
     b0, b1 = b_all[:N_Y], b_all[N_Y:]
     left = lax.optimization_barrier((keep, b0[0]))[0]
     last = width - X_FIRST[1]
@@ -441,20 +441,17 @@
     b0_sum, b1_sum = add(b0[0], b0_up, b0_down), add(b1[0], b1_up, b1_down)
     b0_give, b1_give = narrow(b0_sum[piece:]), narrow(b1_sum[piece:])
     b0_got = send(b0_give, dx=1)
-    low_up = send(low_send[1], dy=1)
-    high_down = send(high_send[3], dy=-1)
-
-    low_far, high_far, b1_give = lax.optimization_barrier((low_far, high_far, b1_give))
-    low_down = send(narrow(add(low[3], low_far)), dy=-1)
-    high_up = send(narrow(add(high[1], high_far)), dy=1)
-    b1_got = send(b1_give, dx=1)
+
+    low_far, high_far = lax.optimization_barrier((low_far, high_far))
+    down = send(jnp.concatenate([narrow(add(low[3], low_far)), high_send[3]], axis=1), dy=-1)
+    up = send(jnp.concatenate([low_send[1], narrow(add(high[1], high_far))], axis=1), dy=1)
+    b1_got = send(lax.optimization_barrier((b1_give, low_far, high_far, b0_got))[0], dx=1)
 
     summed = jnp.concatenate(
         [
             add(b0_sum[:piece], b0_got),
             add(b1_sum[:piece], b1_got),
-            add(low[0], low_up, low_down),
-            add(high[0], high_down, high_up),
+            add(jnp.concatenate([low[0], high[0]], axis=1), up, down),
         ],
         axis=1,
     )

time: 83 us -> 82.3 us (level)
  starting transfers between devices: 23.6 us -> 21 us
  waiting for transfers between devices: 30.1 us -> 32.5 us
    ppermute x18 -> x16, starting transfers between devices: 19.8 us -> 17.1 us  [send(): return lax.ppermute(array, 'tp', moved(**step))]
    ppermute x18 -> x16, waiting for transfers between devices: 25.7 us -> 28.1 us  [send(): return lax.ppermute(array, 'tp', moved(**step))]
  transfers between devices with their start and end apart: 19 -> 17, of which waited for: 11 -> 9; matrix products, arithmetic and copies ran while one was open for 2% -> 2% of each run, Pallas kernels for 28% -> 28%
where the time goes in v7:
time: 82.3 us; the launch traced here: 81.7 us
  waiting for transfers between devices  32.5 us (39%)
  Pallas kernels  25.5 us (31%)
  starting transfers between devices  21 us (26%)
  other arithmetic  2.21 us (3%)
    ppermute x16, waiting for transfers between devices, send(): return lax.ppermute(array, 'tp', moved(**step))  28.1 us
    ppermute x16, starting transfers between devices, send(): return lax.ppermute(array, 'tp', moved(**step))  17.1 us
    pallas_call x4, Pallas kernels, project_call(): pl.pallas_call(kernel, grid=(count // tile,), out_shape=out_shape, in_spe...  16.7 us
    ppermute x1, waiting for transfers between devices, body(): halo = lax.ppermute(rim, 'ctx', [(i, i + 1) for i in range(peers - 1)])  4.4 us
    pallas_call x1, Pallas kernels, gate_late(): pl.pallas_call(functools.partial(late_kernel, EARLY), grid=(channels // W...  3.95 us
    ppermute x1, starting transfers between devices, body(): halo = lax.ppermute(rim, 'ctx', [(i, i + 1) for i in range(peers - 1)])  3.83 us
    pallas_call x1, Pallas kernels, gate_early(): pl.pallas_call(early_kernel, grid_spec=pltpu.PrefetchScalarGridSpec(num_s...  3.58 us
  transfers between devices with their start and end apart: 17, of which 9 were waited for; matrix products, arithmetic and copies ran while one was open for 2% of the time, Pallas kernels for 28%

profile of v7, /device:TPU:4, one launch (start us, length us, event | category | flops | bytes accessed | tf_op | source)
XLA Modules:
  0.0 81.7 jit_solution(8266805657566076176)
XLA Ops:
  0.0 1.2 %rim.1 = bf16[144,512]{1,0:T(8,128)(2,1)S(1)} custom-call(bf16[768,512]{1,0:T(8,128)(2,1)} %q_ref.5, bf16[768,512]{1,0:T(8,128)(2,1)} %k_ref.5, bf16[768,512]{1,0:T(8,128)(2,1)} %v_ref.5, bf16[3,512]{1,0:T(4,128)(2,1)} %taps_ref.5), custom_call_target="tpu_custom_call" | custom-call | flops 1000000000 | bytes 1000000 | tf_op jit(solution)/shard_map/rim/pallas_call | solution.py:160
  1.3 3.8 %collective-permute-start = (bf16[144,512]{1,0:T(8,128)(2,1)S(1)}, bf16[144,512]{1,0:T(8,128)(2,1)S(1)}, u32[]{:S(2)}, u32[]{:S(2)}) collective-permute-start(bf16[144,512]{1,0:T(8,128)(2,1)S(1)} %rim.1), channel_id=1, source_target_pairs={{0,16},{16,32},{32,48},{48,64},{64,80},{80,96},{96,112},{112,128},... | collective-permute-start | bytes 442376 | tf_op jit(solution)/shard_map/ppermute | solution.py:391
  5.1 4.0 %gate_late.1.late_ref = bf16[512,512]{1,0:T(8,128)(2,1)S(1)} custom-call(bf16[768,512]{1,0:T(8,128)(2,1)} %q_ref.5, bf16[768,512]{1,0:T(8,128)(2,1)} %k_ref.5, bf16[768,512]{1,0:T(8,128)(2,1)} %v_ref.5, bf16[3,512]{1,0:T(4,128)(2,1)} %taps_ref.5, bf16[512,128]{1,0:T(8,128)(2,1)} %filt_ref.3, f32[1,512]{1,0:T(1,128)} %bitcast.2, ...), custom_call_target="tpu_custom_call" | custom-call | flops 4000000000 | bytes 3000000 | tf_op jit(solution)/shard_map/gate_late/pallas_call | solution.py:190
  9.1 4.4 %collective-permute-done.halo_ref = bf16[144,512]{1,0:T(8,128)(2,1)S(1)} collective-permute-done((bf16[144,512]{1,0:T(8,128)(2,1)S(1)}, bf16[144,512]{1,0:T(8,128)(2,1)S(1)}, u32[]{:S(2)}, u32[]{:S(2)}) %collective-permute-start) | collective-permute-done | bytes 147488 | tf_op jit(solution)/shard_map/ppermute | solution.py:391
  13.5 3.6 %gate_early.1 = (bf16[384,512]{1,0:T(8,128)(2,1)S(1)}, bf16[384,512]{1,0:T(8,128)(2,1)S(1)}) custom-call(s32[1]{0:T(128)} %bitcast.place_ref, s32[256]{0:T(256)S(1)} %copy-done, bf16[768,512]{1,0:T(8,128)(2,1)} %q_ref.5, bf16[768,512]{1,0:T(8,128)(2,1)} %k_ref.5, bf16[768,512]{1,0:T(8,128)(2,1)} %v_ref.5, ...), custom_call_target="tpu_custom_call" | custom-call | flops 2000000000 | bytes 3000000 | tf_op jit(solution)/shard_map/gate_early/pallas_call | solution.py:206
  17.1 0.1 collective-permute-start.1
  17.2 2.9 %project_own.1.part_ref = f32[384,2304]{1,0:T(8,128)S(1)} custom-call(bf16[384,512]{1,0:T(8,128)(2,1)S(1)} %get-tuple-element.43.a_ref, bf16[512,8192]{1,0:T(8,128)(2,1)} %wa_ref.5), custom_call_target="tpu_custom_call" | custom-call | flops 905969664 | bytes 4128768 | tf_op jit(solution)/shard_map/project_own/pallas_call | solution.py:275
  20.1 2.8 %project_rest.1 = (bf16[192,2304]{1,0:T(8,128)(2,1)S(1)}, bf16[192,2304]{1,0:T(8,128)(2,1)S(1)}) custom-call(bf16[384,512]{1,0:T(8,128)(2,1)S(1)} %collective-permute-done.1.b_ref, bf16[512,8192]{1,0:T(8,128)(2,1)} %collective-permute-done.2.wb_ref, f32[384,2304]{1,0:T(8,128)S(1)} %project_own.1.part_ref), custom_call_target="tpu_custom_call" | custom-call | flops 905969664 | bytes 4128768 | tf_op jit(solution)/shard_map/project_rest/pallas_call | solution.py:275
  22.9 2.2 %collective-permute-start.5 = (bf16[192,2304]{1,0:T(8,128)(2,1)S(1)}, bf16[192,2304]{1,0:T(8,128)(2,1)S(1)}, u32[]{:S(2)}, u32[]{:S(2)}) collective-permute-start(bf16[192,2304]{1,0:T(8,128)(2,1)S(1)} %get-tuple-element.41), channel_id=1, source_target_pairs={{0,2},{1,3},{2,0},{3,1},{4,6},{5,7},{6,4},{7,5},{8,10},{9,11},{10,... | collective-permute-start | bytes 2654216 | tf_op jit(solution)/shard_map/ppermute | solution.py:371
  25.0 6.8 %project.2 = (bf16[96,2304]{1,0:T(8,128)(2,1)S(1)}, bf16[96,2304]{1,0:T(8,128)(2,1)S(1)}, bf16[96,2304]{1,0:T(8,128)(2,1)S(1)}, bf16[96,2304]{1,0:T(8,128)(2,1)S...) custom-call(bf16[384,512]{1,0:T(8,128)(2,1)S(1)} %get-tuple-element., ...), custom_call_target="tpu_custom_call" | custom-call | flops 3623878656 | bytes 12976128 | tf_op jit(solution)/shard_map/project/pallas_call | solution.py:275
  31.8 3.1 %collective-permute-start.3 = (bf16[96,2304]{1,0:T(8,128)(2,1)S(1)}, bf16[96,2304]{1,0:T(8,128)(2,1)S(1)}, u32[]{:S(2)}, u32[]{:S(2)}) collective-permute-start(bf16[96,2304]{1,0:T(8,128)(2,1)S(1)} %get-tuple-element.39), channel_id=1, source_target_pairs={{0,12},{1,13},{2,14},{3,15},{4,0},{5,1},{6,2},{7,3},{8,4},{9,5},{1... | collective-permute-start | bytes 1327112 | tf_op jit(solution)/shard_map/ppermute | solution.py:371
  34.9 0.6 collective-permute-start.7
  35.5 2.7 %collective-permute-start.8 = (bf16[96,2304]{1,0:T(8,128)(2,1)S(1)}, bf16[96,2304]{1,0:T(8,128)(2,1)S(1)}, u32[]{:S(2)}, u32[]{:S(2)}) collective-permute-start(bf16[96,2304]{1,0:T(8,128)(2,1)S(1)} %get-tuple-element.48), channel_id=1, source_target_pairs={{0,12},{1,13},{2,14},{3,15},{4,0},{5,1},{6,2},{7,3},{8,4},{9,5},{1... | collective-permute-start | bytes 1327112 | tf_op jit(solution)/shard_map/ppermute | solution.py:371
  38.2 4.3 %project.3 = (bf16[192,1280]{1,0:T(8,128)(2,1)S(1)}, bf16[192,1280]{1,0:T(8,128)(2,1)S(1)}) custom-call(bf16[384,512]{1,0:T(8,128)(2,1)S(1)} %get-tuple-element.43.a_ref, bf16[384,512]{1,0:T(8,128)(2,1)S(1)} %collective-permute-done.1.b_ref, bf16[512,8192]{1,0:T(8,128)(2,1)} %wa_ref.5, bf16[512,8192]{1,0:T(8,128)(2,1)} %collective-permute-done.2.wb_ref), custom_call_target="tpu_custom_call" | custom-call | flops 1006632960 | bytes 3604480 | tf_op jit(solution)/shard_map/project/pallas_call | solution.py:275
  42.5 2.9 %collective-permute-done.3 = bf16[96,2304]{1,0:T(8,128)(2,1)S(1)} collective-permute-done((bf16[96,2304]{1,0:T(8,128)(2,1)S(1)}, bf16[96,2304]{1,0:T(8,128)(2,1)S(1)}, u32[]{:S(2)}, u32[]{:S(2)}) %collective-permute-start.3) | collective-permute-done | bytes 442400 | tf_op jit(solution)/shard_map/ppermute | solution.py:371
  45.4 3.7 %collective-permute-done.4 = bf16[96,2304]{1,0:T(8,128)(2,1)S(1)} collective-permute-done((bf16[96,2304]{1,0:T(8,128)(2,1)S(1)}, bf16[96,2304]{1,0:T(8,128)(2,1)S(1)}, u32[]{:S(2)}, u32[]{:S(2)}) %collective-permute-start.4) | collective-permute-done | bytes 442400 | tf_op jit(solution)/shard_map/ppermute | solution.py:371
  49.2 0.2 fusion.5
  49.4 0.1 add_convert_fusion.1
  49.6 0.1 add_convert_fusion
  49.7 2.3 %collective-permute-start.11 = (bf16[96,2304]{1,0:T(8,128)(2,1)S(1)}, bf16[96,2304]{1,0:T(8,128)(2,1)S(1)}, u32[]{:S(2)}, u32[]{:S(2)}) collective-permute-start(bf16[96,2304]{1,0:T(8,128)(2,1)S(1)} %add_convert_fusion), channel_id=1, source_target_pairs={{0,4},{1,5},{2,6},{3,7},{4,8},{5,9},{6,10},{7,11},{8,12},{9,13},{1... | collective-permute-start | bytes 1327112 | tf_op jit(solution)/shard_map/ppermute | solution.py:371
  52.1 10.5 %collective-permute-done.6 = bf16[192,1280]{1,0:T(8,128)(2,1)S(1)} collective-permute-done((bf16[192,1280]{1,0:T(8,128)(2,1)S(1)}, bf16[192,1280]{1,0:T(8,128)(2,1)S(1)}, u32[]{:S(2)}, u32[]{:S(2)}) %collective-permute-start.6) | collective-permute-done | bytes 491552 | tf_op jit(solution)/shard_map/ppermute | solution.py:371
  62.6 0.1 fusion.4
  62.8 2.4 %collective-permute-start.12 = (bf16[48,1792]{1,0:T(8,128)(2,1)S(1)}, bf16[48,1792]{1,0:T(8,128)(2,1)S(1)}, u32[]{:S(2)}, u32[]{:S(2)}) collective-permute-start(bf16[48,1792]{1,0:T(8,128)(2,1)S(1)} %get-tuple-element.56), channel_id=1, source_target_pairs={{0,12},{1,13},{2,14},{3,15},{4,0},{5,1},{6,2},{7,3},{8,4},{9,5},{1... | collective-permute-start | bytes 516104 | tf_op jit(solution)/shard_map/ppermute | solution.py:371
  65.2 0.1 convert_add_fusion.3
  65.3 2.5 %collective-permute-done.11 = bf16[96,2304]{1,0:T(8,128)(2,1)S(1)} collective-permute-done((bf16[96,2304]{1,0:T(8,128)(2,1)S(1)}, bf16[96,2304]{1,0:T(8,128)(2,1)S(1)}, u32[]{:S(2)}, u32[]{:S(2)}) %collective-permute-start.11) | collective-permute-done | bytes 442400 | tf_op jit(solution)/shard_map/ppermute | solution.py:371
  67.8 0.1 convert_add_fusion.2
  68.3 3.5 %collective-permute-done.13 = bf16[48,1792]{1,0:T(8,128)(2,1)S(1)} collective-permute-done((bf16[48,1792]{1,0:T(8,128)(2,1)S(1)}, bf16[48,1792]{1,0:T(8,128)(2,1)S(1)}, u32[]{:S(2)}, u32[]{:S(2)}) %collective-permute-start.13) | collective-permute-done | bytes 172064 | tf_op jit(solution)/shard_map/ppermute | solution.py:371
  72.0 2.1 %collective-permute-start.15 = (bf16[48,3584]{1,0:T(8,128)(2,1)S(1)}, bf16[48,3584]{1,0:T(8,128)(2,1)S(1)}, u32[]{:S(2)}, u32[]{:S(2)}) collective-permute-start(bf16[48,3584]{1,0:T(8,128)(2,1)S(1)} %pad_maximum_fusion), channel_id=1, source_target_pairs={{0,4},{1,5},{2,6},{3,7},{4,8},{5,9},{6,10},{7,11},{8,12},{9,13},{1... | collective-permute-start | bytes 1032200 | tf_op jit(solution)/shard_map/ppermute | solution.py:371
  74.1 1.5 %collective-permute-start.14 = (bf16[48,2304]{1,0:T(8,128)(2,1)S(1)}, bf16[48,2304]{1,0:T(8,128)(2,1)S(1)}, u32[]{:S(2)}, u32[]{:S(2)}) collective-permute-start(bf16[48,2304]{1,0:T(8,128)(2,1)S(1)} %slice.92), channel_id=1, source_target_pairs={{0,2},{1,3},{2,0},{3,1},{4,6},{5,7},{6,4},{7,5},{8,10},{9,11},{10,... | collective-permute-start | bytes 663560 | tf_op jit(solution)/shard_map/ppermute | solution.py:371
  75.7 4.3 %collective-permute-done.14 = bf16[48,2304]{1,0:T(8,128)(2,1)S(1)} collective-permute-done((bf16[48,2304]{1,0:T(8,128)(2,1)S(1)}, bf16[48,2304]{1,0:T(8,128)(2,1)S(1)}, u32[]{:S(2)}, u32[]{:S(2)}) %collective-permute-start.14) | collective-permute-done | bytes 221216 | tf_op jit(solution)/shard_map/ppermute | solution.py:371
  80.1 0.5 collective-permute-done.15
  80.7 1.1 %fusion = bf16[48,8192]{1,0:T(8,128)(2,1)} fusion(f32[48,3584]{1,0:T(8,128)S(1)} %fusion.1, f32[48,2304]{1,0:T(8,128)S(1)} %slice_add_fusion, f32[48,2304]{1,0:T(8,128)S(1)} %slice_add_fusion.1, bf16[48,8192]{1,0:T(8,128)(2,1)S(1)} %copy-done.1), kind=kLoop, calls=%fused_computation.2 | loop fusion | flops 1966080 | bytes 3145728 | tf_op jit(solution)/shard_map/convert_element_type | solution.py:403
  (36 shorter events, 0.9 us)
Async XLA Ops:
  0.0 20.1 %collective-permute-start.2 = (bf16[512,8192]{1,0:T(8,128)(2,1)}, bf16[512,8192]{1,0:T(8,128)(2,1)}, u32[]{:S(2)}, u32[]{:S(2)}) collective-permute-start(bf16[512,8192]{1,0:T(8,128)(2,1)} %wa_ref.5), channel_id=1, source_target_pairs={{0,1},{1,0},{2,3},{3,2},{4,5},{5,4},{6,7},{7,6},{8,9},{9,8},{10,11... | collective-permute-start | bytes 25165832 | tf_op jit(solution)/shard_map/ppermute | solution.py:371
  1.3 12.2 %collective-permute-start = (bf16[144,512]{1,0:T(8,128)(2,1)S(1)}, bf16[144,512]{1,0:T(8,128)(2,1)S(1)}, u32[]{:S(2)}, u32[]{:S(2)}) collective-permute-start(bf16[144,512]{1,0:T(8,128)(2,1)S(1)} %rim.1), channel_id=1, source_target_pairs={{0,16},{16,32},{32,48},{48,64},{64,80},{80,96},{96,112},{112,128},... | collective-permute-start | bytes 442376 | tf_op jit(solution)/shard_map/ppermute | solution.py:391
  5.1 8.4 %copy-start = (s32[256]{0:T(256)S(1)}, s32[256]{0:T(256)}, u32[]{:S(2)}) copy-start(s32[256]{0:T(256)} %constant.12.clone.order_ref) | copy-start | bytes 3076
  17.1 3.0 %collective-permute-start.1 = (bf16[384,512]{1,0:T(8,128)(2,1)S(1)}, bf16[384,512]{1,0:T(8,128)(2,1)S(1)}, u32[]{:S(2)}, u32[]{:S(2)}) collective-permute-start(bf16[384,512]{1,0:T(8,128)(2,1)S(1)} %get-tuple-element.35), channel_id=1, source_target_pairs={{0,1},{1,0},{2,3},{3,2},{4,5},{5,4},{6,7},{7,6},{8,9},{9,8},{10,11... | collective-permute-start | bytes 1179656 | tf_op jit(solution)/shard_map/ppermute | solution.py:371
  22.9 26.3 %collective-permute-start.5 = (bf16[192,2304]{1,0:T(8,128)(2,1)S(1)}, bf16[192,2304]{1,0:T(8,128)(2,1)S(1)}, u32[]{:S(2)}, u32[]{:S(2)}) collective-permute-start(bf16[192,2304]{1,0:T(8,128)(2,1)S(1)} %get-tuple-element.41), channel_id=1, source_target_pairs={{0,2},{1,3},{2,0},{3,1},{4,6},{5,7},{6,4},{7,5},{8,10},{9,11},{10,... | collective-permute-start | bytes 2654216 | tf_op jit(solution)/shard_map/ppermute | solution.py:371
  31.8 13.6 %collective-permute-start.3 = (bf16[96,2304]{1,0:T(8,128)(2,1)S(1)}, bf16[96,2304]{1,0:T(8,128)(2,1)S(1)}, u32[]{:S(2)}, u32[]{:S(2)}) collective-permute-start(bf16[96,2304]{1,0:T(8,128)(2,1)S(1)} %get-tuple-element.39), channel_id=1, source_target_pairs={{0,12},{1,13},{2,14},{3,15},{4,0},{5,1},{6,2},{7,3},{8,4},{9,5},{1... | collective-permute-start | bytes 1327112 | tf_op jit(solution)/shard_map/ppermute | solution.py:371
  34.9 14.3 %collective-permute-start.4 = (bf16[96,2304]{1,0:T(8,128)(2,1)S(1)}, bf16[96,2304]{1,0:T(8,128)(2,1)S(1)}, u32[]{:S(2)}, u32[]{:S(2)}) collective-permute-start(bf16[96,2304]{1,0:T(8,128)(2,1)S(1)} %get-tuple-element.40), channel_id=1, source_target_pairs={{0,4},{1,5},{2,6},{3,7},{4,8},{5,9},{6,10},{7,11},{8,12},{9,13},{1... | collective-permute-start | bytes 1327112 | tf_op jit(solution)/shard_map/ppermute | solution.py:371
  34.9 27.9 %collective-permute-start.7 = (bf16[96,2304]{1,0:T(8,128)(2,1)S(1)}, bf16[96,2304]{1,0:T(8,128)(2,1)S(1)}, u32[]{:S(2)}, u32[]{:S(2)}) collective-permute-start(bf16[96,2304]{1,0:T(8,128)(2,1)S(1)} %get-tuple-element.47), channel_id=1, source_target_pairs={{0,4},{1,5},{2,6},{3,7},{4,8},{5,9},{6,10},{7,11},{8,12},{9,13},{1... | collective-permute-start | bytes 1327112 | tf_op jit(solution)/shard_map/ppermute | solution.py:371
  35.5 27.3 %collective-permute-start.8 = (bf16[96,2304]{1,0:T(8,128)(2,1)S(1)}, bf16[96,2304]{1,0:T(8,128)(2,1)S(1)}, u32[]{:S(2)}, u32[]{:S(2)}) collective-permute-start(bf16[96,2304]{1,0:T(8,128)(2,1)S(1)} %get-tuple-element.48), channel_id=1, source_target_pairs={{0,12},{1,13},{2,14},{3,15},{4,0},{5,1},{6,2},{7,3},{8,4},{9,5},{1... | collective-permute-start | bytes 1327112 | tf_op jit(solution)/shard_map/ppermute | solution.py:371
  49.5 15.6 %collective-permute-start.9 = (bf16[96,2304]{1,0:T(8,128)(2,1)S(1)}, bf16[96,2304]{1,0:T(8,128)(2,1)S(1)}, u32[]{:S(2)}, u32[]{:S(2)}) collective-permute-start(bf16[96,2304]{1,0:T(8,128)(2,1)S(1)} %add_convert_fusion.1), channel_id=1, source_target_pairs={{0,12},{1,13},{2,14},{3,15},{4,0},{5,1},{6,2},{7,3},{8,4},{9,5},{1... | collective-permute-start | bytes 1327112 | tf_op jit(solution)/shard_map/ppermute | solution.py:371
  49.7 18.1 %collective-permute-start.11 = (bf16[96,2304]{1,0:T(8,128)(2,1)S(1)}, bf16[96,2304]{1,0:T(8,128)(2,1)S(1)}, u32[]{:S(2)}, u32[]{:S(2)}) collective-permute-start(bf16[96,2304]{1,0:T(8,128)(2,1)S(1)} %add_convert_fusion), channel_id=1, source_target_pairs={{0,4},{1,5},{2,6},{3,7},{4,8},{5,9},{6,10},{7,11},{8,12},{9,13},{1... | collective-permute-start | bytes 1327112 | tf_op jit(solution)/shard_map/ppermute | solution.py:371
  52.0 10.6 %collective-permute-start.6 = (bf16[192,1280]{1,0:T(8,128)(2,1)S(1)}, bf16[192,1280]{1,0:T(8,128)(2,1)S(1)}, u32[]{:S(2)}, u32[]{:S(2)}) collective-permute-start(bf16[192,1280]{1,0:T(8,128)(2,1)S(1)} %get-tuple-element.46), channel_id=1, source_target_pairs={{0,2},{1,3},{2,0},{3,1},{4,6},{5,7},{6,4},{7,5},{8,10},{9,11},{10,... | collective-permute-start | bytes 1474568 | tf_op jit(solution)/shard_map/ppermute | solution.py:371
  62.8 5.5 %collective-permute-start.12 = (bf16[48,1792]{1,0:T(8,128)(2,1)S(1)}, bf16[48,1792]{1,0:T(8,128)(2,1)S(1)}, u32[]{:S(2)}, u32[]{:S(2)}) collective-permute-start(bf16[48,1792]{1,0:T(8,128)(2,1)S(1)} %get-tuple-element.56), channel_id=1, source_target_pairs={{0,12},{1,13},{2,14},{3,15},{4,0},{5,1},{6,2},{7,3},{8,4},{9,5},{1... | collective-permute-start | bytes 516104 | tf_op jit(solution)/shard_map/ppermute | solution.py:371
  65.2 6.6 %collective-permute-start.13 = (bf16[48,1792]{1,0:T(8,128)(2,1)S(1)}, bf16[48,1792]{1,0:T(8,128)(2,1)S(1)}, u32[]{:S(2)}, u32[]{:S(2)}) collective-permute-start(bf16[48,1792]{1,0:T(8,128)(2,1)S(1)} %get-tuple-element.57), channel_id=1, source_target_pairs={{0,4},{1,5},{2,6},{3,7},{4,8},{5,9},{6,10},{7,11},{8,12},{9,13},{1... | collective-permute-start | bytes 516104 | tf_op jit(solution)/shard_map/ppermute | solution.py:371
  68.1 6.0 %collective-permute-start.10 = (bf16[48,2304]{1,0:T(8,128)(2,1)S(1)}, bf16[48,2304]{1,0:T(8,128)(2,1)S(1)}, u32[]{:S(2)}, u32[]{:S(2)}) collective-permute-start(bf16[48,2304]{1,0:T(8,128)(2,1)S(1)} %slice.93), channel_id=1, source_target_pairs={{0,2},{1,3},{2,0},{3,1},{4,6},{5,7},{6,4},{7,5},{8,10},{9,11},{10,... | collective-permute-start | bytes 663560 | tf_op jit(solution)/shard_map/ppermute | solution.py:371
  71.8 8.2 %collective-permute-start.16 = (bf16[48,3584]{1,0:T(8,128)(2,1)S(1)}, bf16[48,3584]{1,0:T(8,128)(2,1)S(1)}, u32[]{:S(2)}, u32[]{:S(2)}) collective-permute-start(bf16[48,3584]{1,0:T(8,128)(2,1)S(1)} %pad_maximum_fusion.1), channel_id=1, source_target_pairs={{0,12},{1,13},{2,14},{3,15},{4,0},{5,1},{6,2},{7,3},{8,4},{9,5},{1... | collective-permute-start | bytes 1032200 | tf_op jit(solution)/shard_map/ppermute | solution.py:371
  72.0 8.5 %collective-permute-start.15 = (bf16[48,3584]{1,0:T(8,128)(2,1)S(1)}, bf16[48,3584]{1,0:T(8,128)(2,1)S(1)}, u32[]{:S(2)}, u32[]{:S(2)}) collective-permute-start(bf16[48,3584]{1,0:T(8,128)(2,1)S(1)} %pad_maximum_fusion), channel_id=1, source_target_pairs={{0,4},{1,5},{2,6},{3,7},{4,8},{5,9},{6,10},{7,11},{8,12},{9,13},{1... | collective-permute-start | bytes 1032200 | tf_op jit(solution)/shard_map/ppermute | solution.py:371
  74.1 5.9 %collective-permute-start.14 = (bf16[48,2304]{1,0:T(8,128)(2,1)S(1)}, bf16[48,2304]{1,0:T(8,128)(2,1)S(1)}, u32[]{:S(2)}, u32[]{:S(2)}) collective-permute-start(bf16[48,2304]{1,0:T(8,128)(2,1)S(1)} %slice.92), channel_id=1, source_target_pairs={{0,2},{1,3},{2,0},{3,1},{4,6},{5,7},{6,4},{7,5},{8,10},{9,11},{10,... | collective-permute-start | bytes 663560 | tf_op jit(solution)/shard_map/ppermute | solution.py:371
  75.7 5.0 %copy-start.1 = (bf16[48,8192]{1,0:T(8,128)(2,1)S(1)}, bf16[48,8192]{1,0:T(8,128)(2,1)}, u32[]{:S(2)}) copy-start(bf16[48,8192]{1,0:T(8,128)(2,1)} %param.18) | copy-start | bytes 2359300

commit v8 on v7

--- a/solution.py
+++ b/solution.py
@@ -75,11 +75,13 @@
     out_ref[BLK:] = packed.astype(jnp.bfloat16)
 
 
-def late_kernel(first, q_ref, k_ref, v_ref, taps_ref, filt_ref, skip_ref, f_ref, g_ref, out_ref, prod_ref):
+def late_kernel(first, q_ref, k_ref, v_ref, taps_ref, filt_ref, skip_ref, f_ref, g_ref, out_ref, spec_ref, prod_ref):
     blocks = q_ref.shape[0] // BLK
     taps = taps_ref[...].astype(jnp.float32)
     skip = skip_ref[...]
     h_re, h_im = spectrum(f_ref, filt_ref)
+    spec_ref[:BLK] = h_re
+    spec_ref[BLK:] = h_im
     for b in range(first - 1, blocks):
         at = (b - first + 1) * BLK
         prod = short_filter(window(k_ref, b), taps) * short_filter(window(v_ref, b), taps)
@@ -92,7 +94,7 @@
 
 
 def early_kernel(
-    place_ref, order_ref, q_ref, k_ref, v_ref, halo_ref, late_ref, taps_ref, filt_ref, skip_ref, f_ref, g_ref,
+    place_ref, order_ref, q_ref, k_ref, v_ref, halo_ref, late_ref, spec_ref, taps_ref, skip_ref, f_ref, g_ref,
     keep_ref, give_ref, prod_ref, gated_ref,
 ):
     blocks = q_ref.shape[0] // BLK
@@ -105,7 +107,7 @@
             return jnp.concatenate([pltpu.roll(rim, turn, 0), ref[:BLK].astype(jnp.float32)], axis=0)
         return window(ref, b)
 
-    h_re, h_im = spectrum(f_ref, filt_ref)
+    h_re, h_im = spec_ref[:BLK], spec_ref[BLK:]
     prod_ref[:BLK] = halo_ref[:BLK]
     for b in range(blocks):
         prod = short_filter(rows_of(k_ref, b, 12), taps) * short_filter(rows_of(v_ref, b, 10), taps)
@@ -146,8 +148,8 @@
     return pltpu.with_memory_space_constraint(array, pltpu.HBM)
 
 
-def column_block(rows, index=0):
-    return pl.BlockSpec((rows, WIDTH), lambda i, *_: (index, i))
+def column_block(rows, index=0, width=WIDTH):
+    return pl.BlockSpec((rows, width), lambda i, *_: (index, i))
 
 
 def whole(shape):
@@ -190,9 +192,12 @@
     return pl.pallas_call(
         functools.partial(late_kernel, EARLY),
         grid=(channels // WIDTH,),
-        out_shape=jax.ShapeDtypeStruct((out_rows, channels), jnp.bfloat16),
+        out_shape=[
+            jax.ShapeDtypeStruct((out_rows, channels), jnp.bfloat16),
+            jax.ShapeDtypeStruct((2 * BLK, channels), jnp.float32),
+        ],
         in_specs=[column_block(rows)] * 3 + parameter_specs(short_taps, filters, tables),
-        out_specs=column_block(out_rows),
+        out_specs=[column_block(out_rows), column_block(2 * BLK)],
         scratch_shapes=[pltpu.VMEM((out_rows + BLK, WIDTH), jnp.bfloat16)],
         compiler_params=pltpu.CompilerParams(vmem_limit_bytes=VMEM_LIMIT),
         cost_estimate=pl.CostEstimate(flops=4 * 10**9, bytes_accessed=3 * 10**6, transcendentals=0),
@@ -200,21 +205,23 @@
     )(*map(stay, (queries, keys_in, values_in, short_taps, filters, skip_gain, *tables)))
 
 
-def gate_early(place, queries, keys_in, values_in, halo, late, short_taps, filters, skip_gain, tables):
+def gate_early(place, queries, keys_in, values_in, halo, late, spec, short_taps, skip_gain, tables):
     rows, channels = queries.shape
     half = jax.ShapeDtypeStruct((rows // 2, channels), jnp.bfloat16)
     return pl.pallas_call(
         early_kernel,
         grid_spec=pltpu.PrefetchScalarGridSpec(
             num_scalar_prefetch=2,
-            grid=(channels // WIDTH,),
-            in_specs=[column_block(EARLY * BLK)] * 3
-            + [column_block(halo.shape[0]), column_block(late.shape[0])]
-            + parameter_specs(short_taps, filters, tables),
-            out_specs=[column_block(rows // 2)] * 2,
+            grid=(1,),
+            in_specs=[
+                column_block(n, 0, channels)
+                for n in [EARLY * BLK] * 3 + [halo.shape[0], late.shape[0], spec.shape[0], short_taps.shape[0], 1]
+            ]
+            + [whole(table.shape) for table in tables],
+            out_specs=[column_block(rows // 2, 0, channels)] * 2,
             scratch_shapes=[
-                pltpu.VMEM(((EARLY + 1) * BLK, WIDTH), jnp.bfloat16),
-                pltpu.VMEM((rows, WIDTH), jnp.bfloat16),
+                pltpu.VMEM(((EARLY + 1) * BLK, channels), jnp.bfloat16),
+                pltpu.VMEM((rows, channels), jnp.bfloat16),
             ],
         ),
         out_shape=[half, half],
@@ -227,7 +234,8 @@
         *map(stay, (queries, keys_in, values_in)),
         halo,
         late,
-        *map(stay, (short_taps, filters, skip_gain, *tables)),
+        spec,
+        *map(stay, (short_taps, skip_gain, *tables)),
     )
 
 
@@ -390,9 +398,9 @@
     rim = make_rim(queries, keys_in, values_in, short_taps)
     halo = lax.ppermute(rim, "ctx", [(i, i + 1) for i in range(peers - 1)])
     parameters = (short_taps, filters, skip_gain[None, :], transform_tables(filters.shape[1]))
-    late = gate_late(queries, keys_in, values_in, *parameters)
+    late, spec = gate_late(queries, keys_in, values_in, *parameters)
     place = lax.axis_index("tp").astype(jnp.int32)[None]
-    keep, give = gate_early(place, queries, keys_in, values_in, halo, late, *parameters)
+    keep, give = gate_early(place, queries, keys_in, values_in, halo, late, spec, short_taps, *parameters[2:])
     theirs = send(give, dc=1)
 
     half = rows // (2 * N_C)

time: 82.3 us -> 85.8 us (1.043)
  starting transfers between devices: 21 us -> 23.8 us
    ppermute x16, starting transfers between devices: 17.1 us -> 20 us  [send(): return lax.ppermute(array, 'tp', moved(**step))]
  transfers between devices with their start and end apart: 17 -> 17, of which waited for: 9 -> 8; matrix products, arithmetic and copies ran while one was open for 2% -> 1% of each run, Pallas kernels for 28% -> 26%
where the time goes in v8:
time: 85.8 us; the launch traced here: 85 us
  waiting for transfers between devices  33.2 us (39%)
  Pallas kernels  25.3 us (29%)
  starting transfers between devices  23.8 us (28%)
  other arithmetic  2.21 us (3%)
    ppermute x16, waiting for transfers between devices, send(): return lax.ppermute(array, 'tp', moved(**step))  28.8 us
    ppermute x16, starting transfers between devices, send(): return lax.ppermute(array, 'tp', moved(**step))  20 us
    pallas_call x4, Pallas kernels, project_call(): pl.pallas_call(kernel, grid=(count // tile,), out_shape=out_shape, in_spe...  16.7 us
    ppermute x1, waiting for transfers between devices, body(): halo = lax.ppermute(rim, 'ctx', [(i, i + 1) for i in range(peers - 1)])  4.35 us
    pallas_call x1, Pallas kernels, gate_late(): pl.pallas_call(functools.partial(late_kernel, EARLY), grid=(channels // W...  4.01 us
    ppermute x1, starting transfers between devices, body(): halo = lax.ppermute(rim, 'ctx', [(i, i + 1) for i in range(peers - 1)])  3.83 us
    pallas_call x1, Pallas kernels, gate_early(): pl.pallas_call(early_kernel, grid_spec=pltpu.PrefetchScalarGridSpec(num_s...  3.31 us
  transfers between devices with their start and end apart: 17, of which 8 were waited for; matrix products, arithmetic and copies ran while one was open for 1% of the time, Pallas kernels for 26%

profile of v8, /device:TPU:4, one launch (start us, length us, event | category | flops | bytes accessed | tf_op | source)
XLA Modules:
  0.0 85.0 jit_solution(3076470975921017184)
XLA Ops:
  0.0 1.2 %rim.1 = bf16[144,512]{1,0:T(8,128)(2,1)S(1)} custom-call(bf16[768,512]{1,0:T(8,128)(2,1)} %q_ref.5, bf16[768,512]{1,0:T(8,128)(2,1)} %k_ref.5, bf16[768,512]{1,0:T(8,128)(2,1)} %v_ref.5, bf16[3,512]{1,0:T(4,128)(2,1)} %taps_ref.5), custom_call_target="tpu_custom_call" | custom-call | flops 1000000000 | bytes 1000000 | tf_op jit(solution)/shard_map/rim/pallas_call | solution.py:162
  1.3 3.8 %collective-permute-start = (bf16[144,512]{1,0:T(8,128)(2,1)S(1)}, bf16[144,512]{1,0:T(8,128)(2,1)S(1)}, u32[]{:S(2)}, u32[]{:S(2)}) collective-permute-start(bf16[144,512]{1,0:T(8,128)(2,1)S(1)} %rim.1), channel_id=1, source_target_pairs={{0,16},{16,32},{32,48},{48,64},{64,80},{80,96},{96,112},{112,128},... | collective-permute-start | bytes 442376 | tf_op jit(solution)/shard_map/ppermute | solution.py:399
  5.1 4.0 %gate_late.1 = (bf16[512,512]{1,0:T(8,128)(2,1)S(1)}, f32[256,512]{1,0:T(8,128)S(1)}) custom-call(bf16[768,512]{1,0:T(8,128)(2,1)} %q_ref.5, bf16[768,512]{1,0:T(8,128)(2,1)} %k_ref.5, bf16[768,512]{1,0:T(8,128)(2,1)} %v_ref.5, bf16[3,512]{1,0:T(4,128)(2,1)} %taps_ref.5, bf16[512,128]{1,0:T(8,128)(2,1)} %filt_ref.1, f32[1,512]{1,0:T(1,128)} %bitcast.2, ...), custom_call_target="tpu_custom_call" | custom-call | flops 4000000000 | bytes 3000000 | tf_op jit(solution)/shard_map/gate_late/pallas_call | solution.py:192
  9.1 4.3 %collective-permute-done.halo_ref = bf16[144,512]{1,0:T(8,128)(2,1)S(1)} collective-permute-done((bf16[144,512]{1,0:T(8,128)(2,1)S(1)}, bf16[144,512]{1,0:T(8,128)(2,1)S(1)}, u32[]{:S(2)}, u32[]{:S(2)}) %collective-permute-start) | collective-permute-done | bytes 147488 | tf_op jit(solution)/shard_map/ppermute | solution.py:399
  13.5 3.3 %gate_early.1 = (bf16[384,512]{1,0:T(8,128)(2,1)S(1)}, bf16[384,512]{1,0:T(8,128)(2,1)S(1)}) custom-call(s32[1]{0:T(128)} %bitcast.place_ref, s32[256]{0:T(256)S(1)} %copy-done, bf16[768,512]{1,0:T(8,128)(2,1)} %q_ref.5, bf16[768,512]{1,0:T(8,128)(2,1)} %k_ref.5, bf16[768,512]{1,0:T(8,128)(2,1)} %v_ref.5, ...), custom_call_target="tpu_custom_call" | custom-call | flops 2000000000 | bytes 3000000 | tf_op jit(solution)/shard_map/gate_early/pallas_call | solution.py:211
  16.9 2.9 %project_own.1.part_ref = f32[384,2304]{1,0:T(8,128)S(1)} custom-call(bf16[384,512]{1,0:T(8,128)(2,1)S(1)} %get-tuple-element.47.a_ref, bf16[512,8192]{1,0:T(8,128)(2,1)} %wa_ref.5), custom_call_target="tpu_custom_call" | custom-call | flops 905969664 | bytes 4128768 | tf_op jit(solution)/shard_map/project_own/pallas_call | solution.py:283
  19.8 2.8 %project_rest.1 = (bf16[192,2304]{1,0:T(8,128)(2,1)S(1)}, bf16[192,2304]{1,0:T(8,128)(2,1)S(1)}) custom-call(bf16[384,512]{1,0:T(8,128)(2,1)S(1)} %collective-permute-done.1.b_ref, bf16[512,8192]{1,0:T(8,128)(2,1)} %collective-permute-done.2.wb_ref, f32[384,2304]{1,0:T(8,128)S(1)} %project_own.1.part_ref), custom_call_target="tpu_custom_call" | custom-call | flops 905969664 | bytes 4128768 | tf_op jit(solution)/shard_map/project_rest/pallas_call | solution.py:283
  22.6 2.2 %collective-permute-start.5 = (bf16[192,2304]{1,0:T(8,128)(2,1)S(1)}, bf16[192,2304]{1,0:T(8,128)(2,1)S(1)}, u32[]{:S(2)}, u32[]{:S(2)}) collective-permute-start(bf16[192,2304]{1,0:T(8,128)(2,1)S(1)} %get-tuple-element.45), channel_id=1, source_target_pairs={{0,2},{1,3},{2,0},{3,1},{4,6},{5,7},{6,4},{7,5},{8,10},{9,11},{10,... | collective-permute-start | bytes 2654216 | tf_op jit(solution)/shard_map/ppermute | solution.py:379
  24.8 6.8 %project.2 = (bf16[96,2304]{1,0:T(8,128)(2,1)S(1)}, bf16[96,2304]{1,0:T(8,128)(2,1)S(1)}, bf16[96,2304]{1,0:T(8,128)(2,1)S(1)}, bf16[96,2304]{1,0:T(8,128)(2,1)S...) custom-call(bf16[384,512]{1,0:T(8,128)(2,1)S(1)} %get-tuple-element., ...), custom_call_target="tpu_custom_call" | custom-call | flops 3623878656 | bytes 12976128 | tf_op jit(solution)/shard_map/project/pallas_call | solution.py:283
  31.5 3.1 %collective-permute-start.3 = (bf16[96,2304]{1,0:T(8,128)(2,1)S(1)}, bf16[96,2304]{1,0:T(8,128)(2,1)S(1)}, u32[]{:S(2)}, u32[]{:S(2)}) collective-permute-start(bf16[96,2304]{1,0:T(8,128)(2,1)S(1)} %get-tuple-element.43), channel_id=1, source_target_pairs={{0,12},{1,13},{2,14},{3,15},{4,0},{5,1},{6,2},{7,3},{8,4},{9,5},{1... | collective-permute-start | bytes 1327112 | tf_op jit(solution)/shard_map/ppermute | solution.py:379
  34.6 0.6 collective-permute-start.7
  35.2 2.7 %collective-permute-start.8 = (bf16[96,2304]{1,0:T(8,128)(2,1)S(1)}, bf16[96,2304]{1,0:T(8,128)(2,1)S(1)}, u32[]{:S(2)}, u32[]{:S(2)}) collective-permute-start(bf16[96,2304]{1,0:T(8,128)(2,1)S(1)} %get-tuple-element.52), channel_id=1, source_target_pairs={{0,12},{1,13},{2,14},{3,15},{4,0},{5,1},{6,2},{7,3},{8,4},{9,5},{1... | collective-permute-start | bytes 1327112 | tf_op jit(solution)/shard_map/ppermute | solution.py:379
  37.9 4.3 %project.3 = (bf16[192,1280]{1,0:T(8,128)(2,1)S(1)}, bf16[192,1280]{1,0:T(8,128)(2,1)S(1)}) custom-call(bf16[384,512]{1,0:T(8,128)(2,1)S(1)} %get-tuple-element.47.a_ref, bf16[384,512]{1,0:T(8,128)(2,1)S(1)} %collective-permute-done.1.b_ref, bf16[512,8192]{1,0:T(8,128)(2,1)} %wa_ref.5, bf16[512,8192]{1,0:T(8,128)(2,1)} %collective-permute-done.2.wb_ref), custom_call_target="tpu_custom_call" | custom-call | flops 1006632960 | bytes 3604480 | tf_op jit(solution)/shard_map/project/pallas_call | solution.py:283
  42.2 2.9 %collective-permute-done.3 = bf16[96,2304]{1,0:T(8,128)(2,1)S(1)} collective-permute-done((bf16[96,2304]{1,0:T(8,128)(2,1)S(1)}, bf16[96,2304]{1,0:T(8,128)(2,1)S(1)}, u32[]{:S(2)}, u32[]{:S(2)}) %collective-permute-start.3) | collective-permute-done | bytes 442400 | tf_op jit(solution)/shard_map/ppermute | solution.py:379
  45.2 3.7 %collective-permute-done.4 = bf16[96,2304]{1,0:T(8,128)(2,1)S(1)} collective-permute-done((bf16[96,2304]{1,0:T(8,128)(2,1)S(1)}, bf16[96,2304]{1,0:T(8,128)(2,1)S(1)}, u32[]{:S(2)}, u32[]{:S(2)}) %collective-permute-start.4) | collective-permute-done | bytes 442400 | tf_op jit(solution)/shard_map/ppermute | solution.py:379
  48.9 0.2 fusion.5
  49.2 0.1 add_convert_fusion.1
  49.4 0.9 %collective-permute-start.6 = (bf16[192,1280]{1,0:T(8,128)(2,1)S(1)}, bf16[192,1280]{1,0:T(8,128)(2,1)S(1)}, u32[]{:S(2)}, u32[]{:S(2)}) collective-permute-start(bf16[192,1280]{1,0:T(8,128)(2,1)S(1)} %get-tuple-element.50), channel_id=1, source_target_pairs={{0,2},{1,3},{2,0},{3,1},{4,6},{5,7},{6,4},{7,5},{8,10},{9,11},{10,... | collective-permute-start | bytes 1474568 | tf_op jit(solution)/shard_map/ppermute | solution.py:379
  50.4 1.2 %collective-permute-start.11 = (bf16[96,2304]{1,0:T(8,128)(2,1)S(1)}, bf16[96,2304]{1,0:T(8,128)(2,1)S(1)}, u32[]{:S(2)}, u32[]{:S(2)}) collective-permute-start(bf16[96,2304]{1,0:T(8,128)(2,1)S(1)} %add_convert_fusion), channel_id=1, source_target_pairs={{0,4},{1,5},{2,6},{3,7},{4,8},{5,9},{6,10},{7,11},{8,12},{9,13},{1... | collective-permute-start | bytes 1327112 | tf_op jit(solution)/shard_map/ppermute | solution.py:379
  51.6 9.7 %collective-permute-done.6 = bf16[192,1280]{1,0:T(8,128)(2,1)S(1)} collective-permute-done((bf16[192,1280]{1,0:T(8,128)(2,1)S(1)}, bf16[192,1280]{1,0:T(8,128)(2,1)S(1)}, u32[]{:S(2)}, u32[]{:S(2)}) %collective-permute-start.6) | collective-permute-done | bytes 491552 | tf_op jit(solution)/shard_map/ppermute | solution.py:379
  61.3 0.1 fusion.4
  61.5 1.9 %collective-permute-done.9 = bf16[96,2304]{1,0:T(8,128)(2,1)S(1)} collective-permute-done((bf16[96,2304]{1,0:T(8,128)(2,1)S(1)}, bf16[96,2304]{1,0:T(8,128)(2,1)S(1)}, u32[]{:S(2)}, u32[]{:S(2)}) %collective-permute-start.9) | collective-permute-done | bytes 442400 | tf_op jit(solution)/shard_map/ppermute | solution.py:379
  63.4 0.1 convert_add_fusion.3
  63.6 0.4 collective-permute-start.10
  64.0 3.7 %collective-permute-start.12 = (bf16[48,1792]{1,0:T(8,128)(2,1)S(1)}, bf16[48,1792]{1,0:T(8,128)(2,1)S(1)}, u32[]{:S(2)}, u32[]{:S(2)}) collective-permute-start(bf16[48,1792]{1,0:T(8,128)(2,1)S(1)} %get-tuple-element.60), channel_id=1, source_target_pairs={{0,12},{1,13},{2,14},{3,15},{4,0},{5,1},{6,2},{7,3},{8,4},{9,5},{1... | collective-permute-start | bytes 516104 | tf_op jit(solution)/shard_map/ppermute | solution.py:379
  67.7 0.1 convert_add_fusion.2
  67.9 3.0 %collective-permute-done.12 = bf16[48,1792]{1,0:T(8,128)(2,1)S(1)} collective-permute-done((bf16[48,1792]{1,0:T(8,128)(2,1)S(1)}, bf16[48,1792]{1,0:T(8,128)(2,1)S(1)}, u32[]{:S(2)}, u32[]{:S(2)}) %collective-permute-start.12) | collective-permute-done | bytes 172064 | tf_op jit(solution)/shard_map/ppermute | solution.py:379
  70.9 3.4 %collective-permute-done.13 = bf16[48,1792]{1,0:T(8,128)(2,1)S(1)} collective-permute-done((bf16[48,1792]{1,0:T(8,128)(2,1)S(1)}, bf16[48,1792]{1,0:T(8,128)(2,1)S(1)}, u32[]{:S(2)}, u32[]{:S(2)}) %collective-permute-start.13) | collective-permute-done | bytes 172064 | tf_op jit(solution)/shard_map/ppermute | solution.py:379
  74.5 3.3 %collective-permute-start.16 = (bf16[48,3584]{1,0:T(8,128)(2,1)S(1)}, bf16[48,3584]{1,0:T(8,128)(2,1)S(1)}, u32[]{:S(2)}, u32[]{:S(2)}) collective-permute-start(bf16[48,3584]{1,0:T(8,128)(2,1)S(1)} %pad_maximum_fusion.1), channel_id=1, source_target_pairs={{0,12},{1,13},{2,14},{3,15},{4,0},{5,1},{6,2},{7,3},{8,4},{9,5},{1... | collective-permute-start | bytes 1032200 | tf_op jit(solution)/shard_map/ppermute | solution.py:379
  77.8 1.7 %collective-permute-start.14 = (bf16[48,2304]{1,0:T(8,128)(2,1)S(1)}, bf16[48,2304]{1,0:T(8,128)(2,1)S(1)}, u32[]{:S(2)}, u32[]{:S(2)}) collective-permute-start(bf16[48,2304]{1,0:T(8,128)(2,1)S(1)} %slice.92), channel_id=1, source_target_pairs={{0,2},{1,3},{2,0},{3,1},{4,6},{5,7},{6,4},{7,5},{8,10},{9,11},{10,... | collective-permute-start | bytes 663560 | tf_op jit(solution)/shard_map/ppermute | solution.py:379
  79.6 4.2 %collective-permute-done.14 = bf16[48,2304]{1,0:T(8,128)(2,1)S(1)} collective-permute-done((bf16[48,2304]{1,0:T(8,128)(2,1)S(1)}, bf16[48,2304]{1,0:T(8,128)(2,1)S(1)}, u32[]{:S(2)}, u32[]{:S(2)}) %collective-permute-start.14) | collective-permute-done | bytes 221216 | tf_op jit(solution)/shard_map/ppermute | solution.py:379
  83.9 1.1 %fusion = bf16[48,8192]{1,0:T(8,128)(2,1)} fusion(f32[48,3584]{1,0:T(8,128)S(1)} %fusion.1, f32[48,2304]{1,0:T(8,128)S(1)} %slice_add_fusion, f32[48,2304]{1,0:T(8,128)S(1)} %slice_add_fusion.1, bf16[48,8192]{1,0:T(8,128)(2,1)S(1)} %copy-done.1), kind=kLoop, calls=%fused_computation.2 | loop fusion | flops 1966080 | bytes 3145728 | tf_op jit(solution)/shard_map/convert_element_type | solution.py:411
  (36 shorter events, 0.9 us)
Async XLA Ops:
  0.0 19.8 %collective-permute-start.2 = (bf16[512,8192]{1,0:T(8,128)(2,1)}, bf16[512,8192]{1,0:T(8,128)(2,1)}, u32[]{:S(2)}, u32[]{:S(2)}) collective-permute-start(bf16[512,8192]{1,0:T(8,128)(2,1)} %wa_ref.5), channel_id=1, source_target_pairs={{0,1},{1,0},{2,3},{3,2},{4,5},{5,4},{6,7},{7,6},{8,9},{9,8},{10,11... | collective-permute-start | bytes 25165832 | tf_op jit(solution)/shard_map/ppermute | solution.py:379
  1.3 12.2 %collective-permute-start = (bf16[144,512]{1,0:T(8,128)(2,1)S(1)}, bf16[144,512]{1,0:T(8,128)(2,1)S(1)}, u32[]{:S(2)}, u32[]{:S(2)}) collective-permute-start(bf16[144,512]{1,0:T(8,128)(2,1)S(1)} %rim.1), channel_id=1, source_target_pairs={{0,16},{16,32},{32,48},{48,64},{64,80},{80,96},{96,112},{112,128},... | collective-permute-start | bytes 442376 | tf_op jit(solution)/shard_map/ppermute | solution.py:399
  5.1 8.4 %copy-start = (s32[256]{0:T(256)S(1)}, s32[256]{0:T(256)}, u32[]{:S(2)}) copy-start(s32[256]{0:T(256)} %constant.12.clone.order_ref) | copy-start | bytes 3076
  16.8 3.0 %collective-permute-start.1 = (bf16[384,512]{1,0:T(8,128)(2,1)S(1)}, bf16[384,512]{1,0:T(8,128)(2,1)S(1)}, u32[]{:S(2)}, u32[]{:S(2)}) collective-permute-start(bf16[384,512]{1,0:T(8,128)(2,1)S(1)} %get-tuple-element.39), channel_id=1, source_target_pairs={{0,1},{1,0},{2,3},{3,2},{4,5},{5,4},{6,7},{7,6},{8,9},{9,8},{10,11... | collective-permute-start | bytes 1179656 | tf_op jit(solution)/shard_map/ppermute | solution.py:379
  22.6 26.3 %collective-permute-start.5 = (bf16[192,2304]{1,0:T(8,128)(2,1)S(1)}, bf16[192,2304]{1,0:T(8,128)(2,1)S(1)}, u32[]{:S(2)}, u32[]{:S(2)}) collective-permute-start(bf16[192,2304]{1,0:T(8,128)(2,1)S(1)} %get-tuple-element.45), channel_id=1, source_target_pairs={{0,2},{1,3},{2,0},{3,1},{4,6},{5,7},{6,4},{7,5},{8,10},{9,11},{10,... | collective-permute-start | bytes 2654216 | tf_op jit(solution)/shard_map/ppermute | solution.py:379
  31.5 13.6 %collective-permute-start.3 = (bf16[96,2304]{1,0:T(8,128)(2,1)S(1)}, bf16[96,2304]{1,0:T(8,128)(2,1)S(1)}, u32[]{:S(2)}, u32[]{:S(2)}) collective-permute-start(bf16[96,2304]{1,0:T(8,128)(2,1)S(1)} %get-tuple-element.43), channel_id=1, source_target_pairs={{0,12},{1,13},{2,14},{3,15},{4,0},{5,1},{6,2},{7,3},{8,4},{9,5},{1... | collective-permute-start | bytes 1327112 | tf_op jit(solution)/shard_map/ppermute | solution.py:379
  34.6 14.3 %collective-permute-start.4 = (bf16[96,2304]{1,0:T(8,128)(2,1)S(1)}, bf16[96,2304]{1,0:T(8,128)(2,1)S(1)}, u32[]{:S(2)}, u32[]{:S(2)}) collective-permute-start(bf16[96,2304]{1,0:T(8,128)(2,1)S(1)} %get-tuple-element.44), channel_id=1, source_target_pairs={{0,4},{1,5},{2,6},{3,7},{4,8},{5,9},{6,10},{7,11},{8,12},{9,13},{1... | collective-permute-start | bytes 1327112 | tf_op jit(solution)/shard_map/ppermute | solution.py:379
  34.6 26.8 %collective-permute-start.7 = (bf16[96,2304]{1,0:T(8,128)(2,1)S(1)}, bf16[96,2304]{1,0:T(8,128)(2,1)S(1)}, u32[]{:S(2)}, u32[]{:S(2)}) collective-permute-start(bf16[96,2304]{1,0:T(8,128)(2,1)S(1)} %get-tuple-element.51), channel_id=1, source_target_pairs={{0,4},{1,5},{2,6},{3,7},{4,8},{5,9},{6,10},{7,11},{8,12},{9,13},{1... | collective-permute-start | bytes 1327112 | tf_op jit(solution)/shard_map/ppermute | solution.py:379
  35.2 26.3 %collective-permute-start.8 = (bf16[96,2304]{1,0:T(8,128)(2,1)S(1)}, bf16[96,2304]{1,0:T(8,128)(2,1)S(1)}, u32[]{:S(2)}, u32[]{:S(2)}) collective-permute-start(bf16[96,2304]{1,0:T(8,128)(2,1)S(1)} %get-tuple-element.52), channel_id=1, source_target_pairs={{0,12},{1,13},{2,14},{3,15},{4,0},{5,1},{6,2},{7,3},{8,4},{9,5},{1... | collective-permute-start | bytes 1327112 | tf_op jit(solution)/shard_map/ppermute | solution.py:379
  49.3 14.1 %collective-permute-start.9 = (bf16[96,2304]{1,0:T(8,128)(2,1)S(1)}, bf16[96,2304]{1,0:T(8,128)(2,1)S(1)}, u32[]{:S(2)}, u32[]{:S(2)}) collective-permute-start(bf16[96,2304]{1,0:T(8,128)(2,1)S(1)} %add_convert_fusion.1), channel_id=1, source_target_pairs={{0,12},{1,13},{2,14},{3,15},{4,0},{5,1},{6,2},{7,3},{8,4},{9,5},{1... | collective-permute-start | bytes 1327112 | tf_op jit(solution)/shard_map/ppermute | solution.py:379
  49.4 11.9 %collective-permute-start.6 = (bf16[192,1280]{1,0:T(8,128)(2,1)S(1)}, bf16[192,1280]{1,0:T(8,128)(2,1)S(1)}, u32[]{:S(2)}, u32[]{:S(2)}) collective-permute-start(bf16[192,1280]{1,0:T(8,128)(2,1)S(1)} %get-tuple-element.50), channel_id=1, source_target_pairs={{0,2},{1,3},{2,0},{3,1},{4,6},{5,7},{6,4},{7,5},{8,10},{9,11},{10,... | collective-permute-start | bytes 1474568 | tf_op jit(solution)/shard_map/ppermute | solution.py:379
  50.4 17.3 %collective-permute-start.11 = (bf16[96,2304]{1,0:T(8,128)(2,1)S(1)}, bf16[96,2304]{1,0:T(8,128)(2,1)S(1)}, u32[]{:S(2)}, u32[]{:S(2)}) collective-permute-start(bf16[96,2304]{1,0:T(8,128)(2,1)S(1)} %add_convert_fusion), channel_id=1, source_target_pairs={{0,4},{1,5},{2,6},{3,7},{4,8},{5,9},{6,10},{7,11},{8,12},{9,13},{1... | collective-permute-start | bytes 1327112 | tf_op jit(solution)/shard_map/ppermute | solution.py:379
  63.6 14.3 %collective-permute-start.10 = (bf16[48,2304]{1,0:T(8,128)(2,1)S(1)}, bf16[48,2304]{1,0:T(8,128)(2,1)S(1)}, u32[]{:S(2)}, u32[]{:S(2)}) collective-permute-start(bf16[48,2304]{1,0:T(8,128)(2,1)S(1)} %slice.93), channel_id=1, source_target_pairs={{0,2},{1,3},{2,0},{3,1},{4,6},{5,7},{6,4},{7,5},{8,10},{9,11},{10,... | collective-permute-start | bytes 663560 | tf_op jit(solution)/shard_map/ppermute | solution.py:379
  64.0 6.9 %collective-permute-start.12 = (bf16[48,1792]{1,0:T(8,128)(2,1)S(1)}, bf16[48,1792]{1,0:T(8,128)(2,1)S(1)}, u32[]{:S(2)}, u32[]{:S(2)}) collective-permute-start(bf16[48,1792]{1,0:T(8,128)(2,1)S(1)} %get-tuple-element.60), channel_id=1, source_target_pairs={{0,12},{1,13},{2,14},{3,15},{4,0},{5,1},{6,2},{7,3},{8,4},{9,5},{1... | collective-permute-start | bytes 516104 | tf_op jit(solution)/shard_map/ppermute | solution.py:379
  67.7 6.6 %collective-permute-start.13 = (bf16[48,1792]{1,0:T(8,128)(2,1)S(1)}, bf16[48,1792]{1,0:T(8,128)(2,1)S(1)}, u32[]{:S(2)}, u32[]{:S(2)}) collective-permute-start(bf16[48,1792]{1,0:T(8,128)(2,1)S(1)} %get-tuple-element.61), channel_id=1, source_target_pairs={{0,4},{1,5},{2,6},{3,7},{4,8},{5,9},{6,10},{7,11},{8,12},{9,13},{1... | collective-permute-start | bytes 516104 | tf_op jit(solution)/shard_map/ppermute | solution.py:379
  74.4 9.4 %collective-permute-start.15 = (bf16[48,3584]{1,0:T(8,128)(2,1)S(1)}, bf16[48,3584]{1,0:T(8,128)(2,1)S(1)}, u32[]{:S(2)}, u32[]{:S(2)}) collective-permute-start(bf16[48,3584]{1,0:T(8,128)(2,1)S(1)} %pad_maximum_fusion), channel_id=1, source_target_pairs={{0,4},{1,5},{2,6},{3,7},{4,8},{5,9},{6,10},{7,11},{8,12},{9,13},{1... | collective-permute-start | bytes 1032200 | tf_op jit(solution)/shard_map/ppermute | solution.py:379
  74.5 9.3 %collective-permute-start.16 = (bf16[48,3584]{1,0:T(8,128)(2,1)S(1)}, bf16[48,3584]{1,0:T(8,128)(2,1)S(1)}, u32[]{:S(2)}, u32[]{:S(2)}) collective-permute-start(bf16[48,3584]{1,0:T(8,128)(2,1)S(1)} %pad_maximum_fusion.1), channel_id=1, source_target_pairs={{0,12},{1,13},{2,14},{3,15},{4,0},{5,1},{6,2},{7,3},{8,4},{9,5},{1... | collective-permute-start | bytes 1032200 | tf_op jit(solution)/shard_map/ppermute | solution.py:379
  77.8 5.9 %collective-permute-start.14 = (bf16[48,2304]{1,0:T(8,128)(2,1)S(1)}, bf16[48,2304]{1,0:T(8,128)(2,1)S(1)}, u32[]{:S(2)}, u32[]{:S(2)}) collective-permute-start(bf16[48,2304]{1,0:T(8,128)(2,1)S(1)} %slice.92), channel_id=1, source_target_pairs={{0,2},{1,3},{2,0},{3,1},{4,6},{5,7},{6,4},{7,5},{8,10},{9,11},{10,... | collective-permute-start | bytes 663560 | tf_op jit(solution)/shard_map/ppermute | solution.py:379
  79.6 4.4 %copy-start.1 = (bf16[48,8192]{1,0:T(8,128)(2,1)S(1)}, bf16[48,8192]{1,0:T(8,128)(2,1)}, u32[]{:S(2)}) copy-start(bf16[48,8192]{1,0:T(8,128)(2,1)} %param.18) | copy-start | bytes 2359300
